TPU v7x, 32 devices: a whole 2x2x4 slice. The times are simulated.
32 devices in a mesh: groups: 2 (over x), shard: 8 (over z, y), sub: 2 (over core).
Axes of the slice: x: 2, y: 2, z: 4, core: 2. Of those that a mesh axis runs over, the one named last changes fastest.
Arguments:
- queries: bfloat16 [256, 32, 128], P(('groups', 'shard', 'sub')), parts along dimension 0, may hold values from -1.796875 to 1.796875
- passages: bfloat16 [2048, 128, 128], P(('shard', 'sub')), may hold values from -1.796875 to 1.796875
- passage_len: int32 [2048], P(('shard', 'sub')), may hold values from 16 to 128, as said below
- slot_query: int32 [32, 16, 24], P('groups', ('shard', 'sub')), parts along dimension 0, may hold values from 0 to 7
- slot_passage: int32 [32, 16, 24], P('groups', ('shard', 'sub')), parts along dimension 0, may hold values from 0 to 127
- slot_count: int32 [32, 16], P('groups', ('shard', 'sub')), parts along dimension 0, may hold values from 1 to 24, as said below
Outputs:
- slot_score: float32 [32, 16, 24], P(('groups', 'shard', 'sub')), parts along dimension 0
There are 2 independent parts, one for each index of `groups`. A program takes and returns all parts, laid end to end along the dimension named above; an argument that names none is the same for every part. Nothing has to cross between parts.
Inputs may be any that keep to these rules, and one draw needn't show every extreme that they name: `passage_len`: live tokens of a passage; some passage has all 128. Live slots from one source to one owner are its first slot_count entries; some owner receives 24 live slots from every source.
All inputs are finite; a program needn't handle non-finite values.
Results may differ from a plain program's by a relative error of at most 0.0003.
Values may be sent and summed in bfloat16 or wider, within the bound.
No kernel may reach another device: no remote copies, remote signals or barrier semaphores. Data moves between devices by JAX's collectives and lax.ppermute only.
A program may use at most 64 MiB of HBM per device.

v0:
```python
import math

import jax
import jax.numpy as jnp
from jax import lax
from jax.sharding import PartitionSpec as P


def slot_scores(query_rows, passage_rows, passages, passage_len):
    pass_total, tok_slots, width = passages.shape
    choose = passage_rows[:, None] == lax.broadcasted_iota(
        jnp.int32, (passage_rows.shape[0], pass_total), 1
    )
    flat_index = passages.reshape(pass_total, tok_slots * width)
    chosen = jnp.dot(choose.astype(jnp.bfloat16), flat_index, preferred_element_type=jnp.float32)
    chosen = chosen.astype(jnp.bfloat16).reshape(passage_rows.shape[0], tok_slots, width)
    sims = jnp.einsum("sqd,skd->sqk", query_rows, chosen, preferred_element_type=jnp.float32)
    limit = jnp.sum(jnp.where(choose, passage_len[None, :], 0), axis=1)
    token_pos = lax.broadcasted_iota(jnp.int32, sims.shape, 2)
    best = jnp.max(jnp.where(token_pos < limit[:, None, None], sims, -1e30), axis=2)
    return jnp.sum(best, axis=1) / best.shape[1]


def on_device(queries, passages, passage_len, slot_query, slot_passage, slot_count):
    q_dev = queries.shape[0]
    src_total = slot_query.shape[0]
    cap = slot_query.shape[2]
    in_query = slot_query[:, 0]
    in_passage = slot_passage[:, 0]
    in_count = slot_count[:, 0][:, None]
    slot_live = lax.broadcasted_iota(jnp.int32, (src_total, cap), 1) < in_count
    piece = lax.all_gather(queries, ("shard", "sub"), axis=0, tiled=True)
    rows = piece.shape[0]
    sources = min(src_total, -(-rows // q_dev) + 1)
    first = jnp.minimum(jnp.int32(0) // q_dev, src_total - sources)
    source_ids = first + lax.broadcasted_iota(jnp.int32, (sources, 1), 0)
    local_row = source_ids * q_dev + in_query
    inside = (local_row >= 0) & (local_row < rows)
    safe_row = jnp.clip(local_row, 0, rows - 1)
    group = math.gcd(sources, 8)

    def one_block(args):
        row_block, pas_block = args
        scored = slot_scores(
            jnp.take(piece, row_block.reshape(-1), axis=0),
            pas_block.reshape(-1),
            passages,
            passage_len,
        )
        return scored.reshape(row_block.shape)

    got = lax.map(
        one_block,
        (
            safe_row.reshape(sources // group, group, cap),
            in_passage.reshape(sources // group, group, cap),
        ),
    )
    got = got.reshape(sources, cap)
    folded = jnp.where(inside, got, 0.0)
    scores = jnp.where(slot_live, folded, 0.0)
    returned = lax.all_to_all(scores, ("shard", "sub"), split_axis=0, concat_axis=0, tiled=True)
    return returned[None]


def solution(mesh):
    return jax.shard_map(
        on_device,
        mesh=mesh,
        in_specs=(
            P(("groups", "shard", "sub"), None, None),
            P(("shard", "sub"), None, None),
            P(("shard", "sub")),
            P("groups", ("shard", "sub"), None),
            P("groups", ("shard", "sub"), None),
            P("groups", ("shard", "sub")),
        ),
        out_specs=P(("groups", "shard", "sub"), None, None),
        check_vma=False,
    )
```

profile of v0, /device:TPU:0, one launch (start us, length us, event | category | flops | bytes accessed | tf_op | source)
XLA Modules:
  0.0 105.1 jit_solution(17398591980274792187)
XLA Ops:
  6.5 0.7 all-gather.2.cloned.1.call-update
  7.3 0.8 fusion.10
  8.1 42.1 %all-gather.2.cloned.1.call-done = bf16[128,32,128]{2,1,0:T(8,128)(2,1)} async-done(((bf16[8,32,128]{2,1,0:T(8,128)(2,1)}), bf16[128,32,128]{2,1,0:T(8,128)(2,1)}) %all-gather.2.cloned.1.call-update) | async-done | bytes 1048592 | tf_op jit(solution)/shard_map/all_gather | solution.py:32
  50.2 37.5 %while.10 = (s32[]{:T(128)}, f32[2,8,24]{2,1,0:T(8,128)S(1)}, s32[2,8,24]{2,1,0:T(8,128)}, s32[128]{0:T(128)}, s32[2,8,24]{2,1,0:T(8,128)S(1)}, /*index=5*/bf16[...) while((s32[]{:T(128)}, f32[2,8,24]{2,1,0:T(8,128)S(1)}, ...), condition=%wide.region_4.5_spmd, body=%wide.region_0.4_spmd.sunk | while | flops 1013025280 | bytes 38356000 | solution.py:52
  50.2 0.7 constant_dynamic-slice_fusion.3
  50.9 0.1 eq.28
  51.0 5.5 %fusion.19 = bf16[24,8,128,128]{3,1,2,0:T(8,128)(2,1)S(1)} fusion(bf16[16,8,128,128]{3,2,1,0:T(8,128)(2,1)} %bitcast.33, s32[192]{0:T(256)S(1)} %eq.28), kind=kOutput, calls=%fused_computation.6.clone.1 | convolution fusion | flops 808476672 | bytes 10486528 | tf_op jit(solution)/shard_map/while/body/eval_jaxpr/dot_general | solution.py:15
  56.5 4.6 %copy.21 = bf16[24,8,128,128]{3,2,1,0:T(8,128)(2,1)} copy(bf16[24,8,128,128]{3,1,2,0:T(8,128)(2,1)S(1)} %fusion.19) | data formatting | bytes 12582912 | tf_op jit(solution)/shard_map/while
  61.2 0.9 gather_fusion
  62.1 0.2 select_reduce_fusion.4
  62.3 0.1 reshape.139
  62.4 6.3 %select_reduce_fusion.5 = f32[192,32]{1,0:T(8,128)S(1)} fusion(bf16[192,128,128]{2,1,0:T(8,128)(2,1)} %bitcast.32, bf16[192,32,128]{2,1,0:T(8,128)(2,1)S(1)} %gather_fusion, s32[192]{0:T(256)S(1)} %select_reduce_fusion.4, pred[192]{0:T(512)(128)(4,1)S(1)} %compare_and_fusion.2), kind=kOutput, calls=%fused_computation.4.clone.1 | convolution fusion | flops 204466176 | bytes 7889856 | tf_op jit(solution)/shard_map/while/body/eval_jaxpr/sqd,skd->sqk/dot_general | solution.py:17
  68.7 0.1 reduce_sum.22
  68.9 0.7 constant_dynamic-slice_fusion.3
  69.6 0.1 eq.28
  69.7 5.5 %fusion.19 = bf16[24,8,128,128]{3,1,2,0:T(8,128)(2,1)S(1)} fusion(bf16[16,8,128,128]{3,2,1,0:T(8,128)(2,1)} %bitcast.33, s32[192]{0:T(256)S(1)} %eq.28), kind=kOutput, calls=%fused_computation.6.clone.1 | convolution fusion | flops 808476672 | bytes 10486528 | tf_op jit(solution)/shard_map/while/body/eval_jaxpr/dot_general | solution.py:15
  75.3 4.6 %copy.21 = bf16[24,8,128,128]{3,2,1,0:T(8,128)(2,1)} copy(bf16[24,8,128,128]{3,1,2,0:T(8,128)(2,1)S(1)} %fusion.19) | data formatting | bytes 12582912 | tf_op jit(solution)/shard_map/while
  79.9 0.9 gather_fusion
  80.9 0.2 select_reduce_fusion.4
  81.1 6.3 %select_reduce_fusion.5 = f32[192,32]{1,0:T(8,128)S(1)} fusion(bf16[192,128,128]{2,1,0:T(8,128)(2,1)} %bitcast.32, bf16[192,32,128]{2,1,0:T(8,128)(2,1)S(1)} %gather_fusion, s32[192]{0:T(256)S(1)} %select_reduce_fusion.4, pred[192]{0:T(512)(128)(4,1)S(1)} %compare_and_fusion.2), kind=kOutput, calls=%fused_computation.4.clone.1 | convolution fusion | flops 204466176 | bytes 7889856 | tf_op jit(solution)/shard_map/while/body/eval_jaxpr/sqd,skd->sqk/dot_general | solution.py:17
  87.4 0.1 reduce_sum.22
  87.7 0.1 compare_select_fusion.2
  87.8 9.8 %all_to_all.6 = f32[16,1,24]{2,1,0:T(1,128)S(1)} all-to-all(f32[16,1,24]{2,1,0:T(1,128)S(1)} %compare_select_fusion.2), channel_id=1, replica_groups=mesh['groups'=2,'shard'=8,'sub'=2] {'shard','sub'}, dimensions={0} | all-to-all | bytes 3072 | tf_op jit(solution)/shard_map/all_to_all | solution.py:62
  97.6 0.6 copy.32
  (31 shorter events, 0.5 us)
Async XLA Ops:
  6.5 43.7 %all-gather.2.cloned.1.call-start = ((), (), s32[]{:S(2)}) async-start(), calls=%async_computation.1 | async-start | bytes 1114112 | tf_op jit(solution)/shard_map/all_gather | solution.py:32
  50.2 37.5 %copy-start.1 = (s32[16,1,24]{2,1,0:T(1,128)S(1)}, s32[16,1,24]{2,1,0:T(1,128)}, u32[]{:S(2)}) copy-start(s32[16,1,24]{2,1,0:T(1,128)} %param.11) | copy-start | bytes 4612
  50.2 37.5 %copy-start.3 = (s32[16,1]{0,1:T(1,128)S(1)}, s32[16,1]{0,1:T(1,128)}, u32[]{:S(2)}) copy-start(s32[16,1]{0,1:T(1,128)} %param.13) | copy-start | bytes 196
  56.5 4.7 %copy-start = (bf16[128,32,128]{2,1,0:T(8,128)(2,1)S(1)}, bf16[128,32,128]{2,1,0:T(8,128)(2,1)}, u32[]{:S(2)}) copy-start(bf16[128,32,128]{2,1,0:T(8,128)(2,1)} %get-tuple-element.129) | copy-start | bytes 3145732 | tf_op jit(solution)/shard_map/while
  61.1 1.0 copy-start.2
  75.3 4.7 %copy-start = (bf16[128,32,128]{2,1,0:T(8,128)(2,1)S(1)}, bf16[128,32,128]{2,1,0:T(8,128)(2,1)}, u32[]{:S(2)}) copy-start(bf16[128,32,128]{2,1,0:T(8,128)(2,1)} %get-tuple-element.129) | copy-start | bytes 3145732 | tf_op jit(solution)/shard_map/while
  79.8 1.0 copy-start.2
Sparse Core Ops, SparseCore 0:
  9.5 40.6 all-gather.1
where the time goes:
time: 105 us
  waiting for transfers between devices  42.8 us (41%)
  matrix products  23.6 us (22%)
  local copies, waits for them, and re-layouts  13.6 us (13%)
  between operations  13.4 us (13%)
  blocking collectives  9.83 us (9%)
  other arithmetic  1.56 us (1%)
    all_gather x1, waiting for transfers between devices, on_device(): piece = lax.all_gather(queries, ('shard', 'sub'), axis=0, tiled=True)  42.1 us
    dot_general x2, matrix products, slot_scores(): jnp.einsum('sqd,skd->sqk', query_rows, chosen, preferred_element_type=jnp...  12.6 us
    dot_general x2, matrix products, slot_scores(): jnp.dot(choose.astype(jnp.bfloat16), flat_index, preferred_element_type=j...  11.1 us
    all_to_all x1, blocking collectives, on_device(): lax.all_to_all(scores, ('shard', 'sub'), split_axis=0, concat_axis=0, til...  9.83 us
    while x10, local copies, waits for them, and re-layouts  9.15 us
  transfers between devices with their start and end apart: 1, of which 1 were waited for; matrix products, arithmetic and copies ran while one was open for 1% of the time, Pallas kernels for 0%

commit v1 on v0

v1 whole, which is shorter than its diff:
```python
import functools

import jax
import jax.numpy as jnp
from jax import lax
from jax.experimental import pallas as pl
from jax.experimental.pallas import tpu as pltpu
from jax.sharding import PartitionSpec as P

STEP = 8


def score_kernel(shards, cap, where_ref, meta_ref, *refs):
    pieces = refs[:shards]
    own_ref, other_ref, out_ref, query_ref, total_ref = refs[shards:]
    q_dev = query_ref.shape[1]
    pass_dev, tok_slots, _ = own_ref.shape
    sources = shards * 2
    me, core = where_ref[0], where_ref[1]
    owner_size = sources * cap * 2 + sources + pass_dev
    for d in range(shards):
        query_ref[d] = pieces[d][...]
    total_ref[...] = jnp.zeros_like(total_ref)
    token = lax.broadcasted_iota(jnp.int32, (tok_slots, query_ref.shape[2]), 0)
    slot = lax.broadcasted_iota(jnp.int32, (STEP, 1), 0)
    lane = lax.broadcasted_iota(jnp.int32, (STEP, total_ref.shape[1]), 1)

    for which, passages in enumerate((own_ref, other_ref)):
        owner = core if which == 0 else 1 - core
        base = which * owner_size

        def one_source(d, carry):
            shard = jnp.bitwise_xor(me, d)
            source = shard * 2 + core
            live = meta_ref[base + sources * cap * 2 + source]

            def one_step(step, carry):
                best = []
                for k in range(STEP):
                    at = base + source * cap + step * STEP + k
                    query = meta_ref[at]
                    passage = meta_ref[at + sources * cap]
                    limit = meta_ref[base + sources * cap * 2 + sources + passage]
                    sims = lax.dot_general(
                        passages[passage], query_ref[d, query],
                        (((1,), (1,)), ((), ())), preferred_element_type=jnp.float32,
                    )
                    best.append(jnp.max(jnp.where(token < limit, sims, -1e30), axis=0, keepdims=True))
                score = jnp.sum(jnp.concatenate(best, axis=0), axis=1, keepdims=True) / query_ref.shape[2]
                score = jnp.where(slot + step * STEP < live, score, 0.0)
                rows = pl.ds(pl.multiple_of(step * STEP, STEP), STEP)
                total_ref[rows, :] = jnp.where(lane == shard * 2 + owner, score, total_ref[rows, :])
                return carry

            lax.fori_loop(0, (live + STEP - 1) // STEP, one_step, 0)
            return carry

        lax.fori_loop(0, shards, one_source, 0)
    out_ref[...] = total_ref[...].T[:sources, :cap]


def on_device(shards, queries, passages, passage_len, slot_query, slot_passage, slot_count):
    sources, _, cap = slot_query.shape
    me, core = lax.axis_index("shard"), lax.axis_index("sub")
    swap = [(0, 1), (1, 0)]
    meta = jnp.concatenate([slot_query.reshape(-1), slot_passage.reshape(-1), slot_count.reshape(-1), passage_len])
    other_passages = lax.ppermute(passages, "sub", swap)
    other_meta = lax.ppermute(meta, "sub", swap)

    def swapped(piece, d):
        return lax.ppermute(piece, "shard", [(i, i ^ d) for i in range(shards)])

    pieces = [queries] + [None] * (shards - 1)
    for d in range(2, shards, 2):
        pieces[d] = swapped(queries, d)
    for d in range(1, shards, 2):
        pieces[d] = swapped(pieces[d - 1], 1)

    vmem, smem = pl.BlockSpec(memory_space=pltpu.VMEM), pl.BlockSpec(memory_space=pltpu.SMEM)
    scores = pl.pallas_call(
        functools.partial(score_kernel, shards, cap),
        out_shape=jax.ShapeDtypeStruct((sources, cap), jnp.float32),
        in_specs=[smem, smem] + [vmem] * (shards + 2),
        out_specs=vmem,
        scratch_shapes=[
            pltpu.VMEM((shards, *queries.shape), queries.dtype),
            pltpu.VMEM((-(-cap // STEP) * STEP, 128), jnp.float32),
        ],
        compiler_params=pltpu.CompilerParams(vmem_limit_bytes=48 * 1024 * 1024),
        cost_estimate=pl.CostEstimate(flops=400_000_000, bytes_accessed=9_000_000, transcendentals=0),
    )(jnp.stack([me, core]).astype(jnp.int32), jnp.concatenate([meta, other_meta]), *pieces, passages, other_passages)
    returned = lax.all_to_all(scores, "shard", split_axis=0, concat_axis=0, tiled=True)
    return returned[None]


def solution(mesh):
    return jax.shard_map(
        functools.partial(on_device, mesh.shape["shard"]),
        mesh=mesh,
        in_specs=(
            P(("groups", "shard", "sub"), None, None),
            P(("shard", "sub"), None, None),
            P(("shard", "sub")),
            P("groups", ("shard", "sub"), None),
            P("groups", ("shard", "sub"), None),
            P("groups", ("shard", "sub")),
        ),
        out_specs=P(("groups", "shard", "sub"), None, None),
        check_vma=False,
    )
```

time: 105 us -> 48.8 us (0.46)
  waiting for transfers between devices: 42.8 us -> 4.97 us
  matrix products: 23.6 us -> 0 us
  between operations: 13.4 us -> 0.03 us
  Pallas kernels: 0 us -> 11.8 us
  starting transfers between devices: 0.01 us -> 9.67 us
  local copies, waits for them, and re-layouts: 13.6 us -> 5.05 us
  blocking collectives: 9.83 us -> 13.5 us
  other arithmetic: 1.56 us -> 3.56 us
    all_gather x1 -> x0, waiting for transfers between devices: 42.1 us -> none  [on_device(): piece = lax.all_gather(queries, ('shard', 'sub'), axis=0, tiled=True)]
    dot_general x4 -> x0, matrix products: 23.6 us -> none  [the longest x2 12.6 us: slot_scores(): jnp.einsum('sqd,skd->sqk', query_rows, chosen, preferred_element_type=jnp...]
    pallas_call x0 -> x1, Pallas kernels: none -> 11.8 us  [on_device(): pl.pallas_call(functools.partial(score_kernel, shards, cap), out_shape=ja...]
    ppermute x0 -> x9, starting transfers between devices: none -> 9.67 us  [the longest x7 9.22 us: swapped(): return lax.ppermute(piece, 'shard', [(i, i ^ d) for i in range(shards)])]
    while x10 -> x0, local copies, waits for them, and re-layouts: 9.15 us -> none
    ppermute x0 -> x9, waiting for transfers between devices: none -> 4.97 us  [the longest x7 3.81 us: swapped(): return lax.ppermute(piece, 'shard', [(i, i ^ d) for i in range(shards)])]
    all_to_all x1, blocking collectives: 9.83 us -> 13.5 us  [on_device(): lax.all_to_all(scores, 'shard', split_axis=0, concat_axis=0, tiled=True)]
    unnamed x5 -> x6, local copies, waits for them, and re-layouts: 0.61 us -> 4.14 us
  transfers between devices with their start and end apart: 1 -> 9, of which waited for: 1 -> 4; matrix products, arithmetic and copies ran while one was open for 1% -> 10% of each run, Pallas kernels for 0% -> 0%
where the time goes in v1:
time: 48.8 us; the launch traced here: 48.6 us
  blocking collectives  13.5 us (28%)
  Pallas kernels  11.8 us (24%)
  starting transfers between devices  9.67 us (20%)
  local copies, waits for them, and re-layouts  5.05 us (10%)
  waiting for transfers between devices  4.97 us (10%)
  other arithmetic  3.56 us (7%)
    all_to_all x1, blocking collectives, on_device(): lax.all_to_all(scores, 'shard', split_axis=0, concat_axis=0, tiled=True)  13.5 us
    pallas_call x1, Pallas kernels, on_device(): pl.pallas_call(functools.partial(score_kernel, shards, cap), out_shape=ja...  11.8 us
    ppermute x7, starting transfers between devices, swapped(): return lax.ppermute(piece, 'shard', [(i, i ^ d) for i in range(shards)])  9.22 us
    unnamed x6, local copies, waits for them, and re-layouts  4.14 us
    ppermute x7, waiting for transfers between devices, swapped(): return lax.ppermute(piece, 'shard', [(i, i ^ d) for i in range(shards)])  3.81 us
    unnamed x2, other arithmetic  2.74 us
    ppermute x1, waiting for transfers between devices, on_device(): other_meta = lax.ppermute(meta, 'sub', swap)  1.16 us
  transfers between devices with their start and end apart: 9, of which 4 were waited for; matrix products, arithmetic and copies ran while one was open for 10% of the time, Pallas kernels for 0%

profile of v1, /device:TPU:0, one launch (start us, length us, event | category | flops | bytes accessed | tf_op | source)
XLA Modules:
  0.0 48.6 jit_solution(2114321817090746366)
XLA Ops:
  0.0 0.5 collective-permute-start.8
  0.5 3.6 %collective-permute-start.4 = (bf16[8,32,128]{2,1,0:T(8,128)(2,1)}, bf16[8,32,128]{2,1,0:T(8,128)(2,1)S(1)}, u32[]{:S(2)}, u32[]{:S(2)}) collective-permute-start(bf16[8,32,128]{2,1,0:T(8,128)(2,1)} %refs_0_.1), channel_id=1, source_target_pairs={{0,8},{2,10},{4,12},{6,14},{8,0},{10,2},{12,4},{14,6},{1,9},{3,11}... | collective-permute-start | bytes 196616 | tf_op jit(solution)/shard_map/ppermute | solution.py:71
  4.0 1.6 %collective-permute-start.2 = (bf16[8,32,128]{2,1,0:T(8,128)(2,1)}, bf16[8,32,128]{2,1,0:T(8,128)(2,1)S(1)}, u32[]{:S(2)}, u32[]{:S(2)}) collective-permute-start(bf16[8,32,128]{2,1,0:T(8,128)(2,1)} %refs_0_.1), channel_id=1, source_target_pairs={{0,4},{2,6},{4,0},{6,2},{8,12},{10,14},{12,8},{14,10},{1,5},{3,7},... | collective-permute-start | bytes 196616 | tf_op jit(solution)/shard_map/ppermute | solution.py:71
  5.6 0.5 %broadcast.6 = s32[]{:T(128)} broadcast(s32[]{:T(128)} %constant.22), dimensions={} | broadcast | bytes 8 | tf_op args[3]
  6.1 1.4 %reduce.6 = s32[16,24]{1,0:T(8,128)S(1)} reduce(s32[16,1,24]{2,1,0:T(1,128)} %param.9, s32[]{:T(128)} %broadcast.6), dimensions={1}, to_apply=%param.9.reduce_sub_computation.3 | reduce | bytes 3076 | tf_op args[3]
  7.5 0.1 reshape.12
  7.6 1.4 %reduce.7 = s32[16,24]{1,0:T(8,128)S(1)} reduce(s32[16,1,24]{2,1,0:T(1,128)} %param.10, s32[]{:T(128)} %broadcast.6), dimensions={1}, to_apply=%param.10.reduce_sub_computation.3 | reduce | bytes 3076 | tf_op args[4]
  9.0 0.1 reshape.13
  9.0 0.8 %pad_add_fusion = s32[912]{0:T(1024)S(1)} fusion(s32[128]{0:T(128)} %param.8, s32[16]{0:T(128)} %bitcast.7, s32[384]{0:T(512)S(1)} %reshape.13, s32[384]{0:T(512)S(1)} %reshape.12), kind=kLoop, calls=%fused_computation | loop fusion | flops 2736 | bytes 7296 | tf_op jit(solution)/shard_map/concatenate | solution.py:66
  9.8 1.2 %collective-permute-done = s32[912]{0:T(1024)S(1)} collective-permute-done((s32[912]{0:T(1024)S(1)}, s32[912]{0:T(1024)S(1)}, u32[]{:S(2)}, u32[]{:S(2)}) %collective-permute-start) | collective-permute-done | bytes 3680 | tf_op jit(solution)/shard_map/ppermute | solution.py:68
  11.0 1.7 %collective-permute-start.1 = (bf16[8,32,128]{2,1,0:T(8,128)(2,1)}, bf16[8,32,128]{2,1,0:T(8,128)(2,1)S(1)}, u32[]{:S(2)}, u32[]{:S(2)}) collective-permute-start(bf16[8,32,128]{2,1,0:T(8,128)(2,1)} %refs_0_.1), channel_id=1, source_target_pairs={{0,2},{2,0},{4,6},{6,4},{8,10},{10,8},{12,14},{14,12},{1,3},{3,1},... | collective-permute-start | bytes 196616 | tf_op jit(solution)/shard_map/ppermute | solution.py:71
  12.7 0.3 collective-permute-start.5
  13.0 1.7 %collective-permute-start.3 = (bf16[8,32,128]{2,1,0:T(8,128)(2,1)S(1)}, bf16[8,32,128]{2,1,0:T(8,128)(2,1)S(1)}, u32[]{:S(2)}, u32[]{:S(2)}) collective-permute-start(bf16[8,32,128]{2,1,0:T(8,128)(2,1)S(1)} %collective-permute-done.2.refs_2_), channel_id=1, source_target_pairs={{0,2},{2,0},{4,6},{6,4},{8,10},{10,8},{12,14},{14,12},{1,3},{3,1},... | collective-permute-start | bytes 196616 | tf_op jit(solution)/shard_map/ppermute | solution.py:71
  14.7 0.3 collective-permute-start.7
  15.0 0.1 pad_add_fusion.1.where_ref
  15.1 0.7 %concatenate.8.meta_ref = s32[1824]{0:T(1024)S(1)} concatenate(s32[384]{0:T(512)S(1)} %reshape.12, s32[384]{0:T(512)S(1)} %reshape.13, s32[16]{0:T(128)} %bitcast.8, s32[128]{0:T(128)} %param.8, s32[912]{0:T(1024)S(1)} %collective-permute-done), dimensions={0} | concatenate | bytes 14592 | tf_op jit(solution)/shard_map/concatenate | solution.py:91
  15.9 1.8 %collective-permute-done.5.refs_5_ = bf16[8,32,128]{2,1,0:T(8,128)(2,1)S(1)} collective-permute-done((bf16[8,32,128]{2,1,0:T(8,128)(2,1)S(1)}, bf16[8,32,128]{2,1,0:T(8,128)(2,1)S(1)}, u32[]{:S(2)}, u32[]{:S(2)}) %collective-permute-start.5) | collective-permute-done | bytes 65568 | tf_op jit(solution)/shard_map/ppermute | solution.py:71
  17.7 1.3 %collective-permute-done.3.refs_3_ = bf16[8,32,128]{2,1,0:T(8,128)(2,1)S(1)} collective-permute-done((bf16[8,32,128]{2,1,0:T(8,128)(2,1)S(1)}, bf16[8,32,128]{2,1,0:T(8,128)(2,1)S(1)}, u32[]{:S(2)}, u32[]{:S(2)}) %collective-permute-start.3) | collective-permute-done | bytes 65568 | tf_op jit(solution)/shard_map/ppermute | solution.py:71
  19.0 0.7 %collective-permute-done.7.refs_7_ = bf16[8,32,128]{2,1,0:T(8,128)(2,1)S(1)} collective-permute-done((bf16[8,32,128]{2,1,0:T(8,128)(2,1)S(1)}, bf16[8,32,128]{2,1,0:T(8,128)(2,1)S(1)}, u32[]{:S(2)}, u32[]{:S(2)}) %collective-permute-start.7) | collective-permute-done | bytes 65568 | tf_op jit(solution)/shard_map/ppermute | solution.py:71
  19.7 2.2 %copy-done = bf16[128,128,128]{2,1,0:T(8,128)(2,1)S(1)} copy-done((bf16[128,128,128]{2,1,0:T(8,128)(2,1)S(1)}, bf16[128,128,128]{2,1,0:T(8,128)(2,1)}, u32[]{:S(2)}) %copy-start) | copy-done | bytes 4194328
  21.9 0.8 %copy-done.1 = bf16[8,32,128]{2,1,0:T(8,128)(2,1)S(1)} copy-done((bf16[8,32,128]{2,1,0:T(8,128)(2,1)S(1)}, bf16[8,32,128]{2,1,0:T(8,128)(2,1)}, u32[]{:S(2)}) %copy-start.1) | copy-done | bytes 65560
  22.7 11.8 %shard_map.64 = f32[16,24]{1,0:T(8,128)S(1)} custom-call(s32[2]{0:T(128)S(1)} %pad_add_fusion.1.where_ref, s32[1824]{0:T(1024)S(1)} %concatenate.8.meta_ref, bf16[8,32,128]{2,1,0:T(8,128)(2,1)S(1)} %copy-done.1, bf16[8,32,128]{2,1,0:T(8,128)(2,1)S(1)} %collective-permute-done.1.refs_1_, bf16[8,32,128]{2,1,0:T(8,128)(2,1)S(1)} %collective-permute-done.2.refs_2_, ...), custom_call_target="tpu_custom_call" | custom-call | flops 400000000 | bytes 9000000 | tf_op jit(solution)/shard_map/pallas_call | solution.py:80
  34.5 13.5 %all_to_all.9 = f32[8,2,24]{2,1,0:T(2,128)S(1)} all-to-all(f32[8,2,24]{2,1,0:T(2,128)S(1)} %bitcast.5), channel_id=1, replica_groups=mesh['groups'=2,'shard'=8,'sub'=2] {'shard'}, dimensions={0} | all-to-all | bytes 3072 | tf_op jit(solution)/shard_map/all_to_all | solution.py:92
  48.0 0.6 %copy.8 = f32[1,16,24]{2,1,0:T(8,128)} copy(f32[1,16,24]{2,1,0:T(8,128)S(1)} %bitcast.6) | data formatting | bytes 3072
  (9 shorter events, 0.0 us)
Async XLA Ops:
  0.0 19.7 %collective-permute-start.8 = (bf16[128,128,128]{2,1,0:T(8,128)(2,1)}, bf16[128,128,128]{2,1,0:T(8,128)(2,1)}, u32[]{:S(2)}, u32[]{:S(2)}) collective-permute-start(bf16[128,128,128]{2,1,0:T(8,128)(2,1)} %refs_8_.1), channel_id=1, source_target_pairs={{0,1},{1,0},{2,3},{3,2},{4,5},{5,4},{6,7},{7,6},{8,9},{9,8},{10,11... | collective-permute-start | bytes 12582920 | tf_op jit(solution)/shard_map/ppermute | solution.py:67
  0.5 12.3 %collective-permute-start.4 = (bf16[8,32,128]{2,1,0:T(8,128)(2,1)}, bf16[8,32,128]{2,1,0:T(8,128)(2,1)S(1)}, u32[]{:S(2)}, u32[]{:S(2)}) collective-permute-start(bf16[8,32,128]{2,1,0:T(8,128)(2,1)} %refs_0_.1), channel_id=1, source_target_pairs={{0,8},{2,10},{4,12},{6,14},{8,0},{10,2},{12,4},{14,6},{1,9},{3,11}... | collective-permute-start | bytes 196616 | tf_op jit(solution)/shard_map/ppermute | solution.py:71
  4.0 9.0 %collective-permute-start.2 = (bf16[8,32,128]{2,1,0:T(8,128)(2,1)}, bf16[8,32,128]{2,1,0:T(8,128)(2,1)S(1)}, u32[]{:S(2)}, u32[]{:S(2)}) collective-permute-start(bf16[8,32,128]{2,1,0:T(8,128)(2,1)} %refs_0_.1), channel_id=1, source_target_pairs={{0,4},{2,6},{4,0},{6,2},{8,12},{10,14},{12,8},{14,10},{1,5},{3,7},... | collective-permute-start | bytes 196616 | tf_op jit(solution)/shard_map/ppermute | solution.py:71
  5.6 9.1 %collective-permute-start.6 = (bf16[8,32,128]{2,1,0:T(8,128)(2,1)}, bf16[8,32,128]{2,1,0:T(8,128)(2,1)S(1)}, u32[]{:S(2)}, u32[]{:S(2)}) collective-permute-start(bf16[8,32,128]{2,1,0:T(8,128)(2,1)} %refs_0_.1), channel_id=1, source_target_pairs={{0,12},{2,14},{4,8},{6,10},{8,4},{10,6},{12,0},{14,2},{1,13},{3,15... | collective-permute-start | bytes 196616 | tf_op jit(solution)/shard_map/ppermute | solution.py:71
  9.8 1.2 %collective-permute-start = (s32[912]{0:T(1024)S(1)}, s32[912]{0:T(1024)S(1)}, u32[]{:S(2)}, u32[]{:S(2)}) collective-permute-start(s32[912]{0:T(1024)S(1)} %pad_add_fusion), channel_id=1, source_target_pairs={{0,1},{1,0},{2,3},{3,2},{4,5},{5,4},{6,7},{7,6},{8,9},{9,8},{10,11... | collective-permute-start | bytes 10952 | tf_op jit(solution)/shard_map/ppermute | solution.py:68
  11.0 4.9 %collective-permute-start.1 = (bf16[8,32,128]{2,1,0:T(8,128)(2,1)}, bf16[8,32,128]{2,1,0:T(8,128)(2,1)S(1)}, u32[]{:S(2)}, u32[]{:S(2)}) collective-permute-start(bf16[8,32,128]{2,1,0:T(8,128)(2,1)} %refs_0_.1), channel_id=1, source_target_pairs={{0,2},{2,0},{4,6},{6,4},{8,10},{10,8},{12,14},{14,12},{1,3},{3,1},... | collective-permute-start | bytes 196616 | tf_op jit(solution)/shard_map/ppermute | solution.py:71
  12.7 5.0 %collective-permute-start.5 = (bf16[8,32,128]{2,1,0:T(8,128)(2,1)S(1)}, bf16[8,32,128]{2,1,0:T(8,128)(2,1)S(1)}, u32[]{:S(2)}, u32[]{:S(2)}) collective-permute-start(bf16[8,32,128]{2,1,0:T(8,128)(2,1)S(1)} %collective-permute-done.4.refs_4_), channel_id=1, source_target_pairs={{0,2},{2,0},{4,6},{6,4},{8,10},{10,8},{12,14},{14,12},{1,3},{3,1},... | collective-permute-start | bytes 196616 | tf_op jit(solution)/shard_map/ppermute | solution.py:71
  13.0 6.0 %collective-permute-start.3 = (bf16[8,32,128]{2,1,0:T(8,128)(2,1)S(1)}, bf16[8,32,128]{2,1,0:T(8,128)(2,1)S(1)}, u32[]{:S(2)}, u32[]{:S(2)}) collective-permute-start(bf16[8,32,128]{2,1,0:T(8,128)(2,1)S(1)} %collective-permute-done.2.refs_2_), channel_id=1, source_target_pairs={{0,2},{2,0},{4,6},{6,4},{8,10},{10,8},{12,14},{14,12},{1,3},{3,1},... | collective-permute-start | bytes 196616 | tf_op jit(solution)/shard_map/ppermute | solution.py:71
  14.7 4.9 %collective-permute-start.7 = (bf16[8,32,128]{2,1,0:T(8,128)(2,1)S(1)}, bf16[8,32,128]{2,1,0:T(8,128)(2,1)S(1)}, u32[]{:S(2)}, u32[]{:S(2)}) collective-permute-start(bf16[8,32,128]{2,1,0:T(8,128)(2,1)S(1)} %collective-permute-done.6.refs_6_), channel_id=1, source_target_pairs={{0,2},{2,0},{4,6},{6,4},{8,10},{10,8},{12,14},{14,12},{1,3},{3,1},... | collective-permute-start | bytes 196616 | tf_op jit(solution)/shard_map/ppermute | solution.py:71
  19.7 2.2 %copy-start = (bf16[128,128,128]{2,1,0:T(8,128)(2,1)S(1)}, bf16[128,128,128]{2,1,0:T(8,128)(2,1)}, u32[]{:S(2)}) copy-start(bf16[128,128,128]{2,1,0:T(8,128)(2,1)} %refs_8_.1) | copy-start | bytes 12582916
  21.9 0.8 %copy-start.1 = (bf16[8,32,128]{2,1,0:T(8,128)(2,1)S(1)}, bf16[8,32,128]{2,1,0:T(8,128)(2,1)}, u32[]{:S(2)}) copy-start(bf16[8,32,128]{2,1,0:T(8,128)(2,1)} %refs_0_.1) | copy-start | bytes 196612

commit v2 on v1

v2 whole, which is shorter than its diff:
```python
import functools

import jax
import jax.numpy as jnp
from jax import lax
from jax.experimental import pallas as pl
from jax.experimental.pallas import tpu as pltpu
from jax.sharding import PartitionSpec as P

GROUPS = 8


def score_kernel(shards, pack, *refs):
    owners = (refs[:4], refs[4:8])
    pieces = refs[8 : 8 + shards]
    own_ref, other_ref, out_ref, query_ref, best_ref, work_ref = refs[8 + shards :]
    q_tok, width = query_ref.shape[2:]
    tok_slots = own_ref.shape[1]
    cap = out_ref.shape[1]
    per_source = best_ref.shape[0]
    lanes = pack * q_tok
    me, core = lax.axis_index("shard"), lax.axis_index("sub")
    for d in range(shards):
        query_ref[d] = pieces[d][...]
    best_ref[...] = jnp.zeros_like(best_ref)
    token = lax.broadcasted_iota(jnp.int32, (tok_slots, lanes), 0)
    place = lax.broadcasted_iota(jnp.int32, (1, lanes), 1) // q_tok
    blank = jnp.zeros((q_tok, width), query_ref.dtype)

    for which, passages in enumerate((own_ref, other_ref)):
        slot_query, slot_passage, slot_count, passage_len = owners[which]
        owner = core if which == 0 else 1 - core

        def list_source(d, total):
            live = slot_count[jnp.bitwise_xor(me, d) * 2 + core]
            for g in range(per_source):
                work_ref[total + g] = d * per_source + g
            return total + (live + pack - 1) // pack

        total = lax.fori_loop(0, shards, list_source, 0)
        for g in range(GROUPS):
            work_ref[total + g] = 0

        def one_step(step, carry):
            for j in range(GROUPS):
                work = work_ref[step * GROUPS + j]
                d, g = work // per_source, work % per_source
                shard = jnp.bitwise_xor(me, d)
                source = shard * 2 + core
                rows, cols, limit = [], [], jnp.zeros((1, lanes), jnp.int32)
                for a in range(pack):
                    slot = jnp.minimum(g * pack + a, cap - 1)
                    query, passage = slot_query[source, slot], slot_passage[source, slot]
                    rows.append(jnp.concatenate([blank] * a + [query_ref[d, query]] + [blank] * (pack - 1 - a), axis=1))
                    cols.append(passages[passage])
                    limit = jnp.where(place == a, passage_len[passage], limit)
                sims = lax.dot_general(
                    jnp.concatenate(cols, axis=1), jnp.concatenate(rows, axis=0),
                    (((1,), (1,)), ((), ())), preferred_element_type=jnp.float32,
                )
                best = jnp.max(jnp.where(token < limit, sims, -1e30), axis=0, keepdims=True)
                best = jnp.where(place + g * pack < slot_count[source], best, 0.0)
                best_ref[g, pl.ds(shard * 2 + owner, 1), :] = best
            return carry

        lax.fori_loop(0, (total + GROUPS - 1) // GROUPS, one_step, 0)

    best = jnp.concatenate([best_ref[g] for g in range(per_source)], axis=1)
    high = best.astype(jnp.bfloat16)
    rest = best - high.astype(jnp.float32)
    middle = rest.astype(jnp.bfloat16)
    low = (rest - middle.astype(jnp.float32)).astype(jnp.bfloat16)
    row = lax.broadcasted_iota(jnp.int32, (per_source * lanes, 128), 0)
    col = lax.broadcasted_iota(jnp.int32, (per_source * lanes, 128), 1)
    add = jnp.where(row // q_tok == col, 1.0, 0.0).astype(jnp.bfloat16)
    parts = jnp.dot(jnp.concatenate([high, middle, low], axis=0), add, preferred_element_type=jnp.float32)
    n = best.shape[0]
    out_ref[...] = ((parts[:n] + parts[n : 2 * n] + parts[2 * n :]) / q_tok)[:, :cap]


def on_device(shards, queries, passages, passage_len, slot_query, slot_passage, slot_count):
    sources, _, cap = slot_query.shape
    q_tok = queries.shape[1]
    pack = 128 // q_tok
    per_source = -(-cap // pack)
    swap = [(0, 1), (1, 0)]

    def swapped(piece, d):
        return lax.ppermute(piece, "shard", [(i, i ^ d) for i in range(shards)])

    other_passages = lax.ppermute(passages, "sub", swap)
    pieces = [queries] + [None] * (shards - 1)
    for d in range(2, shards, 2):
        pieces[d] = swapped(queries, d)
    for d in range(1, shards, 2):
        pieces[d] = swapped(pieces[d - 1], 1)
    own = (slot_query, slot_passage, slot_count, passage_len)
    other = [lax.ppermute(x, "sub", swap) for x in own]
    own, other = (
        [q.reshape(sources, cap), p.reshape(sources, cap), c.reshape(sources), n] for q, p, c, n in (own, other)
    )

    vmem, smem = pl.BlockSpec(memory_space=pltpu.VMEM), pl.BlockSpec(memory_space=pltpu.SMEM)
    scores = pl.pallas_call(
        functools.partial(score_kernel, shards, pack),
        out_shape=jax.ShapeDtypeStruct((sources, cap), jnp.float32),
        in_specs=[smem] * 8 + [vmem] * (shards + 2),
        out_specs=vmem,
        scratch_shapes=[
            pltpu.VMEM((shards, *queries.shape), queries.dtype),
            pltpu.VMEM((per_source, sources, 128), jnp.float32),
            pltpu.SMEM((shards * per_source + 2 * GROUPS,), jnp.int32),
        ],
        compiler_params=pltpu.CompilerParams(vmem_limit_bytes=32 * 1024 * 1024),
        cost_estimate=pl.CostEstimate(flops=400_000_000, bytes_accessed=9_000_000, transcendentals=0),
    )(*own, *other, *pieces, passages, other_passages)
    returned = lax.all_to_all(scores, "shard", split_axis=0, concat_axis=0, tiled=True)
    return returned[None]


def solution(mesh):
    return jax.shard_map(
        functools.partial(on_device, mesh.shape["shard"]),
        mesh=mesh,
        in_specs=(
            P(("groups", "shard", "sub"), None, None),
            P(("shard", "sub"), None, None),
            P(("shard", "sub")),
            P("groups", ("shard", "sub"), None),
            P("groups", ("shard", "sub"), None),
            P("groups", ("shard", "sub")),
        ),
        out_specs=P(("groups", "shard", "sub"), None, None),
        check_vma=False,
    )
```

time: 48.8 us -> 44.8 us (0.918)
  Pallas kernels: 11.8 us -> 3.88 us
  waiting for transfers between devices: 4.97 us -> 9.73 us
  other arithmetic: 3.56 us -> 0 us
  starting transfers between devices: 9.67 us -> 11.5 us
  local copies, waits for them, and re-layouts: 5.05 us -> 6.33 us
    pallas_call x1, Pallas kernels: 11.8 us -> 3.88 us  [on_device(): pl.pallas_call(functools.partial(score_kernel, shards, pack), out_shape=j...]
    ppermute x1 -> x4, waiting for transfers between devices: 1.16 us -> 4.94 us  [on_device(): other = [lax.ppermute(x, 'sub', swap) for x in own]]
    unnamed x2 -> x0, other arithmetic: 2.74 us -> none
    unnamed x6 -> x13, local copies, waits for them, and re-layouts: 4.14 us -> 6.33 us
    ppermute x1 -> x4, starting transfers between devices: 0.01 us -> 0.98 us  [on_device(): other = [lax.ppermute(x, 'sub', swap) for x in own]]
    ppermute x7, waiting for transfers between devices: 3.81 us -> 4.78 us  [swapped(): return lax.ppermute(piece, 'shard', [(i, i ^ d) for i in range(shards)])]
    ppermute x7, starting transfers between devices: 9.22 us -> 10.1 us  [swapped(): return lax.ppermute(piece, 'shard', [(i, i ^ d) for i in range(shards)])]
    concatenate x1 -> x0, other arithmetic: 0.75 us -> none  [on_device(): jnp.concatenate([slot_query.reshape(-1), slot_passage.reshape(-1), slot_c...]
  transfers between devices with their start and end apart: 9 -> 12, of which waited for: 4 -> 8; matrix products, arithmetic and copies ran while one was open for 10% -> 0% of each run, Pallas kernels for 0% -> 0%
where the time goes in v2:
time: 44.8 us; the launch traced here: 45 us
  blocking collectives  13.6 us (30%)
  starting transfers between devices  11.5 us (26%)
  waiting for transfers between devices  9.73 us (22%)
  local copies, waits for them, and re-layouts  6.33 us (14%)
  Pallas kernels  3.88 us (9%)
    all_to_all x1, blocking collectives, on_device(): lax.all_to_all(scores, 'shard', split_axis=0, concat_axis=0, tiled=True)  13.6 us
    ppermute x7, starting transfers between devices, swapped(): return lax.ppermute(piece, 'shard', [(i, i ^ d) for i in range(shards)])  10.1 us
    unnamed x13, local copies, waits for them, and re-layouts  6.33 us
    ppermute x4, waiting for transfers between devices, on_device(): other = [lax.ppermute(x, 'sub', swap) for x in own]  4.94 us
    ppermute x7, waiting for transfers between devices, swapped(): return lax.ppermute(piece, 'shard', [(i, i ^ d) for i in range(shards)])  4.78 us
    pallas_call x1, Pallas kernels, on_device(): pl.pallas_call(functools.partial(score_kernel, shards, pack), out_shape=j...  3.88 us
    ppermute x4, starting transfers between devices, on_device(): other = [lax.ppermute(x, 'sub', swap) for x in own]  0.98 us
  transfers between devices with their start and end apart: 12, of which 8 were waited for; matrix products, arithmetic and copies ran while one was open for 0% of the time, Pallas kernels for 0%

profile of v2, /device:TPU:0, one launch (start us, length us, event | category | flops | bytes accessed | tf_op | source)
XLA Modules:
  0.0 45.0 jit_solution(9576767663829250100)
XLA Ops:
  0.0 0.5 %collective-permute-start.11 = (bf16[128,128,128]{2,1,0:T(8,128)(2,1)}, bf16[128,128,128]{2,1,0:T(8,128)(2,1)S(1)}, u32[]{:S(2)}, u32[]{:S(2)}) collective-permute-start(bf16[128,128,128]{2,1,0:T(8,128)(2,1)} %refs_16_.1), channel_id=1, source_target_pairs={{0,1},{1,0},{2,3},{3,2},{4,5},{5,4},{6,7},{7,6},{8,9},{9,8},{10,11... | collective-permute-start | bytes 12582920 | tf_op jit(solution)/shard_map/ppermute | solution.py:91
  0.5 3.6 %collective-permute-start.7 = (bf16[8,32,128]{2,1,0:T(8,128)(2,1)}, bf16[8,32,128]{2,1,0:T(8,128)(2,1)S(1)}, u32[]{:S(2)}, u32[]{:S(2)}) collective-permute-start(bf16[8,32,128]{2,1,0:T(8,128)(2,1)} %refs_8_.1), channel_id=1, source_target_pairs={{0,8},{2,10},{4,12},{6,14},{8,0},{10,2},{12,4},{14,6},{1,9},{3,11}... | collective-permute-start | bytes 196616 | tf_op jit(solution)/shard_map/ppermute | solution.py:89
  4.0 1.6 %collective-permute-start.5 = (bf16[8,32,128]{2,1,0:T(8,128)(2,1)}, bf16[8,32,128]{2,1,0:T(8,128)(2,1)S(1)}, u32[]{:S(2)}, u32[]{:S(2)}) collective-permute-start(bf16[8,32,128]{2,1,0:T(8,128)(2,1)} %refs_8_.1), channel_id=1, source_target_pairs={{0,4},{2,6},{4,0},{6,2},{8,12},{10,14},{12,8},{14,10},{1,5},{3,7},... | collective-permute-start | bytes 196616 | tf_op jit(solution)/shard_map/ppermute | solution.py:89
  5.6 1.8 %collective-permute-done.2 = s32[16,1]{0,1:T(1,128)S(1)} collective-permute-done((s32[16,1]{0,1:T(1,128)}, s32[16,1]{0,1:T(1,128)S(1)}, u32[]{:S(2)}, u32[]{:S(2)}) %collective-permute-start.2) | collective-permute-done | bytes 96 | tf_op jit(solution)/shard_map/ppermute | solution.py:98
  7.5 0.4 collective-permute-start.3
  7.8 1.0 %collective-permute-done.3.refs_7_ = s32[128]{0:T(128)S(1)} collective-permute-done((s32[128]{0:T(128)}, s32[128]{0:T(128)S(1)}, u32[]{:S(2)}, u32[]{:S(2)}) %collective-permute-start.3) | collective-permute-done | bytes 544 | tf_op jit(solution)/shard_map/ppermute | solution.py:98
  8.8 0.3 collective-permute-start.1
  9.1 1.1 %collective-permute-done.1 = s32[16,1,24]{2,0,1:T(8,128)S(1)} collective-permute-done((s32[16,1,24]{2,0,1:T(8,128)}, s32[16,1,24]{2,0,1:T(8,128)S(1)}, u32[]{:S(2)}, u32[]{:S(2)}) %collective-permute-start.1) | collective-permute-done | bytes 1568 | tf_op jit(solution)/shard_map/ppermute | solution.py:98
  10.5 1.1 %collective-permute-done = s32[16,1,24]{2,0,1:T(8,128)S(1)} collective-permute-done((s32[16,1,24]{2,0,1:T(8,128)}, s32[16,1,24]{2,0,1:T(8,128)S(1)}, u32[]{:S(2)}, u32[]{:S(2)}) %collective-permute-start) | collective-permute-done | bytes 1568 | tf_op jit(solution)/shard_map/ppermute | solution.py:98
  11.5 2.8 %collective-permute-start.4 = (bf16[8,32,128]{2,1,0:T(8,128)(2,1)}, bf16[8,32,128]{2,1,0:T(8,128)(2,1)S(1)}, u32[]{:S(2)}, u32[]{:S(2)}) collective-permute-start(bf16[8,32,128]{2,1,0:T(8,128)(2,1)} %refs_8_.1), channel_id=1, source_target_pairs={{0,2},{2,0},{4,6},{6,4},{8,10},{10,8},{12,14},{14,12},{1,3},{3,1},... | collective-permute-start | bytes 196616 | tf_op jit(solution)/shard_map/ppermute | solution.py:89
  14.4 2.0 %collective-permute-start.6 = (bf16[8,32,128]{2,1,0:T(8,128)(2,1)S(1)}, bf16[8,32,128]{2,1,0:T(8,128)(2,1)S(1)}, u32[]{:S(2)}, u32[]{:S(2)}) collective-permute-start(bf16[8,32,128]{2,1,0:T(8,128)(2,1)S(1)} %collective-permute-done.5.refs_10_), channel_id=1, source_target_pairs={{0,2},{2,0},{4,6},{6,4},{8,10},{10,8},{12,14},{14,12},{1,3},{3,1},... | collective-permute-start | bytes 196616 | tf_op jit(solution)/shard_map/ppermute | solution.py:89
  16.5 0.7 %collective-permute-done.4.refs_9_ = bf16[8,32,128]{2,1,0:T(8,128)(2,1)S(1)} collective-permute-done((bf16[8,32,128]{2,1,0:T(8,128)(2,1)}, bf16[8,32,128]{2,1,0:T(8,128)(2,1)S(1)}, u32[]{:S(2)}, u32[]{:S(2)}) %collective-permute-start.4) | collective-permute-done | bytes 65568 | tf_op jit(solution)/shard_map/ppermute | solution.py:89
  17.2 2.1 %collective-permute-done.8.refs_13_ = bf16[8,32,128]{2,1,0:T(8,128)(2,1)S(1)} collective-permute-done((bf16[8,32,128]{2,1,0:T(8,128)(2,1)S(1)}, bf16[8,32,128]{2,1,0:T(8,128)(2,1)S(1)}, u32[]{:S(2)}, u32[]{:S(2)}) %collective-permute-start.8) | collective-permute-done | bytes 65568 | tf_op jit(solution)/shard_map/ppermute | solution.py:89
  19.3 1.2 %collective-permute-done.6.refs_11_ = bf16[8,32,128]{2,1,0:T(8,128)(2,1)S(1)} collective-permute-done((bf16[8,32,128]{2,1,0:T(8,128)(2,1)S(1)}, bf16[8,32,128]{2,1,0:T(8,128)(2,1)S(1)}, u32[]{:S(2)}, u32[]{:S(2)}) %collective-permute-start.6) | collective-permute-done | bytes 65568 | tf_op jit(solution)/shard_map/ppermute | solution.py:89
  20.5 0.7 %collective-permute-done.10.refs_15_ = bf16[8,32,128]{2,1,0:T(8,128)(2,1)S(1)} collective-permute-done((bf16[8,32,128]{2,1,0:T(8,128)(2,1)S(1)}, bf16[8,32,128]{2,1,0:T(8,128)(2,1)S(1)}, u32[]{:S(2)}, u32[]{:S(2)}) %collective-permute-start.10) | collective-permute-done | bytes 65568 | tf_op jit(solution)/shard_map/ppermute | solution.py:89
  21.3 2.2 %copy-done = bf16[128,128,128]{2,1,0:T(8,128)(2,1)S(1)} copy-done((bf16[128,128,128]{2,1,0:T(8,128)(2,1)S(1)}, bf16[128,128,128]{2,1,0:T(8,128)(2,1)}, u32[]{:S(2)}) %copy-start) | copy-done | bytes 4194328
  23.4 0.8 %copy-done.1 = bf16[8,32,128]{2,1,0:T(8,128)(2,1)S(1)} copy-done((bf16[8,32,128]{2,1,0:T(8,128)(2,1)S(1)}, bf16[8,32,128]{2,1,0:T(8,128)(2,1)}, u32[]{:S(2)}) %copy-start.1) | copy-done | bytes 65560
  24.3 0.7 %copy-done.2 = s32[16,1,24]{2,1,0:T(1,128)S(1)} copy-done((s32[16,1,24]{2,1,0:T(1,128)S(1)}, s32[16,1,24]{2,1,0:T(1,128)}, u32[]{:S(2)}) %copy-start.2) | copy-done | bytes 1560
  25.0 0.7 %copy-done.3 = s32[16,1,24]{2,1,0:T(1,128)S(1)} copy-done((s32[16,1,24]{2,1,0:T(1,128)S(1)}, s32[16,1,24]{2,1,0:T(1,128)}, u32[]{:S(2)}) %copy-start.3) | copy-done | bytes 1560
  25.7 0.7 %copy-done.4 = s32[16,1]{0,1:T(1,128)S(1)} copy-done((s32[16,1]{0,1:T(1,128)S(1)}, s32[16,1]{0,1:T(1,128)}, u32[]{:S(2)}) %copy-start.4) | copy-done | bytes 88
  26.3 0.7 %copy-done.5 = s32[128]{0:T(128)S(1)} copy-done((s32[128]{0:T(128)S(1)}, s32[128]{0:T(128)}, u32[]{:S(2)}) %copy-start.5) | copy-done | bytes 536
  27.0 3.9 %shard_map.64 = f32[16,24]{1,0:T(8,128)S(1)} custom-call(s32[16,24]{1,0:T(8,128)S(1)} %bitcast.12, s32[16,24]{1,0:T(8,128)S(1)} %bitcast.14, s32[16]{0:T(128)S(1)} %bitcast.17, s32[128]{0:T(128)S(1)} %copy-done.5, s32[16,24]{1,0:T(8,128)S(1)} %bitcast.16, s32[16,24]{1,0:T(8,128)S(1)} %bitcast.15, s32[16]{0:T(128)S(1)} %bitcast.18, ...), custom_call_target="tpu_custom_call" | custom-call | flops 400000000 | bytes 9000000 | tf_op jit(solution)/shard_map/pallas_call | solution.py:104
  30.9 13.6 %all_to_all.9 = f32[8,2,24]{2,1,0:T(2,128)S(1)} all-to-all(f32[8,2,24]{2,1,0:T(2,128)S(1)} %bitcast.10), channel_id=1, replica_groups=mesh['groups'=2,'shard'=8,'sub'=2] {'shard'}, dimensions={0} | all-to-all | bytes 3072 | tf_op jit(solution)/shard_map/all_to_all | solution.py:117
  44.4 0.6 %copy.10 = f32[1,16,24]{2,1,0:T(8,128)} copy(f32[1,16,24]{2,1,0:T(8,128)S(1)} %bitcast.19) | data formatting | bytes 3072
  (15 shorter events, 0.4 us)
Async XLA Ops:
  0.0 21.3 %collective-permute-start.11 = (bf16[128,128,128]{2,1,0:T(8,128)(2,1)}, bf16[128,128,128]{2,1,0:T(8,128)(2,1)S(1)}, u32[]{:S(2)}, u32[]{:S(2)}) collective-permute-start(bf16[128,128,128]{2,1,0:T(8,128)(2,1)} %refs_16_.1), channel_id=1, source_target_pairs={{0,1},{1,0},{2,3},{3,2},{4,5},{5,4},{6,7},{7,6},{8,9},{9,8},{10,11... | collective-permute-start | bytes 12582920 | tf_op jit(solution)/shard_map/ppermute | solution.py:91
  0.5 13.9 %collective-permute-start.7 = (bf16[8,32,128]{2,1,0:T(8,128)(2,1)}, bf16[8,32,128]{2,1,0:T(8,128)(2,1)S(1)}, u32[]{:S(2)}, u32[]{:S(2)}) collective-permute-start(bf16[8,32,128]{2,1,0:T(8,128)(2,1)} %refs_8_.1), channel_id=1, source_target_pairs={{0,8},{2,10},{4,12},{6,14},{8,0},{10,2},{12,4},{14,6},{1,9},{3,11}... | collective-permute-start | bytes 196616 | tf_op jit(solution)/shard_map/ppermute | solution.py:89
  4.0 10.4 %collective-permute-start.5 = (bf16[8,32,128]{2,1,0:T(8,128)(2,1)}, bf16[8,32,128]{2,1,0:T(8,128)(2,1)S(1)}, u32[]{:S(2)}, u32[]{:S(2)}) collective-permute-start(bf16[8,32,128]{2,1,0:T(8,128)(2,1)} %refs_8_.1), channel_id=1, source_target_pairs={{0,4},{2,6},{4,0},{6,2},{8,12},{10,14},{12,8},{14,10},{1,5},{3,7},... | collective-permute-start | bytes 196616 | tf_op jit(solution)/shard_map/ppermute | solution.py:89
  5.6 10.8 %collective-permute-start.9 = (bf16[8,32,128]{2,1,0:T(8,128)(2,1)}, bf16[8,32,128]{2,1,0:T(8,128)(2,1)S(1)}, u32[]{:S(2)}, u32[]{:S(2)}) collective-permute-start(bf16[8,32,128]{2,1,0:T(8,128)(2,1)} %refs_8_.1), channel_id=1, source_target_pairs={{0,12},{2,14},{4,8},{6,10},{8,4},{10,6},{12,0},{14,2},{1,13},{3,15... | collective-permute-start | bytes 196616 | tf_op jit(solution)/shard_map/ppermute | solution.py:89
  5.6 1.8 %collective-permute-start.2 = (s32[16,1]{0,1:T(1,128)}, s32[16,1]{0,1:T(1,128)S(1)}, u32[]{:S(2)}, u32[]{:S(2)}) collective-permute-start(s32[16,1]{0,1:T(1,128)} %param.11), channel_id=1, source_target_pairs={{0,1},{1,0},{2,3},{3,2},{4,5},{5,4},{6,7},{7,6},{8,9},{9,8},{10,11... | collective-permute-start | bytes 200 | tf_op jit(solution)/shard_map/ppermute | solution.py:98
  7.5 1.3 %collective-permute-start.3 = (s32[128]{0:T(128)}, s32[128]{0:T(128)S(1)}, u32[]{:S(2)}, u32[]{:S(2)}) collective-permute-start(s32[128]{0:T(128)} %refs_3_.1), channel_id=1, source_target_pairs={{0,1},{1,0},{2,3},{3,2},{4,5},{5,4},{6,7},{7,6},{8,9},{9,8},{10,11... | collective-permute-start | bytes 1544 | tf_op jit(solution)/shard_map/ppermute | solution.py:98
  8.8 1.4 %collective-permute-start.1 = (s32[16,1,24]{2,0,1:T(8,128)}, s32[16,1,24]{2,0,1:T(8,128)S(1)}, u32[]{:S(2)}, u32[]{:S(2)}) collective-permute-start(s32[16,1,24]{2,0,1:T(8,128)} %bitcast.13), channel_id=1, source_target_pairs={{0,1},{1,0},{2,3},{3,2},{4,5},{5,4},{6,7},{7,6},{8,9},{9,8},{10,11... | collective-permute-start | bytes 4616 | tf_op jit(solution)/shard_map/ppermute | solution.py:98
  10.2 1.4 %collective-permute-start = (s32[16,1,24]{2,0,1:T(8,128)}, s32[16,1,24]{2,0,1:T(8,128)S(1)}, u32[]{:S(2)}, u32[]{:S(2)}) collective-permute-start(s32[16,1,24]{2,0,1:T(8,128)} %bitcast.11), channel_id=1, source_target_pairs={{0,1},{1,0},{2,3},{3,2},{4,5},{5,4},{6,7},{7,6},{8,9},{9,8},{10,11... | collective-permute-start | bytes 4616 | tf_op jit(solution)/shard_map/ppermute | solution.py:98
  11.5 5.7 %collective-permute-start.4 = (bf16[8,32,128]{2,1,0:T(8,128)(2,1)}, bf16[8,32,128]{2,1,0:T(8,128)(2,1)S(1)}, u32[]{:S(2)}, u32[]{:S(2)}) collective-permute-start(bf16[8,32,128]{2,1,0:T(8,128)(2,1)} %refs_8_.1), channel_id=1, source_target_pairs={{0,2},{2,0},{4,6},{6,4},{8,10},{10,8},{12,14},{14,12},{1,3},{3,1},... | collective-permute-start | bytes 196616 | tf_op jit(solution)/shard_map/ppermute | solution.py:89
  14.4 5.0 %collective-permute-start.8 = (bf16[8,32,128]{2,1,0:T(8,128)(2,1)S(1)}, bf16[8,32,128]{2,1,0:T(8,128)(2,1)S(1)}, u32[]{:S(2)}, u32[]{:S(2)}) collective-permute-start(bf16[8,32,128]{2,1,0:T(8,128)(2,1)S(1)} %collective-permute-done.7.refs_12_), channel_id=1, source_target_pairs={{0,2},{2,0},{4,6},{6,4},{8,10},{10,8},{12,14},{14,12},{1,3},{3,1},... | collective-permute-start | bytes 196616 | tf_op jit(solution)/shard_map/ppermute | solution.py:89
  14.4 6.1 %collective-permute-start.6 = (bf16[8,32,128]{2,1,0:T(8,128)(2,1)S(1)}, bf16[8,32,128]{2,1,0:T(8,128)(2,1)S(1)}, u32[]{:S(2)}, u32[]{:S(2)}) collective-permute-start(bf16[8,32,128]{2,1,0:T(8,128)(2,1)S(1)} %collective-permute-done.5.refs_10_), channel_id=1, source_target_pairs={{0,2},{2,0},{4,6},{6,4},{8,10},{10,8},{12,14},{14,12},{1,3},{3,1},... | collective-permute-start | bytes 196616 | tf_op jit(solution)/shard_map/ppermute | solution.py:89
  16.4 4.8 %collective-permute-start.10 = (bf16[8,32,128]{2,1,0:T(8,128)(2,1)S(1)}, bf16[8,32,128]{2,1,0:T(8,128)(2,1)S(1)}, u32[]{:S(2)}, u32[]{:S(2)}) collective-permute-start(bf16[8,32,128]{2,1,0:T(8,128)(2,1)S(1)} %collective-permute-done.9.refs_14_), channel_id=1, source_target_pairs={{0,2},{2,0},{4,6},{6,4},{8,10},{10,8},{12,14},{14,12},{1,3},{3,1},... | collective-permute-start | bytes 196616 | tf_op jit(solution)/shard_map/ppermute | solution.py:89
  21.3 2.2 %copy-start = (bf16[128,128,128]{2,1,0:T(8,128)(2,1)S(1)}, bf16[128,128,128]{2,1,0:T(8,128)(2,1)}, u32[]{:S(2)}) copy-start(bf16[128,128,128]{2,1,0:T(8,128)(2,1)} %refs_16_.1) | copy-start | bytes 12582916
  23.4 0.8 %copy-start.1 = (bf16[8,32,128]{2,1,0:T(8,128)(2,1)S(1)}, bf16[8,32,128]{2,1,0:T(8,128)(2,1)}, u32[]{:S(2)}) copy-start(bf16[8,32,128]{2,1,0:T(8,128)(2,1)} %refs_8_.1) | copy-start | bytes 196612
  24.3 0.7 %copy-start.2 = (s32[16,1,24]{2,1,0:T(1,128)S(1)}, s32[16,1,24]{2,1,0:T(1,128)}, u32[]{:S(2)}) copy-start(s32[16,1,24]{2,1,0:T(1,128)} %param.9) | copy-start | bytes 4612
  25.0 0.7 %copy-start.3 = (s32[16,1,24]{2,1,0:T(1,128)S(1)}, s32[16,1,24]{2,1,0:T(1,128)}, u32[]{:S(2)}) copy-start(s32[16,1,24]{2,1,0:T(1,128)} %param.10) | copy-start | bytes 4612
  25.7 0.7 %copy-start.4 = (s32[16,1]{0,1:T(1,128)S(1)}, s32[16,1]{0,1:T(1,128)}, u32[]{:S(2)}) copy-start(s32[16,1]{0,1:T(1,128)} %param.11) | copy-start | bytes 196
  26.3 0.7 %copy-start.5 = (s32[128]{0:T(128)S(1)}, s32[128]{0:T(128)}, u32[]{:S(2)}) copy-start(s32[128]{0:T(128)} %refs_3_.1) | copy-start | bytes 1540

commit v3 on v2

v3 whole, which is shorter than its diff:
```python
import functools

import jax
import jax.numpy as jnp
from jax import lax
from jax.experimental import pallas as pl
from jax.experimental.pallas import tpu as pltpu
from jax.sharding import PartitionSpec as P

GROUPS = 8
CHUNKS = 4


def pack_kernel(query_hbm, passage_hbm, count_hbm, length_hbm, out_ref, query_ref, passage_ref, count_ref, length_ref, sems):
    copies = [
        pltpu.make_async_copy(src, dst, sems.at[i])
        for i, (src, dst) in enumerate(
            ((query_hbm, query_ref), (passage_hbm, passage_ref), (count_hbm, count_ref), (length_hbm, length_ref))
        )
    ]
    for copy in copies:
        copy.start()
    for copy in copies:
        copy.wait()
    sources, cap = query_ref.shape
    out_ref[:sources, :cap] = query_ref[...]
    out_ref[sources : 2 * sources, :cap] = passage_ref[...]
    out_ref[2 * sources : 2 * sources + 1, :sources] = count_ref[...].reshape(1, sources)
    out_ref[2 * sources + 1 : 2 * sources + 2, : length_ref.shape[0]] = length_ref[...].reshape(1, -1)


def score_kernel(shards, distances, first, pack, cap, *refs):
    meta_hbm, refs = refs[:2], refs[2:]
    pieces, refs = refs[: len(distances)], refs[len(distances) :]
    own_hbm, other_ref, refs = refs[0], refs[1], refs[2:]
    earlier_ref, refs = (None, refs) if first else (refs[0], refs[1:])
    out_ref, refs = refs[0], refs[1:]
    own_ref, refs = (refs[0], refs[1:]) if first else (own_hbm, refs)
    query_ref, best_ref, meta_ref, work_ref, meta_sems, own_sems, piece_sems = refs
    q_tok, width = query_ref.shape[2:]
    pass_dev, tok_slots = own_ref.shape[:2]
    sources = shards * 2
    per_source = best_ref.shape[0]
    lanes = pack * q_tok
    me, core = lax.axis_index("shard"), lax.axis_index("sub")
    copies = [pltpu.make_async_copy(meta_hbm[i], meta_ref.at[i], meta_sems.at[i]) for i in range(2)]
    copies += [pltpu.make_async_copy(piece, query_ref.at[i], piece_sems.at[i]) for i, piece in enumerate(pieces)]
    own_copies = []
    if first:
        size = pass_dev // CHUNKS
        own_copies = [
            pltpu.make_async_copy(own_hbm.at[pl.ds(i * size, size)], own_ref.at[pl.ds(i * size, size)], own_sems.at[i])
            for i in range(CHUNKS)
        ]
    for copy in copies + own_copies:
        copy.start()
    best_ref[...] = jnp.zeros_like(best_ref)
    token = lax.broadcasted_iota(jnp.int32, (tok_slots, lanes), 0)
    place = lax.broadcasted_iota(jnp.int32, (1, lanes), 1) // q_tok
    blank = jnp.zeros((q_tok, width), query_ref.dtype)
    for copy in copies:
        copy.wait()

    for which, passages in ((1, other_ref), (0, own_ref)):
        owner = core if which == 0 else 1 - core
        if which == 0:
            for copy in own_copies:
                copy.wait()

        def shard_of(i):
            return jnp.bitwise_xor(me, i * 2 + distances[0])

        def list_source(i, total):
            live = meta_ref[which, 2 * sources, shard_of(i) * 2 + core]
            for g in range(per_source):
                work_ref[total + g] = i * per_source + g
            return total + (live + pack - 1) // pack

        total = lax.fori_loop(0, len(distances), list_source, 0)
        for g in range(GROUPS):
            work_ref[total + g] = 0

        def one_step(step, carry):
            for j in range(GROUPS):
                work = work_ref[step * GROUPS + j]
                i, g = work // per_source, work % per_source
                source = shard_of(i) * 2 + core
                rows, cols, limit = [], [], jnp.zeros((1, lanes), jnp.int32)
                for a in range(pack):
                    slot = jnp.minimum(g * pack + a, cap - 1)
                    query, passage = meta_ref[which, source, slot], meta_ref[which, sources + source, slot]
                    rows.append(jnp.concatenate([blank] * a + [query_ref[i, query]] + [blank] * (pack - 1 - a), axis=1))
                    cols.append(passages[passage])
                    limit = jnp.where(place == a, meta_ref[which, 2 * sources + 1, passage], limit)
                sims = lax.dot_general(
                    jnp.concatenate(cols, axis=1), jnp.concatenate(rows, axis=0),
                    (((1,), (1,)), ((), ())), preferred_element_type=jnp.float32,
                )
                best = jnp.max(jnp.where(token < limit, sims, -1e30), axis=0, keepdims=True)
                best = jnp.where(place + g * pack < meta_ref[which, 2 * sources, source], best, 0.0)
                best_ref[g, pl.ds(shard_of(i) * 2 + owner, 1), :] = best
            return carry

        lax.fori_loop(0, (total + GROUPS - 1) // GROUPS, one_step, 0)

    best = jnp.concatenate([best_ref[g] for g in range(per_source)], axis=1)
    high = best.astype(jnp.bfloat16)
    rest = best - high.astype(jnp.float32)
    middle = rest.astype(jnp.bfloat16)
    low = (rest - middle.astype(jnp.float32)).astype(jnp.bfloat16)
    row = lax.broadcasted_iota(jnp.int32, (per_source * lanes, 128), 0)
    col = lax.broadcasted_iota(jnp.int32, (per_source * lanes, 128), 1)
    add = jnp.where(row // q_tok == col, 1.0, 0.0).astype(jnp.bfloat16)
    parts = jnp.dot(jnp.concatenate([high, middle, low], axis=0), add, preferred_element_type=jnp.float32)
    n = best.shape[0]
    score = ((parts[:n] + parts[n : 2 * n] + parts[2 * n :]) / q_tok)[:, :cap]
    out_ref[...] = score if first else earlier_ref[...] + score


def on_device(shards, queries, passages, passage_len, slot_query, slot_passage, slot_count):
    sources, _, cap = slot_query.shape
    q_dev, q_tok, width = queries.shape
    pack = 128 // q_tok
    per_source = -(-cap // pack)
    swap = [(0, 1), (1, 0)]
    vmem, hbm, anywhere = (pl.BlockSpec(memory_space=space) for space in (pltpu.VMEM, pltpu.HBM, pl.ANY))

    def swapped(piece, d):
        return lax.ppermute(piece, "shard", [(i, i ^ d) for i in range(shards)])

    def in_hbm(x):
        return pltpu.with_memory_space_constraint(x, pltpu.HBM)

    other_passages = lax.ppermute(passages, "sub", swap)
    pieces = [queries] + [None] * (shards - 1)
    for d in range(2, shards, 2):
        pieces[d] = swapped(queries, d)
    for d in range(1, shards, 2):
        pieces[d] = swapped(pieces[d - 1], 1)

    meta_rows = -(-(2 * sources + 2) // 8) * 8
    meta = pl.pallas_call(
        pack_kernel,
        out_shape=jax.ShapeDtypeStruct((meta_rows, 128), jnp.int32),
        in_specs=[hbm] * 4,
        out_specs=vmem,
        scratch_shapes=[
            pltpu.VMEM((sources, cap), jnp.int32),
            pltpu.VMEM((sources, cap), jnp.int32),
            pltpu.VMEM((sources,), jnp.int32),
            pltpu.VMEM(passage_len.shape, jnp.int32),
            pltpu.SemaphoreType.DMA((4,)),
        ],
        compiler_params=pltpu.CompilerParams(vmem_limit_bytes=4 * 1024 * 1024),
    )(*map(in_hbm, (slot_query.reshape(sources, cap), slot_passage.reshape(sources, cap), slot_count.reshape(sources), passage_len)))
    other_meta = lax.ppermute(meta, "sub", swap)

    def scored(first, own_passages, earlier):
        distances = range(0 if first else 1, shards, 2)
        scores = jax.ShapeDtypeStruct((sources, cap), jnp.float32)
        return pl.pallas_call(
            functools.partial(score_kernel, shards, distances, first, pack, cap),
            out_shape=(scores, jax.ShapeDtypeStruct(passages.shape, passages.dtype)) if first else scores,
            in_specs=[anywhere] * (2 + len(distances)) + [hbm if first else vmem, vmem] + [vmem] * len(earlier),
            out_specs=(vmem, vmem) if first else vmem,
            scratch_shapes=[
                pltpu.VMEM((len(distances), *queries.shape), queries.dtype),
                pltpu.VMEM((per_source, sources, 128), jnp.float32),
                pltpu.SMEM((2, meta_rows, 128), jnp.int32),
                pltpu.SMEM((len(distances) * per_source + 2 * GROUPS,), jnp.int32),
                pltpu.SemaphoreType.DMA((2,)),
                pltpu.SemaphoreType.DMA((CHUNKS,)),
                pltpu.SemaphoreType.DMA((len(distances),)),
            ],
            compiler_params=pltpu.CompilerParams(vmem_limit_bytes=20 * 1024 * 1024),
            cost_estimate=pl.CostEstimate(flops=1_000_000_000, bytes_accessed=9_000_000, transcendentals=0),
        )(meta, other_meta, *(pieces[d] for d in distances), own_passages, other_passages, *earlier)

    pieces[0] = in_hbm(queries)
    scores, own_passages = scored(True, in_hbm(passages), ())
    scores = scored(False, own_passages, (scores,))
    returned = lax.all_to_all(scores, "shard", split_axis=0, concat_axis=0, tiled=True)
    return returned[None]


def solution(mesh):
    return jax.shard_map(
        functools.partial(on_device, mesh.shape["shard"]),
        mesh=mesh,
        in_specs=(
            P(("groups", "shard", "sub"), None, None),
            P(("shard", "sub"), None, None),
            P(("shard", "sub")),
            P("groups", ("shard", "sub"), None),
            P("groups", ("shard", "sub"), None),
            P("groups", ("shard", "sub")),
        ),
        out_specs=P(("groups", "shard", "sub"), None, None),
        check_vma=False,
    )
```

time: 44.8 us -> 32.8 us (0.73); the launches traced: 45 us -> 32.6 us
  waiting for transfers between devices: 9.73 us -> 1.51 us
  local copies, waits for them, and re-layouts: 6.33 us -> 0.6 us
  Pallas kernels: 3.88 us -> 6.52 us
  blocking collectives: 13.6 us -> 12.4 us
    unnamed x13 -> x1, local copies, waits for them, and re-layouts: 6.33 us -> 0.6 us
    ppermute x7, waiting for transfers between devices: 4.78 us -> 0.34 us  [swapped(): return lax.ppermute(piece, 'shard', [(i, i ^ d) for i in range(shards)])]
    ppermute x4 -> x1, waiting for transfers between devices: 4.94 us -> 1.18 us  [on_device(): other_meta = lax.ppermute(meta, 'sub', swap)]
    pallas_call x1 -> x3, Pallas kernels: 3.88 us -> 6.52 us  [the longest x2 5.77 us: scored(): pl.pallas_call(functools.partial(score_kernel, shards, distances, first,...]
    all_to_all x1, blocking collectives: 13.6 us -> 12.4 us  [on_device(): lax.all_to_all(scores, 'shard', split_axis=0, concat_axis=0, tiled=True)]
    ppermute x4 -> x1, starting transfers between devices: 0.98 us -> 0.07 us  [on_device(): other_meta = lax.ppermute(meta, 'sub', swap)]
    ppermute x7, starting transfers between devices: 10.1 us -> 11 us  [swapped(): return lax.ppermute(piece, 'shard', [(i, i ^ d) for i in range(shards)])]
  transfers between devices with their start and end apart: 12 -> 9, of which waited for: 8 -> 2; matrix products, arithmetic and copies ran while one was open for 0% -> 0% of each run, Pallas kernels for 0% -> 12%
where the time goes in v3:
time: 32.8 us; the launch traced here: 32.6 us
  blocking collectives  12.4 us (38%)
  starting transfers between devices  11.5 us (35%)
  Pallas kernels  6.52 us (20%)
  waiting for transfers between devices  1.51 us (5%)
  local copies, waits for them, and re-layouts  0.6 us (2%)
    all_to_all x1, blocking collectives, on_device(): lax.all_to_all(scores, 'shard', split_axis=0, concat_axis=0, tiled=True)  12.4 us
    ppermute x7, starting transfers between devices, swapped(): return lax.ppermute(piece, 'shard', [(i, i ^ d) for i in range(shards)])  11 us
    pallas_call x2, Pallas kernels, scored(): pl.pallas_call(functools.partial(score_kernel, shards, distances, first,...  5.77 us
    ppermute x1, waiting for transfers between devices, on_device(): other_meta = lax.ppermute(meta, 'sub', swap)  1.18 us
    pallas_call x1, Pallas kernels, on_device(): pl.pallas_call(pack_kernel, out_shape=jax.ShapeDtypeStruct((meta_rows, 12...  0.75 us
  transfers between devices with their start and end apart: 9, of which 2 were waited for; matrix products, arithmetic and copies ran while one was open for 0% of the time, Pallas kernels for 12%

profile of v3, /device:TPU:0, one launch (start us, length us, event | category | flops | bytes accessed | tf_op | source)
XLA Modules:
  0.0 32.6 jit_solution(6381646636674529165)
XLA Ops:
  0.0 0.5 %collective-permute-start.8 = (bf16[128,128,128]{2,1,0:T(8,128)(2,1)}, bf16[128,128,128]{2,1,0:T(8,128)(2,1)S(1)}, u32[]{:S(2)}, u32[]{:S(2)}) collective-permute-start(bf16[128,128,128]{2,1,0:T(8,128)(2,1)} %refs_6_.1), channel_id=1, source_target_pairs={{0,1},{1,0},{2,3},{3,2},{4,5},{5,4},{6,7},{7,6},{8,9},{9,8},{10,11... | collective-permute-start | bytes 12582920 | tf_op jit(solution)/shard_map/ppermute | solution.py:134
  0.5 2.6 %collective-permute-start.2 = (bf16[8,32,128]{2,1,0:T(8,128)(2,1)}, bf16[8,32,128]{2,1,0:T(8,128)(2,1)S(1)}, u32[]{:S(2)}, u32[]{:S(2)}) collective-permute-start(bf16[8,32,128]{2,1,0:T(8,128)(2,1)} %refs_2_.1), channel_id=1, source_target_pairs={{0,4},{2,6},{4,0},{6,2},{8,12},{10,14},{12,8},{14,10},{1,5},{3,7},... | collective-permute-start | bytes 196616 | tf_op jit(solution)/shard_map/ppermute | solution.py:129
  3.0 2.6 %collective-permute-start.4 = (bf16[8,32,128]{2,1,0:T(8,128)(2,1)}, bf16[8,32,128]{2,1,0:T(8,128)(2,1)S(1)}, u32[]{:S(2)}, u32[]{:S(2)}) collective-permute-start(bf16[8,32,128]{2,1,0:T(8,128)(2,1)} %refs_2_.1), channel_id=1, source_target_pairs={{0,8},{2,10},{4,12},{6,14},{8,0},{10,2},{12,4},{14,6},{1,9},{3,11}... | collective-permute-start | bytes 196616 | tf_op jit(solution)/shard_map/ppermute | solution.py:129
  5.6 0.0 collective-permute-start.6
  5.6 0.8 %shard_map.64.refs_0_ = s32[40,128]{1,0:T(8,128)S(1)} custom-call(s32[16,24]{1,0:T(8,128)} %bitcast.7, s32[16,24]{1,0:T(8,128)} %bitcast.8, s32[16]{0:T(128)} %bitcast.9, s32[128]{0:T(128)} %length_hbm.1), custom_call_target="tpu_custom_call" | custom-call | tf_op jit(solution)/shard_map/pallas_call | solution.py:142
  6.4 0.1 collective-permute-start
  6.5 1.2 %collective-permute-done.refs_1_ = s32[40,128]{1,0:T(8,128)S(1)} collective-permute-done((s32[40,128]{1,0:T(8,128)S(1)}, s32[40,128]{1,0:T(8,128)S(1)}, u32[]{:S(2)}, u32[]{:S(2)}) %collective-permute-start) | collective-permute-done | bytes 20512 | tf_op jit(solution)/shard_map/ppermute | solution.py:156
  7.6 2.5 %collective-permute-start.1 = (bf16[8,32,128]{2,1,0:T(8,128)(2,1)}, bf16[8,32,128]{2,1,0:T(8,128)(2,1)S(1)}, u32[]{:S(2)}, u32[]{:S(2)}) collective-permute-start(bf16[8,32,128]{2,1,0:T(8,128)(2,1)} %refs_2_.1), channel_id=1, source_target_pairs={{0,2},{2,0},{4,6},{6,4},{8,10},{10,8},{12,14},{14,12},{1,3},{3,1},... | collective-permute-start | bytes 196616 | tf_op jit(solution)/shard_map/ppermute | solution.py:129
  10.2 0.0 collective-permute-done.2.refs_3_
  10.2 0.0 collective-permute-start.3
  10.2 0.0 collective-permute-done.4.refs_4_
  10.2 2.0 %collective-permute-start.5 = (bf16[8,32,128]{2,1,0:T(8,128)(2,1)S(1)}, bf16[8,32,128]{2,1,0:T(8,128)(2,1)S(1)}, u32[]{:S(2)}, u32[]{:S(2)}) collective-permute-start(bf16[8,32,128]{2,1,0:T(8,128)(2,1)S(1)} %collective-permute-done.4.refs_4_), channel_id=1, source_target_pairs={{0,2},{2,0},{4,6},{6,4},{8,10},{10,8},{12,14},{14,12},{1,3},{3,1},... | collective-permute-start | bytes 196616 | tf_op jit(solution)/shard_map/ppermute | solution.py:129
  12.2 0.0 collective-permute-done.6.refs_5_
  12.2 1.3 %collective-permute-start.7 = (bf16[8,32,128]{2,1,0:T(8,128)(2,1)S(1)}, bf16[8,32,128]{2,1,0:T(8,128)(2,1)S(1)}, u32[]{:S(2)}, u32[]{:S(2)}) collective-permute-start(bf16[8,32,128]{2,1,0:T(8,128)(2,1)S(1)} %collective-permute-done.6.refs_5_), channel_id=1, source_target_pairs={{0,2},{2,0},{4,6},{6,4},{8,10},{10,8},{12,14},{14,12},{1,3},{3,1},... | collective-permute-start | bytes 196616 | tf_op jit(solution)/shard_map/ppermute | solution.py:129
  13.5 0.0 collective-permute-done.8.refs_7_
  13.5 3.1 %shard_map.65 = (f32[16,24]{1,0:T(8,128)S(1)}, bf16[128,128,128]{2,1,0:T(8,128)(2,1)S(1)}) custom-call(s32[40,128]{1,0:T(8,128)S(1)} %shard_map.64.refs_0_, s32[40,128]{1,0:T(8,128)S(1)} %collective-permute-done.refs_1_, bf16[8,32,128]{2,1,0:T(8,128)(2,1)} %refs_2_.1, bf16[8,32,128]{2,1,0:T(8,128)(2,1)S(1)} %collective-permute-done.2.refs_3_, ...), custom_call_target="tpu_custom_call" | custom-call | flops 1000000000 | bytes 9000000 | tf_op jit(solution)/shard_map/pallas_call | solution.py:161
  16.6 0.0 collective-permute-done.1.refs_2_
  16.6 0.0 collective-permute-done.3.refs_3_
  16.6 0.0 collective-permute-done.5.refs_4_
  16.7 0.3 collective-permute-done.7.refs_5_
  17.0 2.6 %shard_map.66 = f32[16,24]{1,0:T(8,128)S(1)} custom-call(s32[40,128]{1,0:T(8,128)S(1)} %shard_map.64.refs_0_, s32[40,128]{1,0:T(8,128)S(1)} %collective-permute-done.refs_1_, bf16[8,32,128]{2,1,0:T(8,128)(2,1)S(1)} %collective-permute-done.1.refs_2_, bf16[8,32,128]{2,1,0:T(8,128)(2,1)S(1)} %collective-permute-done.3.refs_3_, ...), custom_call_target="tpu_custom_call" | custom-call | flops 1000000000 | bytes 9000000 | tf_op jit(solution)/shard_map/pallas_call | solution.py:161
  19.6 12.4 %all_to_all.9 = f32[8,2,24]{2,1,0:T(2,128)S(1)} all-to-all(f32[8,2,24]{2,1,0:T(2,128)S(1)} %bitcast.5), channel_id=1, replica_groups=mesh['groups'=2,'shard'=8,'sub'=2] {'shard'}, dimensions={0} | all-to-all | bytes 3072 | tf_op jit(solution)/shard_map/all_to_all | solution.py:182
  32.0 0.6 %copy.8 = f32[1,16,24]{2,1,0:T(8,128)} copy(f32[1,16,24]{2,1,0:T(8,128)S(1)} %bitcast.6) | data formatting | bytes 3072
Async XLA Ops:
  0.0 13.5 %collective-permute-start.8 = (bf16[128,128,128]{2,1,0:T(8,128)(2,1)}, bf16[128,128,128]{2,1,0:T(8,128)(2,1)S(1)}, u32[]{:S(2)}, u32[]{:S(2)}) collective-permute-start(bf16[128,128,128]{2,1,0:T(8,128)(2,1)} %refs_6_.1), channel_id=1, source_target_pairs={{0,1},{1,0},{2,3},{3,2},{4,5},{5,4},{6,7},{7,6},{8,9},{9,8},{10,11... | collective-permute-start | bytes 12582920 | tf_op jit(solution)/shard_map/ppermute | solution.py:134
  0.5 9.7 %collective-permute-start.2 = (bf16[8,32,128]{2,1,0:T(8,128)(2,1)}, bf16[8,32,128]{2,1,0:T(8,128)(2,1)S(1)}, u32[]{:S(2)}, u32[]{:S(2)}) collective-permute-start(bf16[8,32,128]{2,1,0:T(8,128)(2,1)} %refs_2_.1), channel_id=1, source_target_pairs={{0,4},{2,6},{4,0},{6,2},{8,12},{10,14},{12,8},{14,10},{1,5},{3,7},... | collective-permute-start | bytes 196616 | tf_op jit(solution)/shard_map/ppermute | solution.py:129
  3.0 7.2 %collective-permute-start.4 = (bf16[8,32,128]{2,1,0:T(8,128)(2,1)}, bf16[8,32,128]{2,1,0:T(8,128)(2,1)S(1)}, u32[]{:S(2)}, u32[]{:S(2)}) collective-permute-start(bf16[8,32,128]{2,1,0:T(8,128)(2,1)} %refs_2_.1), channel_id=1, source_target_pairs={{0,8},{2,10},{4,12},{6,14},{8,0},{10,2},{12,4},{14,6},{1,9},{3,11}... | collective-permute-start | bytes 196616 | tf_op jit(solution)/shard_map/ppermute | solution.py:129
  5.6 6.6 %collective-permute-start.6 = (bf16[8,32,128]{2,1,0:T(8,128)(2,1)}, bf16[8,32,128]{2,1,0:T(8,128)(2,1)S(1)}, u32[]{:S(2)}, u32[]{:S(2)}) collective-permute-start(bf16[8,32,128]{2,1,0:T(8,128)(2,1)} %refs_2_.1), channel_id=1, source_target_pairs={{0,12},{2,14},{4,8},{6,10},{8,4},{10,6},{12,0},{14,2},{1,13},{3,15... | collective-permute-start | bytes 196616 | tf_op jit(solution)/shard_map/ppermute | solution.py:129
  6.4 1.3 %collective-permute-start = (s32[40,128]{1,0:T(8,128)S(1)}, s32[40,128]{1,0:T(8,128)S(1)}, u32[]{:S(2)}, u32[]{:S(2)}) collective-permute-start(s32[40,128]{1,0:T(8,128)S(1)} %shard_map.64.refs_0_), channel_id=1, source_target_pairs={{0,1},{1,0},{2,3},{3,2},{4,5},{5,4},{6,7},{7,6},{8,9},{9,8},{10,11... | collective-permute-start | bytes 61448 | tf_op jit(solution)/shard_map/ppermute | solution.py:156
  7.6 9.0 %collective-permute-start.1 = (bf16[8,32,128]{2,1,0:T(8,128)(2,1)}, bf16[8,32,128]{2,1,0:T(8,128)(2,1)S(1)}, u32[]{:S(2)}, u32[]{:S(2)}) collective-permute-start(bf16[8,32,128]{2,1,0:T(8,128)(2,1)} %refs_2_.1), channel_id=1, source_target_pairs={{0,2},{2,0},{4,6},{6,4},{8,10},{10,8},{12,14},{14,12},{1,3},{3,1},... | collective-permute-start | bytes 196616 | tf_op jit(solution)/shard_map/ppermute | solution.py:129
  10.2 6.5 %collective-permute-start.3 = (bf16[8,32,128]{2,1,0:T(8,128)(2,1)S(1)}, bf16[8,32,128]{2,1,0:T(8,128)(2,1)S(1)}, u32[]{:S(2)}, u32[]{:S(2)}) collective-permute-start(bf16[8,32,128]{2,1,0:T(8,128)(2,1)S(1)} %collective-permute-done.2.refs_3_), channel_id=1, source_target_pairs={{0,2},{2,0},{4,6},{6,4},{8,10},{10,8},{12,14},{14,12},{1,3},{3,1},... | collective-permute-start | bytes 196616 | tf_op jit(solution)/shard_map/ppermute | solution.py:129
  10.2 6.5 %collective-permute-start.5 = (bf16[8,32,128]{2,1,0:T(8,128)(2,1)S(1)}, bf16[8,32,128]{2,1,0:T(8,128)(2,1)S(1)}, u32[]{:S(2)}, u32[]{:S(2)}) collective-permute-start(bf16[8,32,128]{2,1,0:T(8,128)(2,1)S(1)} %collective-permute-done.4.refs_4_), channel_id=1, source_target_pairs={{0,2},{2,0},{4,6},{6,4},{8,10},{10,8},{12,14},{14,12},{1,3},{3,1},... | collective-permute-start | bytes 196616 | tf_op jit(solution)/shard_map/ppermute | solution.py:129
  12.2 4.8 %collective-permute-start.7 = (bf16[8,32,128]{2,1,0:T(8,128)(2,1)S(1)}, bf16[8,32,128]{2,1,0:T(8,128)(2,1)S(1)}, u32[]{:S(2)}, u32[]{:S(2)}) collective-permute-start(bf16[8,32,128]{2,1,0:T(8,128)(2,1)S(1)} %collective-permute-done.6.refs_5_), channel_id=1, source_target_pairs={{0,2},{2,0},{4,6},{6,4},{8,10},{10,8},{12,14},{14,12},{1,3},{3,1},... | collective-permute-start | bytes 196616 | tf_op jit(solution)/shard_map/ppermute | solution.py:129

commit v4 on v3

v4 whole, which is shorter than its diff:
```python
import functools

import jax
import jax.numpy as jnp
from jax import lax
from jax.experimental import pallas as pl
from jax.experimental.pallas import tpu as pltpu
from jax.sharding import PartitionSpec as P

GROUPS = 8
CHUNKS = 8
SHIFT = 8


def pack_kernel(query_hbm, passage_hbm, count_hbm, length_hbm, out_ref, query_ref, passage_ref, count_ref, length_ref, sems):
    copies = [
        pltpu.make_async_copy(src, dst, sems.at[i])
        for i, (src, dst) in enumerate(
            ((query_hbm, query_ref), (passage_hbm, passage_ref), (count_hbm, count_ref), (length_hbm, length_ref))
        )
    ]
    for copy in copies:
        copy.start()
    for copy in copies:
        copy.wait()
    sources, cap = query_ref.shape
    out_ref[:sources, :cap] = query_ref[...]
    out_ref[sources : 2 * sources, :cap] = passage_ref[...]
    out_ref[2 * sources : 2 * sources + 1, :sources] = count_ref[...].reshape(1, sources)
    out_ref[2 * sources + 1 : 2 * sources + 2, : length_ref.shape[0]] = length_ref[...].reshape(1, -1)


def score_kernel(shards, distances, pack, cap, first, *refs):
    n = len(distances)
    meta_hbm, pieces, (own_hbm, other_ref), refs = refs[:2], refs[2 : 2 + n], refs[2 + n : 4 + n], refs[4 + n :]
    outs, refs = refs[:n], refs[n:]
    own_ref, refs = (refs[0], refs[1:]) if first else (own_hbm, refs)
    query_ref, best_ref, meta_ref, work_ref, meta_sems, piece_sems, own_sems = refs
    q_tok, width = query_ref.shape[2:]
    pass_dev, tok_slots = other_ref.shape[:2]
    sources = shards * 2
    per_source = best_ref.shape[0]
    lanes = pack * q_tok
    q_bits = q_tok.bit_length() - 1
    me, core = lax.axis_index("shard"), lax.axis_index("sub")
    copies = [pltpu.make_async_copy(meta_hbm[i], meta_ref.at[i], meta_sems.at[i]) for i in range(2)]
    copies += [pltpu.make_async_copy(piece, query_ref.at[i], piece_sems.at[i]) for i, piece in enumerate(pieces)]
    size = pass_dev // CHUNKS
    own_copies = [
        pltpu.make_async_copy(own_hbm.at[pl.ds(i * size, size)], own_ref.at[pl.ds(i * size, size)], own_sems.at[i])
        for i in range(CHUNKS if first else 0)
    ]
    for copy in copies + own_copies:
        copy.start()
    best_ref[...] = jnp.zeros_like(best_ref)
    token = lax.broadcasted_iota(jnp.int32, (tok_slots, lanes), 0)
    place = lax.shift_right_logical(lax.broadcasted_iota(jnp.int32, (1, lanes), 1), q_bits)
    blank = jnp.zeros((q_tok, width), query_ref.dtype)
    for copy in copies:
        copy.wait()

    for which, passages in ((1, other_ref), (0, own_ref)):
        owner = core if which == 0 else 1 - core
        if which == 0:
            for copy in own_copies:
                copy.wait()

        def source_of(i):
            return jnp.bitwise_xor(me, i * 2 + distances[0]) * 2 + core

        def list_source(i, total):
            live = meta_ref[which, 2 * sources, source_of(i)]
            for g in range(per_source):
                work_ref[total + g] = (i << SHIFT) + g
            return total + lax.shift_right_logical(live + pack - 1, pack.bit_length() - 1)

        total = lax.fori_loop(0, n, list_source, 0)
        for g in range(GROUPS):
            work_ref[total + g] = 0

        def one_step(step, carry):
            for j in range(GROUPS):
                work = work_ref[step * GROUPS + j]
                i, g = lax.shift_right_logical(work, SHIFT), jnp.bitwise_and(work, (1 << SHIFT) - 1)
                source = source_of(i)
                rows, cols, limit = [], [], jnp.zeros((1, lanes), jnp.int32)
                for a in range(pack):
                    slot = g * pack + a
                    if cap % pack:
                        slot = jnp.minimum(slot, cap - 1)
                    query, passage = meta_ref[which, source, slot], meta_ref[which, sources + source, slot]
                    rows.append(jnp.concatenate([blank] * a + [query_ref[i, query]] + [blank] * (pack - 1 - a), axis=1))
                    cols.append(passages[passage])
                    limit = jnp.where(place == a, meta_ref[which, 2 * sources + 1, passage], limit)
                sims = lax.dot_general(
                    jnp.concatenate(cols, axis=1), jnp.concatenate(rows, axis=0),
                    (((1,), (1,)), ((), ())), preferred_element_type=jnp.float32,
                )
                best = jnp.max(jnp.where(token < limit, sims, -1e30), axis=0, keepdims=True)
                best = jnp.where(place + g * pack < meta_ref[which, 2 * sources, source], best, 0.0)
                best_ref[g, pl.ds(i * 2 + owner, 1), :] = best
            return carry

        lax.fori_loop(0, lax.shift_right_logical(total + GROUPS - 1, GROUPS.bit_length() - 1), one_step, 0)

    best = jnp.concatenate([best_ref[g] for g in range(per_source)], axis=1)
    high = best.astype(jnp.bfloat16)
    rest = best - high.astype(jnp.float32)
    middle = rest.astype(jnp.bfloat16)
    low = (rest - middle.astype(jnp.float32)).astype(jnp.bfloat16)
    row = lax.broadcasted_iota(jnp.int32, (per_source * lanes, 128), 0)
    col = lax.broadcasted_iota(jnp.int32, (per_source * lanes, 128), 1)
    add = jnp.where(lax.shift_right_logical(row, q_bits) == col, 1.0, 0.0).astype(jnp.bfloat16)
    parts = jnp.dot(jnp.concatenate([high, middle, low], axis=0), add, preferred_element_type=jnp.float32)
    rows = best.shape[0]
    score = (parts[:rows] + parts[rows : 2 * rows] + parts[2 * rows :]) * (1.0 / q_tok)
    for i, out in enumerate(outs):
        out[...] = score[2 * i : 2 * i + 2, :cap]


def order_kernel(shards, *refs):
    refs, out_ref = list(refs[:-1]), refs[-1]
    me = lax.axis_index("shard")
    odd = jnp.bitwise_and(me, 1) == 1
    for d in range(shards):
        piece = refs.pop(0)[...]
        if d % 2:
            piece = jnp.where(odd, piece, refs.pop(0)[...])
        out_ref[0, pl.ds(jnp.bitwise_xor(me, d) * 2, 2), :] = piece


def on_device(shards, queries, passages, passage_len, slot_query, slot_passage, slot_count):
    sources, _, cap = slot_query.shape
    q_dev, q_tok, width = queries.shape
    pack = 128 // q_tok
    per_source = -(-cap // pack)
    swap = [(0, 1), (1, 0)]
    vmem, hbm, anywhere = (pl.BlockSpec(memory_space=space) for space in (pltpu.VMEM, pltpu.HBM, pl.ANY))
    params = pltpu.CompilerParams(vmem_limit_bytes=12 * 1024 * 1024)

    def placed(space, *arrays):
        return [pltpu.with_memory_space_constraint(x, space) for x in arrays]

    def swapped(piece, d, senders=range(shards)):
        return lax.ppermute(piece, "shard", [(i, i ^ d) for i in senders])

    meta_rows = -(-(2 * sources + 2) // 8) * 8
    meta = pl.pallas_call(
        pack_kernel,
        out_shape=jax.ShapeDtypeStruct((meta_rows, 128), jnp.int32),
        in_specs=[hbm] * 4,
        out_specs=vmem,
        scratch_shapes=[
            pltpu.VMEM((sources, cap), jnp.int32),
            pltpu.VMEM((sources, cap), jnp.int32),
            pltpu.VMEM((sources,), jnp.int32),
            pltpu.VMEM(passage_len.shape, jnp.int32),
            pltpu.SemaphoreType.DMA((4,)),
        ],
        compiler_params=params,
    )(*placed(pltpu.HBM, slot_query.reshape(sources, cap), slot_passage.reshape(sources, cap), slot_count.reshape(sources), passage_len))
    other_passages = lax.ppermute(passages, "sub", swap)

    pieces = [queries] + [None] * (shards - 1)
    for d in range(2, shards, 2):
        pieces[d] = swapped(queries, d)
    sent_meta, pieces[2] = lax.optimization_barrier((meta, pieces[2]))
    other_meta = lax.ppermute(sent_meta, "sub", swap)
    for d in range(1, shards, 2):
        pieces[d] = swapped(pieces[d - 1], 1)

    def scored(distances, own_passages, first):
        n = len(distances)
        scores = [jax.ShapeDtypeStruct((2, cap), jnp.float32)] * n
        loaded = [jax.ShapeDtypeStruct(passages.shape, passages.dtype)] if first else []
        return pl.pallas_call(
            functools.partial(score_kernel, shards, distances, pack, cap, first),
            out_shape=scores + loaded,
            in_specs=[anywhere] * (2 + n) + [hbm if first else vmem, vmem],
            out_specs=[vmem] * (n + len(loaded)),
            scratch_shapes=[
                pltpu.VMEM((n, *queries.shape), queries.dtype),
                pltpu.VMEM((per_source, 2 * n, 128), jnp.float32),
                pltpu.SMEM((2, meta_rows, 128), jnp.int32),
                pltpu.SMEM((n * per_source + 2 * GROUPS,), jnp.int32),
                pltpu.SemaphoreType.DMA((2,)),
                pltpu.SemaphoreType.DMA((n,)),
                pltpu.SemaphoreType.DMA((CHUNKS,)),
            ],
            compiler_params=params,
            cost_estimate=pl.CostEstimate(flops=1_000_000_000, bytes_accessed=9_000_000, transcendentals=0),
        )(meta, other_meta, *(pieces[d] for d in distances), own_passages, *placed(pltpu.VMEM, other_passages))

    pieces[0] = placed(pltpu.HBM, queries)[0]
    even, odd = range(0, shards, 2), range(1, shards, 2)
    returned = [None] * shards
    *scores, own_passages = scored(even, *placed(pltpu.HBM, passages), True)
    for d, score in zip(even, scores):
        returned[d] = [swapped(score, d) if d else score]
    scores = scored(odd, *placed(pltpu.VMEM, own_passages), False)
    for d, score in zip(odd, scores):
        returned[d] = [swapped(score, d, even)]
    scores, returned[1][0] = lax.optimization_barrier((scores, returned[1][0]))
    for d, score in zip(odd, scores):
        returned[d] += [swapped(score, d, odd)]
    returned = [x for at in returned for x in at]
    return pl.pallas_call(
        functools.partial(order_kernel, shards),
        out_shape=jax.ShapeDtypeStruct((1, sources, cap), jnp.float32),
        in_specs=[vmem] * len(returned),
        out_specs=vmem,
        compiler_params=params,
    )(*returned)


def solution(mesh):
    return jax.shard_map(
        functools.partial(on_device, mesh.shape["shard"]),
        mesh=mesh,
        in_specs=(
            P(("groups", "shard", "sub"), None, None),
            P(("shard", "sub"), None, None),
            P(("shard", "sub")),
            P("groups", ("shard", "sub"), None),
            P("groups", ("shard", "sub"), None),
            P("groups", ("shard", "sub")),
        ),
        out_specs=P(("groups", "shard", "sub"), None, None),
        check_vma=False,
    )
```

time: 32.8 us -> 47.9 us (1.46)
  starting transfers between devices: 11.5 us -> 29.6 us
  blocking collectives: 12.4 us -> 0 us
  waiting for transfers between devices: 1.51 us -> 9.04 us
  Pallas kernels: 6.52 us -> 8.82 us
  local copies, waits for them, and re-layouts: 0.6 us -> 0 us
    ppermute x8 -> x19, starting transfers between devices: 11.1 us -> 29.1 us  [the longest x18 29 us: swapped(): return lax.ppermute(piece, 'shard', [(i, i ^ d) for i in senders])]
    all_to_all x1 -> x0, blocking collectives: 12.4 us -> none  [on_device(): lax.all_to_all(scores, 'shard', split_axis=0, concat_axis=0, tiled=True)]
    ppermute x8 -> x19, waiting for transfers between devices: 1.51 us -> 9.03 us  [the longest x18 9.03 us: swapped(): return lax.ppermute(piece, 'shard', [(i, i ^ d) for i in senders])]
    pallas_call x2 -> x3, Pallas kernels: 5.77 us -> 8.06 us  [the longest x2 7.45 us: scored(): pl.pallas_call(functools.partial(score_kernel, shards, distances, pack, c...]
    unnamed x1 -> x0, local copies, waits for them, and re-layouts: 0.6 us -> none
  transfers between devices with their start and end apart: 9 -> 20, of which waited for: 2 -> 6; matrix products, arithmetic and copies ran while one was open for 0% -> 0% of each run, Pallas kernels for 12% -> 10%
where the time goes in v4:
time: 47.9 us; the launch traced here: 47.6 us
  starting transfers between devices  29.6 us (62%)
  waiting for transfers between devices  9.04 us (19%)
  Pallas kernels  8.82 us (18%)
    ppermute x18, starting transfers between devices, swapped(): return lax.ppermute(piece, 'shard', [(i, i ^ d) for i in senders])  29 us
    ppermute x18, waiting for transfers between devices, swapped(): return lax.ppermute(piece, 'shard', [(i, i ^ d) for i in senders])  9.03 us
    pallas_call x2, Pallas kernels, scored(): pl.pallas_call(functools.partial(score_kernel, shards, distances, pack, c...  7.45 us
  transfers between devices with their start and end apart: 20, of which 6 were waited for; matrix products, arithmetic and copies ran while one was open for 0% of the time, Pallas kernels for 10%

profile of v4, /device:TPU:0, one launch (start us, length us, event | category | flops | bytes accessed | tf_op | source)
XLA Modules:
  0.0 47.6 jit_solution(8616116079500185440)
XLA Ops:
  0.5 2.6 %collective-permute-start = (bf16[8,32,128]{2,1,0:T(8,128)(2,1)}, bf16[8,32,128]{2,1,0:T(8,128)(2,1)S(1)}, u32[]{:S(2)}, u32[]{:S(2)}) collective-permute-start(bf16[8,32,128]{2,1,0:T(8,128)(2,1)} %refs_2_.1), channel_id=1, source_target_pairs={{0,4},{2,6},{4,0},{6,2},{8,12},{10,14},{12,8},{14,10},{1,5},{3,7},... | collective-permute-start | bytes 196616 | tf_op jit(solution)/shard_map/ppermute | solution.py:145
  3.0 2.6 %collective-permute-start.2 = (bf16[8,32,128]{2,1,0:T(8,128)(2,1)}, bf16[8,32,128]{2,1,0:T(8,128)(2,1)S(1)}, u32[]{:S(2)}, u32[]{:S(2)}) collective-permute-start(bf16[8,32,128]{2,1,0:T(8,128)(2,1)} %refs_2_.1), channel_id=1, source_target_pairs={{0,8},{2,10},{4,12},{6,14},{8,0},{10,2},{12,4},{14,6},{1,9},{3,11}... | collective-permute-start | bytes 196616 | tf_op jit(solution)/shard_map/ppermute | solution.py:145
  5.6 0.8 %shard_map.64.refs_0_ = s32[40,128]{1,0:T(8,128)S(1)} custom-call(s32[16,24]{1,0:T(8,128)} %bitcast.3, s32[16,24]{1,0:T(8,128)} %bitcast.4, s32[16]{0:T(128)} %bitcast.5, s32[128]{0:T(128)} %length_hbm.1), custom_call_target="tpu_custom_call" | custom-call | tf_op jit(solution)/shard_map/pallas_call | solution.py:148
  6.5 1.8 %collective-permute-start.5 = (bf16[8,32,128]{2,1,0:T(8,128)(2,1)}, bf16[8,32,128]{2,1,0:T(8,128)(2,1)S(1)}, u32[]{:S(2)}, u32[]{:S(2)}) collective-permute-start(bf16[8,32,128]{2,1,0:T(8,128)(2,1)} %refs_2_.1), channel_id=1, source_target_pairs={{0,2},{2,0},{4,6},{6,4},{8,10},{10,8},{12,14},{14,12},{1,3},{3,1},... | collective-permute-start | bytes 196616 | tf_op jit(solution)/shard_map/ppermute | solution.py:145
  8.3 1.9 %collective-permute-done.2.refs_4_ = bf16[8,32,128]{2,1,0:T(8,128)(2,1)S(1)} collective-permute-done((bf16[8,32,128]{2,1,0:T(8,128)(2,1)}, bf16[8,32,128]{2,1,0:T(8,128)(2,1)S(1)}, u32[]{:S(2)}, u32[]{:S(2)}) %collective-permute-start.2) | collective-permute-done | bytes 65568 | tf_op jit(solution)/shard_map/ppermute | solution.py:145
  10.2 1.5 %collective-permute-start.6 = (bf16[8,32,128]{2,1,0:T(8,128)(2,1)S(1)}, bf16[8,32,128]{2,1,0:T(8,128)(2,1)S(1)}, u32[]{:S(2)}, u32[]{:S(2)}) collective-permute-start(bf16[8,32,128]{2,1,0:T(8,128)(2,1)S(1)} %collective-permute-done.refs_3_), channel_id=1, source_target_pairs={{0,2},{2,0},{4,6},{6,4},{8,10},{10,8},{12,14},{14,12},{1,3},{3,1},... | collective-permute-start | bytes 196616 | tf_op jit(solution)/shard_map/ppermute | solution.py:145
  11.9 1.5 %collective-permute-start.7 = (bf16[8,32,128]{2,1,0:T(8,128)(2,1)S(1)}, bf16[8,32,128]{2,1,0:T(8,128)(2,1)S(1)}, u32[]{:S(2)}, u32[]{:S(2)}) collective-permute-start(bf16[8,32,128]{2,1,0:T(8,128)(2,1)S(1)} %collective-permute-done.2.refs_4_), channel_id=1, source_target_pairs={{0,2},{2,0},{4,6},{6,4},{8,10},{10,8},{12,14},{14,12},{1,3},{3,1},... | collective-permute-start | bytes 196616 | tf_op jit(solution)/shard_map/ppermute | solution.py:145
  14.0 3.9 %shard_map.65 = (f32[2,24]{1,0:T(2,128)S(1)}, f32[2,24]{1,0:T(2,128)S(1)}, f32[2,24]{1,0:T(2,128)S(1)}, f32[2,24]{1,0:T(2,128)S(1)}, bf16[128,128,128]{2,1,0:T(8,128)(2,1)S(1)}) custom-call(s32[40,128]{1,0:T(8,128)S(1)} %shard_map.64.refs_0_, s32[40,128]{1,0:T(8,128)S(1)} %collective-permute-done.1.refs_1_, bf16[8,32,128]{2,1,0:T(8,128)(2,1)} %refs_2_.1, ...), custom_call_target="tpu_custom_call" | custom-call | flops 1000000000 | bytes 9000000 | tf_op jit(solution)/shard_map/pallas_call | solution.py:176
  18.0 3.5 %shard_map.66 = (f32[2,24]{1,0:T(2,128)S(1)}, f32[2,24]{1,0:T(2,128)S(1)}, f32[2,24]{1,0:T(2,128)S(1)}, f32[2,24]{1,0:T(2,128)S(1)}) custom-call(s32[40,128]{1,0:T(8,128)S(1)} %shard_map.64.refs_0_, s32[40,128]{1,0:T(8,128)S(1)} %collective-permute-done.1.refs_1_, bf16[8,32,128]{2,1,0:T(8,128)(2,1)S(1)} %collective-permute-done.5.refs_2_, ...), custom_call_target="tpu_custom_call" | custom-call | flops 1000000000 | bytes 9000000 | tf_op jit(solution)/shard_map/pallas_call | solution.py:176
  21.5 2.1 %collective-permute-start.9 = (f32[2,24]{1,0:T(2,128)S(1)}, f32[2,24]{1,0:T(2,128)S(1)}, u32[]{:S(2)}, u32[]{:S(2)}) collective-permute-start(f32[2,24]{1,0:T(2,128)S(1)} %get-tuple-element.30), channel_id=1, source_target_pairs={{0,2},{4,6},{8,10},{12,14},{1,3},{5,7},{9,11},{13,15},{16,18},{20,... | collective-permute-start | bytes 584 | tf_op jit(solution)/shard_map/ppermute | solution.py:145
  23.6 1.8 %collective-permute-start.12 = (f32[2,24]{1,0:T(2,128)S(1)}, f32[2,24]{1,0:T(2,128)S(1)}, u32[]{:S(2)}, u32[]{:S(2)}) collective-permute-start(f32[2,24]{1,0:T(2,128)S(1)} %get-tuple-element.32), channel_id=1, source_target_pairs={{0,6},{4,2},{8,14},{12,10},{1,7},{5,3},{9,15},{13,11},{16,22},{20,... | collective-permute-start | bytes 584 | tf_op jit(solution)/shard_map/ppermute | solution.py:145
  25.4 2.4 %collective-permute-start.15 = (f32[2,24]{1,0:T(2,128)S(1)}, f32[2,24]{1,0:T(2,128)S(1)}, u32[]{:S(2)}, u32[]{:S(2)}) collective-permute-start(f32[2,24]{1,0:T(2,128)S(1)} %get-tuple-element.34), channel_id=1, source_target_pairs={{0,10},{4,14},{8,2},{12,6},{1,11},{5,15},{9,3},{13,7},{16,26},{20,... | collective-permute-start | bytes 584 | tf_op jit(solution)/shard_map/ppermute | solution.py:145
  27.9 2.6 %collective-permute-start.18 = (f32[2,24]{1,0:T(2,128)S(1)}, f32[2,24]{1,0:T(2,128)S(1)}, u32[]{:S(2)}, u32[]{:S(2)}) collective-permute-start(f32[2,24]{1,0:T(2,128)S(1)} %get-tuple-element.36), channel_id=1, source_target_pairs={{0,14},{4,10},{8,6},{12,2},{1,15},{5,11},{9,7},{13,3},{16,30},{20,... | collective-permute-start | bytes 584 | tf_op jit(solution)/shard_map/ppermute | solution.py:145
  30.4 0.6 %collective-permute-start.11 = (f32[2,24]{1,0:T(2,128)S(1)}, f32[2,24]{1,0:T(2,128)S(1)}, u32[]{:S(2)}, u32[]{:S(2)}) collective-permute-start(f32[2,24]{1,0:T(2,128)S(1)} %get-tuple-element.31), channel_id=1, source_target_pairs={{0,4},{2,6},{4,0},{6,2},{8,12},{10,14},{12,8},{14,10},{1,5},{3,7},... | collective-permute-start | bytes 584 | tf_op jit(solution)/shard_map/ppermute | solution.py:145
  31.1 0.6 %collective-permute-start.14 = (f32[2,24]{1,0:T(2,128)S(1)}, f32[2,24]{1,0:T(2,128)S(1)}, u32[]{:S(2)}, u32[]{:S(2)}) collective-permute-start(f32[2,24]{1,0:T(2,128)S(1)} %get-tuple-element.33), channel_id=1, source_target_pairs={{0,8},{2,10},{4,12},{6,14},{8,0},{10,2},{12,4},{14,6},{1,9},{3,11}... | collective-permute-start | bytes 584 | tf_op jit(solution)/shard_map/ppermute | solution.py:145
  31.6 3.3 %collective-permute-start.17 = (f32[2,24]{1,0:T(2,128)S(1)}, f32[2,24]{1,0:T(2,128)S(1)}, u32[]{:S(2)}, u32[]{:S(2)}) collective-permute-start(f32[2,24]{1,0:T(2,128)S(1)} %get-tuple-element.35), channel_id=1, source_target_pairs={{0,12},{2,14},{4,8},{6,10},{8,4},{10,6},{12,0},{14,2},{1,13},{3,15... | collective-permute-start | bytes 584 | tf_op jit(solution)/shard_map/ppermute | solution.py:145
  34.9 1.3 %collective-permute-start.10 = (f32[2,24]{1,0:T(2,128)S(1)}, f32[2,24]{1,0:T(2,128)S(1)}, u32[]{:S(2)}, u32[]{:S(2)}) collective-permute-start(f32[2,24]{1,0:T(2,128)S(1)} %get-tuple-element.30), channel_id=1, source_target_pairs={{2,0},{6,4},{10,8},{14,12},{3,1},{7,5},{11,9},{15,13},{18,16},{22,... | collective-permute-start | bytes 584 | tf_op jit(solution)/shard_map/ppermute | solution.py:145
  36.2 1.3 %collective-permute-start.13 = (f32[2,24]{1,0:T(2,128)S(1)}, f32[2,24]{1,0:T(2,128)S(1)}, u32[]{:S(2)}, u32[]{:S(2)}) collective-permute-start(f32[2,24]{1,0:T(2,128)S(1)} %get-tuple-element.32), channel_id=1, source_target_pairs={{2,4},{6,0},{10,12},{14,8},{3,5},{7,1},{11,13},{15,9},{18,20},{22,... | collective-permute-start | bytes 584 | tf_op jit(solution)/shard_map/ppermute | solution.py:145
  37.5 1.3 %collective-permute-start.16 = (f32[2,24]{1,0:T(2,128)S(1)}, f32[2,24]{1,0:T(2,128)S(1)}, u32[]{:S(2)}, u32[]{:S(2)}) collective-permute-start(f32[2,24]{1,0:T(2,128)S(1)} %get-tuple-element.34), channel_id=1, source_target_pairs={{2,8},{6,12},{10,0},{14,4},{3,9},{7,13},{11,1},{15,5},{18,24},{22,... | collective-permute-start | bytes 584 | tf_op jit(solution)/shard_map/ppermute | solution.py:145
  38.8 1.3 %collective-permute-start.19 = (f32[2,24]{1,0:T(2,128)S(1)}, f32[2,24]{1,0:T(2,128)S(1)}, u32[]{:S(2)}, u32[]{:S(2)}) collective-permute-start(f32[2,24]{1,0:T(2,128)S(1)} %get-tuple-element.36), channel_id=1, source_target_pairs={{2,12},{6,8},{10,4},{14,0},{3,13},{7,9},{11,5},{15,1},{18,28},{22,... | collective-permute-start | bytes 584 | tf_op jit(solution)/shard_map/ppermute | solution.py:145
  40.4 2.2 %collective-permute-done.13.refs_5_ = f32[2,24]{1,0:T(2,128)S(1)} collective-permute-done((f32[2,24]{1,0:T(2,128)S(1)}, f32[2,24]{1,0:T(2,128)S(1)}, u32[]{:S(2)}, u32[]{:S(2)}) %collective-permute-start.13) | collective-permute-done | bytes 224 | tf_op jit(solution)/shard_map/ppermute | solution.py:145
  42.6 2.2 %collective-permute-done.16.refs_8_ = f32[2,24]{1,0:T(2,128)S(1)} collective-permute-done((f32[2,24]{1,0:T(2,128)S(1)}, f32[2,24]{1,0:T(2,128)S(1)}, u32[]{:S(2)}, u32[]{:S(2)}) %collective-permute-start.16) | collective-permute-done | bytes 224 | tf_op jit(solution)/shard_map/ppermute | solution.py:145
  44.8 2.2 %collective-permute-done.19.refs_11_ = f32[2,24]{1,0:T(2,128)S(1)} collective-permute-done((f32[2,24]{1,0:T(2,128)S(1)}, f32[2,24]{1,0:T(2,128)S(1)}, u32[]{:S(2)}, u32[]{:S(2)}) %collective-permute-start.19) | collective-permute-done | bytes 224 | tf_op jit(solution)/shard_map/ppermute | solution.py:145
  47.0 0.6 %shard_map.67 = f32[1,16,24]{2,1,0:T(8,128)} custom-call(f32[2,24]{1,0:T(2,128)S(1)} %get-tuple-element.23.refs_0_, f32[2,24]{1,0:T(2,128)S(1)} %collective-permute-done.9.refs_1_, f32[2,24]{1,0:T(2,128)S(1)} %collective-permute-done.10.refs_2_, f32[2,24]{1,0:T(2,128)S(1)} %collective-permute-done.11.refs_3_, f32[2,24]{1,0:T(2,128)S(1)} %collective-permute-done.12.refs_4_, ...), custom_call_target="tpu_custom_call" | custom-call | tf_op jit(solution)/shard_map/pallas_call | solution.py:207
  (20 shorter events, 1.5 us)
Async XLA Ops:
  0.0 14.0 %collective-permute-start.4 = (bf16[128,128,128]{2,1,0:T(8,128)(2,1)}, bf16[128,128,128]{2,1,0:T(8,128)(2,1)S(1)}, u32[]{:S(2)}, u32[]{:S(2)}) collective-permute-start(bf16[128,128,128]{2,1,0:T(8,128)(2,1)} %refs_6_.1), channel_id=1, source_target_pairs={{0,1},{1,0},{2,3},{3,2},{4,5},{5,4},{6,7},{7,6},{8,9},{9,8},{10,11... | collective-permute-start | bytes 12582920 | tf_op jit(solution)/shard_map/ppermute | solution.py:162
  0.5 5.9 %collective-permute-start = (bf16[8,32,128]{2,1,0:T(8,128)(2,1)}, bf16[8,32,128]{2,1,0:T(8,128)(2,1)S(1)}, u32[]{:S(2)}, u32[]{:S(2)}) collective-permute-start(bf16[8,32,128]{2,1,0:T(8,128)(2,1)} %refs_2_.1), channel_id=1, source_target_pairs={{0,4},{2,6},{4,0},{6,2},{8,12},{10,14},{12,8},{14,10},{1,5},{3,7},... | collective-permute-start | bytes 196616 | tf_op jit(solution)/shard_map/ppermute | solution.py:145
  3.0 7.2 %collective-permute-start.2 = (bf16[8,32,128]{2,1,0:T(8,128)(2,1)}, bf16[8,32,128]{2,1,0:T(8,128)(2,1)S(1)}, u32[]{:S(2)}, u32[]{:S(2)}) collective-permute-start(bf16[8,32,128]{2,1,0:T(8,128)(2,1)} %refs_2_.1), channel_id=1, source_target_pairs={{0,8},{2,10},{4,12},{6,14},{8,0},{10,2},{12,4},{14,6},{1,9},{3,11}... | collective-permute-start | bytes 196616 | tf_op jit(solution)/shard_map/ppermute | solution.py:145
  5.6 6.3 %collective-permute-start.3 = (bf16[8,32,128]{2,1,0:T(8,128)(2,1)}, bf16[8,32,128]{2,1,0:T(8,128)(2,1)S(1)}, u32[]{:S(2)}, u32[]{:S(2)}) collective-permute-start(bf16[8,32,128]{2,1,0:T(8,128)(2,1)} %refs_2_.1), channel_id=1, source_target_pairs={{0,12},{2,14},{4,8},{6,10},{8,4},{10,6},{12,0},{14,2},{1,13},{3,15... | collective-permute-start | bytes 196616 | tf_op jit(solution)/shard_map/ppermute | solution.py:145
  6.4 7.1 %collective-permute-start.1 = (s32[40,128]{1,0:T(8,128)S(1)}, s32[40,128]{1,0:T(8,128)S(1)}, u32[]{:S(2)}, u32[]{:S(2)}) collective-permute-start(s32[40,128]{1,0:T(8,128)S(1)} %shard_map.64.refs_0_), channel_id=1, source_target_pairs={{0,1},{1,0},{2,3},{3,2},{4,5},{5,4},{6,7},{7,6},{8,9},{9,8},{10,11... | collective-permute-start | bytes 61448 | tf_op jit(solution)/shard_map/ppermute | solution.py:168
  6.5 11.5 %collective-permute-start.5 = (bf16[8,32,128]{2,1,0:T(8,128)(2,1)}, bf16[8,32,128]{2,1,0:T(8,128)(2,1)S(1)}, u32[]{:S(2)}, u32[]{:S(2)}) collective-permute-start(bf16[8,32,128]{2,1,0:T(8,128)(2,1)} %refs_2_.1), channel_id=1, source_target_pairs={{0,2},{2,0},{4,6},{6,4},{8,10},{10,8},{12,14},{14,12},{1,3},{3,1},... | collective-permute-start | bytes 196616 | tf_op jit(solution)/shard_map/ppermute | solution.py:145
  10.2 7.8 %collective-permute-start.6 = (bf16[8,32,128]{2,1,0:T(8,128)(2,1)S(1)}, bf16[8,32,128]{2,1,0:T(8,128)(2,1)S(1)}, u32[]{:S(2)}, u32[]{:S(2)}) collective-permute-start(bf16[8,32,128]{2,1,0:T(8,128)(2,1)S(1)} %collective-permute-done.refs_3_), channel_id=1, source_target_pairs={{0,2},{2,0},{4,6},{6,4},{8,10},{10,8},{12,14},{14,12},{1,3},{3,1},... | collective-permute-start | bytes 196616 | tf_op jit(solution)/shard_map/ppermute | solution.py:145
  11.9 6.0 %collective-permute-start.7 = (bf16[8,32,128]{2,1,0:T(8,128)(2,1)S(1)}, bf16[8,32,128]{2,1,0:T(8,128)(2,1)S(1)}, u32[]{:S(2)}, u32[]{:S(2)}) collective-permute-start(bf16[8,32,128]{2,1,0:T(8,128)(2,1)S(1)} %collective-permute-done.2.refs_4_), channel_id=1, source_target_pairs={{0,2},{2,0},{4,6},{6,4},{8,10},{10,8},{12,14},{14,12},{1,3},{3,1},... | collective-permute-start | bytes 196616 | tf_op jit(solution)/shard_map/ppermute | solution.py:145
  13.5 4.5 %collective-permute-start.8 = (bf16[8,32,128]{2,1,0:T(8,128)(2,1)S(1)}, bf16[8,32,128]{2,1,0:T(8,128)(2,1)S(1)}, u32[]{:S(2)}, u32[]{:S(2)}) collective-permute-start(bf16[8,32,128]{2,1,0:T(8,128)(2,1)S(1)} %collective-permute-done.3.refs_5_), channel_id=1, source_target_pairs={{0,2},{2,0},{4,6},{6,4},{8,10},{10,8},{12,14},{14,12},{1,3},{3,1},... | collective-permute-start | bytes 196616 | tf_op jit(solution)/shard_map/ppermute | solution.py:145
  21.5 9.6 %collective-permute-start.9 = (f32[2,24]{1,0:T(2,128)S(1)}, f32[2,24]{1,0:T(2,128)S(1)}, u32[]{:S(2)}, u32[]{:S(2)}) collective-permute-start(f32[2,24]{1,0:T(2,128)S(1)} %get-tuple-element.30), channel_id=1, source_target_pairs={{0,2},{4,6},{8,10},{12,14},{1,3},{5,7},{9,11},{13,15},{16,18},{20,... | collective-permute-start | bytes 584 | tf_op jit(solution)/shard_map/ppermute | solution.py:145
  23.6 8.0 %collective-permute-start.12 = (f32[2,24]{1,0:T(2,128)S(1)}, f32[2,24]{1,0:T(2,128)S(1)}, u32[]{:S(2)}, u32[]{:S(2)}) collective-permute-start(f32[2,24]{1,0:T(2,128)S(1)} %get-tuple-element.32), channel_id=1, source_target_pairs={{0,6},{4,2},{8,14},{12,10},{1,7},{5,3},{9,15},{13,11},{16,22},{20,... | collective-permute-start | bytes 584 | tf_op jit(solution)/shard_map/ppermute | solution.py:145
  25.4 9.5 %collective-permute-start.15 = (f32[2,24]{1,0:T(2,128)S(1)}, f32[2,24]{1,0:T(2,128)S(1)}, u32[]{:S(2)}, u32[]{:S(2)}) collective-permute-start(f32[2,24]{1,0:T(2,128)S(1)} %get-tuple-element.34), channel_id=1, source_target_pairs={{0,10},{4,14},{8,2},{12,6},{1,11},{5,15},{9,3},{13,7},{16,26},{20,... | collective-permute-start | bytes 584 | tf_op jit(solution)/shard_map/ppermute | solution.py:145
  27.9 8.3 %collective-permute-start.18 = (f32[2,24]{1,0:T(2,128)S(1)}, f32[2,24]{1,0:T(2,128)S(1)}, u32[]{:S(2)}, u32[]{:S(2)}) collective-permute-start(f32[2,24]{1,0:T(2,128)S(1)} %get-tuple-element.36), channel_id=1, source_target_pairs={{0,14},{4,10},{8,6},{12,2},{1,15},{5,11},{9,7},{13,3},{16,30},{20,... | collective-permute-start | bytes 584 | tf_op jit(solution)/shard_map/ppermute | solution.py:145
  30.4 7.1 %collective-permute-start.11 = (f32[2,24]{1,0:T(2,128)S(1)}, f32[2,24]{1,0:T(2,128)S(1)}, u32[]{:S(2)}, u32[]{:S(2)}) collective-permute-start(f32[2,24]{1,0:T(2,128)S(1)} %get-tuple-element.31), channel_id=1, source_target_pairs={{0,4},{2,6},{4,0},{6,2},{8,12},{10,14},{12,8},{14,10},{1,5},{3,7},... | collective-permute-start | bytes 584 | tf_op jit(solution)/shard_map/ppermute | solution.py:145
  31.1 7.7 %collective-permute-start.14 = (f32[2,24]{1,0:T(2,128)S(1)}, f32[2,24]{1,0:T(2,128)S(1)}, u32[]{:S(2)}, u32[]{:S(2)}) collective-permute-start(f32[2,24]{1,0:T(2,128)S(1)} %get-tuple-element.33), channel_id=1, source_target_pairs={{0,8},{2,10},{4,12},{6,14},{8,0},{10,2},{12,4},{14,6},{1,9},{3,11}... | collective-permute-start | bytes 584 | tf_op jit(solution)/shard_map/ppermute | solution.py:145
  31.6 8.5 %collective-permute-start.17 = (f32[2,24]{1,0:T(2,128)S(1)}, f32[2,24]{1,0:T(2,128)S(1)}, u32[]{:S(2)}, u32[]{:S(2)}) collective-permute-start(f32[2,24]{1,0:T(2,128)S(1)} %get-tuple-element.35), channel_id=1, source_target_pairs={{0,12},{2,14},{4,8},{6,10},{8,4},{10,6},{12,0},{14,2},{1,13},{3,15... | collective-permute-start | bytes 584 | tf_op jit(solution)/shard_map/ppermute | solution.py:145
  34.9 5.5 %collective-permute-start.10 = (f32[2,24]{1,0:T(2,128)S(1)}, f32[2,24]{1,0:T(2,128)S(1)}, u32[]{:S(2)}, u32[]{:S(2)}) collective-permute-start(f32[2,24]{1,0:T(2,128)S(1)} %get-tuple-element.30), channel_id=1, source_target_pairs={{2,0},{6,4},{10,8},{14,12},{3,1},{7,5},{11,9},{15,13},{18,16},{22,... | collective-permute-start | bytes 584 | tf_op jit(solution)/shard_map/ppermute | solution.py:145
  36.2 6.4 %collective-permute-start.13 = (f32[2,24]{1,0:T(2,128)S(1)}, f32[2,24]{1,0:T(2,128)S(1)}, u32[]{:S(2)}, u32[]{:S(2)}) collective-permute-start(f32[2,24]{1,0:T(2,128)S(1)} %get-tuple-element.32), channel_id=1, source_target_pairs={{2,4},{6,0},{10,12},{14,8},{3,5},{7,1},{11,13},{15,9},{18,20},{22,... | collective-permute-start | bytes 584 | tf_op jit(solution)/shard_map/ppermute | solution.py:145
  37.5 7.3 %collective-permute-start.16 = (f32[2,24]{1,0:T(2,128)S(1)}, f32[2,24]{1,0:T(2,128)S(1)}, u32[]{:S(2)}, u32[]{:S(2)}) collective-permute-start(f32[2,24]{1,0:T(2,128)S(1)} %get-tuple-element.34), channel_id=1, source_target_pairs={{2,8},{6,12},{10,0},{14,4},{3,9},{7,13},{11,1},{15,5},{18,24},{22,... | collective-permute-start | bytes 584 | tf_op jit(solution)/shard_map/ppermute | solution.py:145
  38.8 8.2 %collective-permute-start.19 = (f32[2,24]{1,0:T(2,128)S(1)}, f32[2,24]{1,0:T(2,128)S(1)}, u32[]{:S(2)}, u32[]{:S(2)}) collective-permute-start(f32[2,24]{1,0:T(2,128)S(1)} %get-tuple-element.36), channel_id=1, source_target_pairs={{2,12},{6,8},{10,4},{14,0},{3,13},{7,9},{11,5},{15,1},{18,28},{22,... | collective-permute-start | bytes 584 | tf_op jit(solution)/shard_map/ppermute | solution.py:145

commit v5 on v4

v5 whole, which is shorter than its diff:
```python
import functools

import jax
import jax.numpy as jnp
from jax import lax
from jax.experimental import pallas as pl
from jax.experimental.pallas import tpu as pltpu
from jax.sharding import PartitionSpec as P

GROUPS = 8
CHUNKS = 8
SHIFT = 8
QUERY, PASSAGE, LENGTH, COUNT = 0, 32, 64, 96


def pack_kernel(shards, query_hbm, passage_hbm, count_hbm, length_hbm, own_hbm, mine_ref, theirs_ref, own_ref, query_ref, passage_ref, count_ref, length_ref, sems, own_sems):
    copies = [
        pltpu.make_async_copy(src, dst, sems.at[i])
        for i, (src, dst) in enumerate(
            ((query_hbm, query_ref), (passage_hbm, passage_ref), (count_hbm, count_ref), (length_hbm, length_ref))
        )
    ]
    size = own_ref.shape[0] // CHUNKS
    own_copies = [
        pltpu.make_async_copy(own_hbm.at[pl.ds(i * size, size)], own_ref.at[pl.ds(i * size, size)], own_sems.at[i])
        for i in range(CHUNKS)
    ]
    for copy in copies + own_copies:
        copy.start()
    for copy in copies:
        copy.wait()
    cap = query_ref.shape[1]
    lengths = length_ref[...].reshape(1, -1)
    counts = jnp.broadcast_to(count_ref[...].reshape(1, -1), (2 * shards, 2 * shards))
    row = lax.broadcasted_iota(jnp.int32, counts.shape, 0)
    col = lax.broadcasted_iota(jnp.int32, counts.shape, 1)
    counts = jnp.sum(jnp.where(row == col, counts, 0), axis=1, keepdims=True)
    blank = jnp.zeros((2 * shards, 32 - cap), jnp.int32)
    passage = jnp.concatenate([passage_ref[...], blank], axis=1)
    passage = jnp.concatenate([passage] * 4, axis=1)
    length = jnp.take_along_axis(jnp.broadcast_to(lengths, passage.shape), passage, axis=1)
    query = jnp.concatenate([jnp.concatenate([query_ref[...], blank], axis=1)] * 4, axis=1)
    lane = lax.broadcasted_iota(jnp.int32, passage.shape, 1)
    packed = jnp.where(lane < PASSAGE, query, jnp.where(lane < LENGTH, passage, jnp.where(lane < COUNT, length, counts)))
    packed = packed.reshape(shards, 2, 128)
    first = lax.axis_index("sub") == 0
    mine_ref[...] = jnp.where(first, packed[:, 0], packed[:, 1])
    theirs_ref[...] = jnp.where(first, packed[:, 1], packed[:, 0])
    for copy in own_copies:
        copy.wait()


def score_kernel(shards, distances, pack, cap, *refs):
    n = len(distances)
    meta_hbm, pieces, passage_refs, refs = refs[:2], refs[2 : 2 + n], refs[2 + n : 4 + n], refs[-7:]
    out_ref, query_ref, best_ref, meta_ref, work_ref, meta_sems, piece_sems = refs
    q_tok, width = query_ref.shape[2:]
    tok_slots = passage_refs[0].shape[1]
    per_source = best_ref.shape[0]
    lanes = pack * q_tok
    q_bits = q_tok.bit_length() - 1
    me, core = lax.axis_index("shard"), lax.axis_index("sub")
    copies = [pltpu.make_async_copy(meta_hbm[i], meta_ref.at[i], meta_sems.at[i]) for i in range(2)]
    copies += [pltpu.make_async_copy(piece, query_ref.at[i], piece_sems.at[i]) for i, piece in enumerate(reversed(pieces))]
    for copy in copies:
        copy.start()
    best_ref[...] = jnp.zeros_like(best_ref)
    token = lax.broadcasted_iota(jnp.int32, (tok_slots, lanes), 0)
    place = lax.shift_right_logical(lax.broadcasted_iota(jnp.int32, (1, lanes), 1), q_bits)
    blank = jnp.zeros((q_tok, width), query_ref.dtype)
    for copy in copies:
        copy.wait()

    for which, passages in ((0, passage_refs[0]), (1, passage_refs[1])):
        owner = core if which == 0 else 1 - core

        def shard_of(i):
            return jnp.bitwise_xor(me, i * 2 + distances[0])

        def list_source(i, total):
            live = meta_ref[which, shard_of(i), COUNT]
            for g in range(per_source):
                work_ref[total + g] = (i << SHIFT) + g
            return total + lax.shift_right_logical(live + pack - 1, pack.bit_length() - 1)

        total = lax.fori_loop(0, n, list_source, 0)
        for g in range(GROUPS):
            work_ref[total + g] = 0

        def one_step(step, carry):
            for j in range(GROUPS):
                work = work_ref[step * GROUPS + j]
                i, g = lax.shift_right_logical(work, SHIFT), jnp.bitwise_and(work, (1 << SHIFT) - 1)
                shard = shard_of(i)
                rows, cols, limit = [], [], jnp.zeros((1, lanes), jnp.int32)
                for a in range(pack):
                    slot = g * pack + a
                    query, passage = meta_ref[which, shard, QUERY + slot], meta_ref[which, shard, PASSAGE + slot]
                    rows.append(jnp.concatenate([blank] * a + [query_ref[i, query]] + [blank] * (pack - 1 - a), axis=1))
                    cols.append(passages[passage])
                    limit = jnp.where(place == a, meta_ref[which, shard, LENGTH + slot], limit)
                sims = lax.dot_general(
                    jnp.concatenate(cols, axis=1), jnp.concatenate(rows, axis=0),
                    (((1,), (1,)), ((), ())), preferred_element_type=jnp.float32,
                )
                best = jnp.max(jnp.where(token < limit, sims, -1e30), axis=0, keepdims=True)
                best = jnp.where(place + g * pack < meta_ref[which, shard, COUNT], best, 0.0)
                best_ref[g, pl.ds(i * 2 + owner, 1), :] = best
            return carry

        lax.fori_loop(0, lax.shift_right_logical(total + GROUPS - 1, GROUPS.bit_length() - 1), one_step, 0)

    best = jnp.concatenate([best_ref[g] for g in range(per_source)], axis=1)
    high = best.astype(jnp.bfloat16)
    rest = best - high.astype(jnp.float32)
    middle = rest.astype(jnp.bfloat16)
    low = (rest - middle.astype(jnp.float32)).astype(jnp.bfloat16)
    row = lax.broadcasted_iota(jnp.int32, (per_source * lanes, 128), 0)
    col = lax.broadcasted_iota(jnp.int32, (per_source * lanes, 128), 1)
    add = jnp.where(lax.shift_right_logical(row, q_bits) == col, 1.0, 0.0).astype(jnp.bfloat16)
    parts = jnp.dot(jnp.concatenate([high, middle, low], axis=0), add, preferred_element_type=jnp.float32)
    rows = best.shape[0]
    score = (parts[:rows] + parts[rows : 2 * rows] + parts[2 * rows :]) * (1.0 / q_tok)
    out_ref[...] = score[:, :cap]


def merge_kernel(here_ref, there_ref, *outs):
    for i, out in enumerate(outs):
        out[:2] = here_ref[2 * i : 2 * i + 2]
        out[2:] = there_ref[2 * i : 2 * i + 2]


def order_kernel(*refs):
    refs, out_ref = refs[:-1], refs[-1]
    me = lax.axis_index("shard")
    for i, piece in enumerate(refs):
        shard = jnp.bitwise_xor(me, 2 * i)
        out_ref[0, pl.ds(shard * 2, 2), :] = piece[:2]
        out_ref[0, pl.ds(jnp.bitwise_xor(shard, 1) * 2, 2), :] = piece[2:]


def on_device(shards, queries, passages, passage_len, slot_query, slot_passage, slot_count):
    sources, _, cap = slot_query.shape
    q_dev, q_tok, width = queries.shape
    pack = 128 // q_tok
    per_source = -(-cap // pack)
    swap = [(0, 1), (1, 0)]
    vmem, hbm, anywhere = (pl.BlockSpec(memory_space=space) for space in (pltpu.VMEM, pltpu.HBM, pl.ANY))
    params = pltpu.CompilerParams(vmem_limit_bytes=12 * 1024 * 1024)
    row = jax.ShapeDtypeStruct((shards, 128), jnp.int32)

    def placed(space, *arrays):
        return [pltpu.with_memory_space_constraint(x, space) for x in arrays]

    def swapped(piece, d):
        return lax.ppermute(piece, "shard", [(i, i ^ d) for i in range(shards)])

    pieces = [queries] + [None] * (shards - 1)
    for d in reversed(range(2, shards, 2)):
        pieces[d] = swapped(queries, d)
    other_passages = lax.ppermute(passages, "sub", swap)

    mine, theirs, own_passages = pl.pallas_call(
        functools.partial(pack_kernel, shards),
        out_shape=[row, row, jax.ShapeDtypeStruct(passages.shape, passages.dtype)],
        in_specs=[hbm] * 5,
        out_specs=[vmem] * 3,
        scratch_shapes=[
            pltpu.VMEM((sources, cap), jnp.int32),
            pltpu.VMEM((sources, cap), jnp.int32),
            pltpu.VMEM((sources,), jnp.int32),
            pltpu.VMEM(passage_len.shape, jnp.int32),
            pltpu.SemaphoreType.DMA((4,)),
            pltpu.SemaphoreType.DMA((CHUNKS,)),
        ],
        compiler_params=params,
    )(*placed(pltpu.HBM, slot_query.reshape(sources, cap), slot_passage.reshape(sources, cap), slot_count.reshape(sources), passage_len, passages))
    theirs, pieces[-2] = lax.optimization_barrier((theirs, pieces[-2]))
    other = lax.ppermute(theirs, "sub", swap)
    for d in range(1, shards, 2):
        pieces[d] = swapped(pieces[d - 1], 1)

    def scored(distances, after):
        n = len(distances)
        return pl.pallas_call(
            functools.partial(score_kernel, shards, distances, pack, cap),
            out_shape=jax.ShapeDtypeStruct((2 * n, cap), jnp.float32),
            in_specs=[anywhere] * (2 + n) + [vmem] * 2 + [anywhere] * len(after),
            out_specs=vmem,
            scratch_shapes=[
                pltpu.VMEM((n, *queries.shape), queries.dtype),
                pltpu.VMEM((per_source, 2 * n, 128), jnp.float32),
                pltpu.SMEM((2, shards, 128), jnp.int32),
                pltpu.SMEM((n * per_source + 2 * GROUPS,), jnp.int32),
                pltpu.SemaphoreType.DMA((2,)),
                pltpu.SemaphoreType.DMA((n,)),
            ],
            compiler_params=params,
            cost_estimate=pl.CostEstimate(flops=1_000_000_000, bytes_accessed=9_000_000, transcendentals=0),
        )(mine, other, *(pieces[d] for d in reversed(distances)), *placed(pltpu.VMEM, own_passages, other_passages), *after)

    pieces[0] = placed(pltpu.HBM, queries)[0]
    even, odd = range(0, shards, 2), range(1, shards, 2)
    here = scored(even, ())
    there = swapped(scored(odd, (here,)), 1)
    merged = pl.pallas_call(
        merge_kernel,
        out_shape=[jax.ShapeDtypeStruct((4, cap), jnp.float32)] * len(even),
        in_specs=[vmem] * 2,
        out_specs=[vmem] * len(even),
        compiler_params=params,
    )(here, there)
    return pl.pallas_call(
        order_kernel,
        out_shape=jax.ShapeDtypeStruct((1, sources, cap), jnp.float32),
        in_specs=[vmem] * len(even),
        out_specs=vmem,
        compiler_params=params,
    )(*(swapped(piece, d) if d else piece for d, piece in zip(even, merged)))


def solution(mesh):
    return jax.shard_map(
        functools.partial(on_device, mesh.shape["shard"]),
        mesh=mesh,
        in_specs=(
            P(("groups", "shard", "sub"), None, None),
            P(("shard", "sub"), None, None),
            P(("shard", "sub")),
            P("groups", ("shard", "sub"), None),
            P("groups", ("shard", "sub"), None),
            P("groups", ("shard", "sub")),
        ),
        out_specs=P(("groups", "shard", "sub"), None, None),
        check_vma=False,
    )
```

time: 47.9 us -> 34.1 us (0.71)
  starting transfers between devices: 29.6 us -> 16 us
    ppermute x19 -> x12, starting transfers between devices: 29.1 us -> 15.5 us  [the longest x11 15.5 us: swapped(): return lax.ppermute(piece, 'shard', [(i, i ^ d) for i in range(shards)])]
    pallas_call x2, Pallas kernels: 7.45 us -> 5.67 us  [scored(): pl.pallas_call(functools.partial(score_kernel, shards, distances, pack, c...]
    pallas_call x2 -> x3, Pallas kernels: 1.36 us -> 2.9 us  [the longest x1 2.29 us: on_device(): pl.pallas_call(functools.partial(pack_kernel, shards), out_shape=[row, ro...]
    ppermute x19 -> x12, waiting for transfers between devices: 9.03 us -> 9.36 us  [the longest x11 9.36 us: swapped(): return lax.ppermute(piece, 'shard', [(i, i ^ d) for i in range(shards)])]
  transfers between devices with their start and end apart: 20 -> 13, of which waited for: 6 -> 6; matrix products, arithmetic and copies ran while one was open for 0% -> 0% of each run, Pallas kernels for 10% -> 15%
where the time goes in v5:
time: 34.1 us; the launch traced here: 34 us
  starting transfers between devices  16 us (47%)
  waiting for transfers between devices  9.37 us (27%)
  Pallas kernels  8.57 us (25%)
    ppermute x11, starting transfers between devices, swapped(): return lax.ppermute(piece, 'shard', [(i, i ^ d) for i in range(shards)])  15.5 us
    ppermute x11, waiting for transfers between devices, swapped(): return lax.ppermute(piece, 'shard', [(i, i ^ d) for i in range(shards)])  9.36 us
    pallas_call x2, Pallas kernels, scored(): pl.pallas_call(functools.partial(score_kernel, shards, distances, pack, c...  5.67 us
    pallas_call x1, Pallas kernels, on_device(): pl.pallas_call(functools.partial(pack_kernel, shards), out_shape=[row, ro...  2.29 us
  transfers between devices with their start and end apart: 13, of which 6 were waited for; matrix products, arithmetic and copies ran while one was open for 0% of the time, Pallas kernels for 15%

profile of v5, /device:TPU:0, one launch (start us, length us, event | category | flops | bytes accessed | tf_op | source)
XLA Modules:
  0.0 34.0 jit_solution(10363222054728889672)
XLA Ops:
  0.0 0.5 %collective-permute-start.4 = (bf16[128,128,128]{2,1,0:T(8,128)(2,1)}, bf16[128,128,128]{2,1,0:T(8,128)(2,1)S(1)}, u32[]{:S(2)}, u32[]{:S(2)}) collective-permute-start(bf16[128,128,128]{2,1,0:T(8,128)(2,1)} %own_hbm.1), channel_id=1, source_target_pairs={{0,1},{1,0},{2,3},{3,2},{4,5},{5,4},{6,7},{7,6},{8,9},{9,8},{10,11... | collective-permute-start | bytes 12582920 | tf_op jit(solution)/shard_map/ppermute | solution.py:161
  0.5 4.7 %collective-permute-start = (bf16[8,32,128]{2,1,0:T(8,128)(2,1)}, bf16[8,32,128]{2,1,0:T(8,128)(2,1)S(1)}, u32[]{:S(2)}, u32[]{:S(2)}) collective-permute-start(bf16[8,32,128]{2,1,0:T(8,128)(2,1)} %refs_5_.1), channel_id=1, source_target_pairs={{0,12},{2,14},{4,8},{6,10},{8,4},{10,6},{12,0},{14,2},{1,13},{3,15... | collective-permute-start | bytes 196616 | tf_op jit(solution)/shard_map/ppermute | solution.py:156
  5.1 0.0 collective-permute-start.2
  5.1 0.7 %collective-permute-start.3 = (bf16[8,32,128]{2,1,0:T(8,128)(2,1)}, bf16[8,32,128]{2,1,0:T(8,128)(2,1)S(1)}, u32[]{:S(2)}, u32[]{:S(2)}) collective-permute-start(bf16[8,32,128]{2,1,0:T(8,128)(2,1)} %refs_5_.1), channel_id=1, source_target_pairs={{0,4},{2,6},{4,0},{6,2},{8,12},{10,14},{12,8},{14,10},{1,5},{3,7},... | collective-permute-start | bytes 196616 | tf_op jit(solution)/shard_map/ppermute | solution.py:156
  5.8 2.3 %shard_map.64 = (s32[8,128]{1,0:T(8,128)S(1)}, s32[8,128]{1,0:T(8,128)S(1)}, bf16[128,128,128]{2,1,0:T(8,128)(2,1)S(1)}) custom-call(s32[16,24]{1,0:T(8,128)} %bitcast.3, s32[16,24]{1,0:T(8,128)} %bitcast.4, s32[16]{0:T(128)} %bitcast.5, s32[128]{0:T(128)} %length_hbm.1, bf16[128,128,128]{2,1,0:T(8,128)(2,1)} %own_hbm.1), custom_call_target="tpu_custom_call" | custom-call | tf_op jit(solution)/shard_map/pallas_call | solution.py:163
  8.1 0.1 collective-permute-done.refs_2_
  8.2 1.7 %collective-permute-start.8 = (bf16[8,32,128]{2,1,0:T(8,128)(2,1)S(1)}, bf16[8,32,128]{2,1,0:T(8,128)(2,1)S(1)}, u32[]{:S(2)}, u32[]{:S(2)}) collective-permute-start(bf16[8,32,128]{2,1,0:T(8,128)(2,1)S(1)} %copy-done), channel_id=1, source_target_pairs={{0,2},{2,0},{4,6},{6,4},{8,10},{10,8},{12,14},{14,12},{1,3},{3,1},... | collective-permute-start | bytes 196616 | tf_op jit(solution)/shard_map/ppermute | solution.py:156
  9.9 1.5 %collective-permute-done.2.refs_3_ = bf16[8,32,128]{2,1,0:T(8,128)(2,1)S(1)} collective-permute-done((bf16[8,32,128]{2,1,0:T(8,128)(2,1)}, bf16[8,32,128]{2,1,0:T(8,128)(2,1)S(1)}, u32[]{:S(2)}, u32[]{:S(2)}) %collective-permute-start.2) | collective-permute-done | bytes 65568 | tf_op jit(solution)/shard_map/ppermute | solution.py:156
  11.4 1.5 %collective-permute-start.5 = (bf16[8,32,128]{2,1,0:T(8,128)(2,1)S(1)}, bf16[8,32,128]{2,1,0:T(8,128)(2,1)S(1)}, u32[]{:S(2)}, u32[]{:S(2)}) collective-permute-start(bf16[8,32,128]{2,1,0:T(8,128)(2,1)S(1)} %collective-permute-done.refs_2_), channel_id=1, source_target_pairs={{0,2},{2,0},{4,6},{6,4},{8,10},{10,8},{12,14},{14,12},{1,3},{3,1},... | collective-permute-start | bytes 196616 | tf_op jit(solution)/shard_map/ppermute | solution.py:156
  12.9 0.5 %collective-permute-start.6 = (bf16[8,32,128]{2,1,0:T(8,128)(2,1)S(1)}, bf16[8,32,128]{2,1,0:T(8,128)(2,1)S(1)}, u32[]{:S(2)}, u32[]{:S(2)}) collective-permute-start(bf16[8,32,128]{2,1,0:T(8,128)(2,1)S(1)} %collective-permute-done.2.refs_3_), channel_id=1, source_target_pairs={{0,2},{2,0},{4,6},{6,4},{8,10},{10,8},{12,14},{14,12},{1,3},{3,1},... | collective-permute-start | bytes 196616 | tf_op jit(solution)/shard_map/ppermute | solution.py:156
  13.4 0.0 collective-permute-done.1.refs_1_
  13.4 1.5 %collective-permute-start.7 = (bf16[8,32,128]{2,1,0:T(8,128)(2,1)S(1)}, bf16[8,32,128]{2,1,0:T(8,128)(2,1)S(1)}, u32[]{:S(2)}, u32[]{:S(2)}) collective-permute-start(bf16[8,32,128]{2,1,0:T(8,128)(2,1)S(1)} %collective-permute-done.3.refs_4_), channel_id=1, source_target_pairs={{0,2},{2,0},{4,6},{6,4},{8,10},{10,8},{12,14},{14,12},{1,3},{3,1},... | collective-permute-start | bytes 196616 | tf_op jit(solution)/shard_map/ppermute | solution.py:156
  14.9 0.0 collective-permute-done.4.refs_7_
  15.0 2.9 %shard_map.65.refs_8_.here_ref = f32[8,24]{1,0:T(8,128)S(1)} custom-call(s32[8,128]{1,0:T(8,128)S(1)} %get-tuple-element.14.refs_0_, s32[8,128]{1,0:T(8,128)S(1)} %collective-permute-done.1.refs_1_, bf16[8,32,128]{2,1,0:T(8,128)(2,1)S(1)} %collective-permute-done.refs_2_, bf16[8,32,128]{2,1,0:T(8,128)(2,1)S(1)} %collective-permute-done.2.refs_3_, ...), custom_call_target="tpu_custom_call" | custom-call | flops 1000000000 | bytes 9000000 | tf_op jit(solution)/shard_map/pallas_call | solution.py:185
  17.9 0.5 %collective-permute-done.7.refs_4_ = bf16[8,32,128]{2,1,0:T(8,128)(2,1)S(1)} collective-permute-done((bf16[8,32,128]{2,1,0:T(8,128)(2,1)S(1)}, bf16[8,32,128]{2,1,0:T(8,128)(2,1)S(1)}, u32[]{:S(2)}, u32[]{:S(2)}) %collective-permute-start.7) | collective-permute-done | bytes 65568 | tf_op jit(solution)/shard_map/ppermute | solution.py:156
  18.4 2.8 %shard_map.66 = f32[8,24]{1,0:T(8,128)S(1)} custom-call(s32[8,128]{1,0:T(8,128)S(1)} %get-tuple-element.14.refs_0_, s32[8,128]{1,0:T(8,128)S(1)} %collective-permute-done.1.refs_1_, bf16[8,32,128]{2,1,0:T(8,128)(2,1)S(1)} %collective-permute-done.5.refs_2_, bf16[8,32,128]{2,1,0:T(8,128)(2,1)S(1)} %collective-permute-done.6.refs_3_, ...), custom_call_target="tpu_custom_call" | custom-call | flops 1000000000 | bytes 9000000 | tf_op jit(solution)/shard_map/pallas_call | solution.py:185
  21.2 0.6 %collective-permute-start.9 = (f32[8,24]{1,0:T(8,128)S(1)}, f32[8,24]{1,0:T(8,128)S(1)}, u32[]{:S(2)}, u32[]{:S(2)}) collective-permute-start(f32[8,24]{1,0:T(8,128)S(1)} %shard_map.66), channel_id=1, source_target_pairs={{0,2},{2,0},{4,6},{6,4},{8,10},{10,8},{12,14},{14,12},{1,3},{3,1},... | collective-permute-start | bytes 2312 | tf_op jit(solution)/shard_map/ppermute | solution.py:156
  21.8 3.1 %collective-permute-done.9.there_ref = f32[8,24]{1,0:T(8,128)S(1)} collective-permute-done((f32[8,24]{1,0:T(8,128)S(1)}, f32[8,24]{1,0:T(8,128)S(1)}, u32[]{:S(2)}, u32[]{:S(2)}) %collective-permute-start.9) | collective-permute-done | bytes 800 | tf_op jit(solution)/shard_map/ppermute | solution.py:156
  24.9 0.4 %collective-permute-start.10 = (f32[4,24]{1,0:T(4,128)S(1)}, f32[4,24]{1,0:T(4,128)S(1)}, u32[]{:S(2)}, u32[]{:S(2)}) collective-permute-start(f32[4,24]{1,0:T(4,128)S(1)} %get-tuple-element.20), channel_id=1, source_target_pairs={{0,4},{2,6},{4,0},{6,2},{8,12},{10,14},{12,8},{14,10},{1,5},{3,7},... | collective-permute-start | bytes 1160 | tf_op jit(solution)/shard_map/ppermute | solution.py:156
  25.3 2.7 %collective-permute-start.11 = (f32[4,24]{1,0:T(4,128)S(1)}, f32[4,24]{1,0:T(4,128)S(1)}, u32[]{:S(2)}, u32[]{:S(2)}) collective-permute-start(f32[4,24]{1,0:T(4,128)S(1)} %get-tuple-element.21), channel_id=1, source_target_pairs={{0,8},{2,10},{4,12},{6,14},{8,0},{10,2},{12,4},{14,6},{1,9},{3,11}... | collective-permute-start | bytes 1160 | tf_op jit(solution)/shard_map/ppermute | solution.py:156
  28.0 1.3 %collective-permute-start.12 = (f32[4,24]{1,0:T(4,128)S(1)}, f32[4,24]{1,0:T(4,128)S(1)}, u32[]{:S(2)}, u32[]{:S(2)}) collective-permute-start(f32[4,24]{1,0:T(4,128)S(1)} %get-tuple-element.22), channel_id=1, source_target_pairs={{0,12},{2,14},{4,8},{6,10},{8,4},{10,6},{12,0},{14,2},{1,13},{3,15... | collective-permute-start | bytes 1160 | tf_op jit(solution)/shard_map/ppermute | solution.py:156
  29.3 0.5 %collective-permute-done.11.refs_2_ = f32[4,24]{1,0:T(4,128)S(1)} collective-permute-done((f32[4,24]{1,0:T(4,128)S(1)}, f32[4,24]{1,0:T(4,128)S(1)}, u32[]{:S(2)}, u32[]{:S(2)}) %collective-permute-start.11) | collective-permute-done | bytes 416 | tf_op jit(solution)/shard_map/ppermute | solution.py:156
  29.8 3.6 %collective-permute-done.12.refs_3_ = f32[4,24]{1,0:T(4,128)S(1)} collective-permute-done((f32[4,24]{1,0:T(4,128)S(1)}, f32[4,24]{1,0:T(4,128)S(1)}, u32[]{:S(2)}, u32[]{:S(2)}) %collective-permute-start.12) | collective-permute-done | bytes 416 | tf_op jit(solution)/shard_map/ppermute | solution.py:156
  33.4 0.6 %shard_map.68 = f32[1,16,24]{2,1,0:T(8,128)} custom-call(f32[4,24]{1,0:T(4,128)S(1)} %get-tuple-element.19.refs_0_, f32[4,24]{1,0:T(4,128)S(1)} %collective-permute-done.10.refs_1_, f32[4,24]{1,0:T(4,128)S(1)} %collective-permute-done.11.refs_2_, f32[4,24]{1,0:T(4,128)S(1)} %collective-permute-done.12.refs_3_), custom_call_target="tpu_custom_call" | custom-call | tf_op jit(solution)/shard_map/pallas_call | solution.py:213
  (9 shorter events, 0.0 us)
Async XLA Ops:
  0.0 8.2 %copy-start = (bf16[8,32,128]{2,1,0:T(8,128)(2,1)S(1)}, bf16[8,32,128]{2,1,0:T(8,128)(2,1)}, u32[]{:S(2)}) copy-start(bf16[8,32,128]{2,1,0:T(8,128)(2,1)} %refs_5_.1) | copy-start | bytes 196612
  0.0 14.9 %collective-permute-start.4 = (bf16[128,128,128]{2,1,0:T(8,128)(2,1)}, bf16[128,128,128]{2,1,0:T(8,128)(2,1)S(1)}, u32[]{:S(2)}, u32[]{:S(2)}) collective-permute-start(bf16[128,128,128]{2,1,0:T(8,128)(2,1)} %own_hbm.1), channel_id=1, source_target_pairs={{0,1},{1,0},{2,3},{3,2},{4,5},{5,4},{6,7},{7,6},{8,9},{9,8},{10,11... | collective-permute-start | bytes 12582920 | tf_op jit(solution)/shard_map/ppermute | solution.py:161
  0.5 7.8 %collective-permute-start = (bf16[8,32,128]{2,1,0:T(8,128)(2,1)}, bf16[8,32,128]{2,1,0:T(8,128)(2,1)S(1)}, u32[]{:S(2)}, u32[]{:S(2)}) collective-permute-start(bf16[8,32,128]{2,1,0:T(8,128)(2,1)} %refs_5_.1), channel_id=1, source_target_pairs={{0,12},{2,14},{4,8},{6,10},{8,4},{10,6},{12,0},{14,2},{1,13},{3,15... | collective-permute-start | bytes 196616 | tf_op jit(solution)/shard_map/ppermute | solution.py:156
  5.1 6.3 %collective-permute-start.2 = (bf16[8,32,128]{2,1,0:T(8,128)(2,1)}, bf16[8,32,128]{2,1,0:T(8,128)(2,1)S(1)}, u32[]{:S(2)}, u32[]{:S(2)}) collective-permute-start(bf16[8,32,128]{2,1,0:T(8,128)(2,1)} %refs_5_.1), channel_id=1, source_target_pairs={{0,8},{2,10},{4,12},{6,14},{8,0},{10,2},{12,4},{14,6},{1,9},{3,11}... | collective-permute-start | bytes 196616 | tf_op jit(solution)/shard_map/ppermute | solution.py:156
  5.1 7.8 %collective-permute-start.3 = (bf16[8,32,128]{2,1,0:T(8,128)(2,1)}, bf16[8,32,128]{2,1,0:T(8,128)(2,1)S(1)}, u32[]{:S(2)}, u32[]{:S(2)}) collective-permute-start(bf16[8,32,128]{2,1,0:T(8,128)(2,1)} %refs_5_.1), channel_id=1, source_target_pairs={{0,4},{2,6},{4,0},{6,2},{8,12},{10,14},{12,8},{14,10},{1,5},{3,7},... | collective-permute-start | bytes 196616 | tf_op jit(solution)/shard_map/ppermute | solution.py:156
  8.2 5.2 %collective-permute-start.1 = (s32[8,128]{1,0:T(8,128)S(1)}, s32[8,128]{1,0:T(8,128)S(1)}, u32[]{:S(2)}, u32[]{:S(2)}) collective-permute-start(s32[8,128]{1,0:T(8,128)S(1)} %get-tuple-element.16), channel_id=1, source_target_pairs={{0,1},{1,0},{2,3},{3,2},{4,5},{5,4},{6,7},{7,6},{8,9},{9,8},{10,11... | collective-permute-start | bytes 12296 | tf_op jit(solution)/shard_map/ppermute | solution.py:179
  8.2 9.6 %collective-permute-start.8 = (bf16[8,32,128]{2,1,0:T(8,128)(2,1)S(1)}, bf16[8,32,128]{2,1,0:T(8,128)(2,1)S(1)}, u32[]{:S(2)}, u32[]{:S(2)}) collective-permute-start(bf16[8,32,128]{2,1,0:T(8,128)(2,1)S(1)} %copy-done), channel_id=1, source_target_pairs={{0,2},{2,0},{4,6},{6,4},{8,10},{10,8},{12,14},{14,12},{1,3},{3,1},... | collective-permute-start | bytes 196616 | tf_op jit(solution)/shard_map/ppermute | solution.py:156
  11.4 6.5 %collective-permute-start.5 = (bf16[8,32,128]{2,1,0:T(8,128)(2,1)S(1)}, bf16[8,32,128]{2,1,0:T(8,128)(2,1)S(1)}, u32[]{:S(2)}, u32[]{:S(2)}) collective-permute-start(bf16[8,32,128]{2,1,0:T(8,128)(2,1)S(1)} %collective-permute-done.refs_2_), channel_id=1, source_target_pairs={{0,2},{2,0},{4,6},{6,4},{8,10},{10,8},{12,14},{14,12},{1,3},{3,1},... | collective-permute-start | bytes 196616 | tf_op jit(solution)/shard_map/ppermute | solution.py:156
  12.9 5.0 %collective-permute-start.6 = (bf16[8,32,128]{2,1,0:T(8,128)(2,1)S(1)}, bf16[8,32,128]{2,1,0:T(8,128)(2,1)S(1)}, u32[]{:S(2)}, u32[]{:S(2)}) collective-permute-start(bf16[8,32,128]{2,1,0:T(8,128)(2,1)S(1)} %collective-permute-done.2.refs_3_), channel_id=1, source_target_pairs={{0,2},{2,0},{4,6},{6,4},{8,10},{10,8},{12,14},{14,12},{1,3},{3,1},... | collective-permute-start | bytes 196616 | tf_op jit(solution)/shard_map/ppermute | solution.py:156
  13.4 5.0 %collective-permute-start.7 = (bf16[8,32,128]{2,1,0:T(8,128)(2,1)S(1)}, bf16[8,32,128]{2,1,0:T(8,128)(2,1)S(1)}, u32[]{:S(2)}, u32[]{:S(2)}) collective-permute-start(bf16[8,32,128]{2,1,0:T(8,128)(2,1)S(1)} %collective-permute-done.3.refs_4_), channel_id=1, source_target_pairs={{0,2},{2,0},{4,6},{6,4},{8,10},{10,8},{12,14},{14,12},{1,3},{3,1},... | collective-permute-start | bytes 196616 | tf_op jit(solution)/shard_map/ppermute | solution.py:156
  21.2 3.7 %collective-permute-start.9 = (f32[8,24]{1,0:T(8,128)S(1)}, f32[8,24]{1,0:T(8,128)S(1)}, u32[]{:S(2)}, u32[]{:S(2)}) collective-permute-start(f32[8,24]{1,0:T(8,128)S(1)} %shard_map.66), channel_id=1, source_target_pairs={{0,2},{2,0},{4,6},{6,4},{8,10},{10,8},{12,14},{14,12},{1,3},{3,1},... | collective-permute-start | bytes 2312 | tf_op jit(solution)/shard_map/ppermute | solution.py:156
  24.9 4.4 %collective-permute-start.10 = (f32[4,24]{1,0:T(4,128)S(1)}, f32[4,24]{1,0:T(4,128)S(1)}, u32[]{:S(2)}, u32[]{:S(2)}) collective-permute-start(f32[4,24]{1,0:T(4,128)S(1)} %get-tuple-element.20), channel_id=1, source_target_pairs={{0,4},{2,6},{4,0},{6,2},{8,12},{10,14},{12,8},{14,10},{1,5},{3,7},... | collective-permute-start | bytes 1160 | tf_op jit(solution)/shard_map/ppermute | solution.py:156
  25.3 4.5 %collective-permute-start.11 = (f32[4,24]{1,0:T(4,128)S(1)}, f32[4,24]{1,0:T(4,128)S(1)}, u32[]{:S(2)}, u32[]{:S(2)}) collective-permute-start(f32[4,24]{1,0:T(4,128)S(1)} %get-tuple-element.21), channel_id=1, source_target_pairs={{0,8},{2,10},{4,12},{6,14},{8,0},{10,2},{12,4},{14,6},{1,9},{3,11}... | collective-permute-start | bytes 1160 | tf_op jit(solution)/shard_map/ppermute | solution.py:156
  28.0 5.4 %collective-permute-start.12 = (f32[4,24]{1,0:T(4,128)S(1)}, f32[4,24]{1,0:T(4,128)S(1)}, u32[]{:S(2)}, u32[]{:S(2)}) collective-permute-start(f32[4,24]{1,0:T(4,128)S(1)} %get-tuple-element.22), channel_id=1, source_target_pairs={{0,12},{2,14},{4,8},{6,10},{8,4},{10,6},{12,0},{14,2},{1,13},{3,15... | collective-permute-start | bytes 1160 | tf_op jit(solution)/shard_map/ppermute | solution.py:156

commit v6 on v5

--- a/solution.py
+++ b/solution.py
@@ -13,19 +13,14 @@
 QUERY, PASSAGE, LENGTH, COUNT = 0, 32, 64, 96
 
 
-def pack_kernel(shards, query_hbm, passage_hbm, count_hbm, length_hbm, own_hbm, mine_ref, theirs_ref, own_ref, query_ref, passage_ref, count_ref, length_ref, sems, own_sems):
+def pack_kernel(shards, query_hbm, passage_hbm, count_hbm, length_hbm, mine_ref, theirs_ref, query_ref, passage_ref, count_ref, length_ref, sems):
     copies = [
         pltpu.make_async_copy(src, dst, sems.at[i])
         for i, (src, dst) in enumerate(
             ((query_hbm, query_ref), (passage_hbm, passage_ref), (count_hbm, count_ref), (length_hbm, length_ref))
         )
     ]
-    size = own_ref.shape[0] // CHUNKS
-    own_copies = [
-        pltpu.make_async_copy(own_hbm.at[pl.ds(i * size, size)], own_ref.at[pl.ds(i * size, size)], own_sems.at[i])
-        for i in range(CHUNKS)
-    ]
-    for copy in copies + own_copies:
+    for copy in copies:
         copy.start()
     for copy in copies:
         copy.wait()
@@ -46,23 +41,30 @@
     first = lax.axis_index("sub") == 0
     mine_ref[...] = jnp.where(first, packed[:, 0], packed[:, 1])
     theirs_ref[...] = jnp.where(first, packed[:, 1], packed[:, 0])
-    for copy in own_copies:
-        copy.wait()
-
-
-def score_kernel(shards, distances, pack, cap, *refs):
+
+
+def score_kernel(shards, distances, pack, cap, first, *refs):
     n = len(distances)
-    meta_hbm, pieces, passage_refs, refs = refs[:2], refs[2 : 2 + n], refs[2 + n : 4 + n], refs[-7:]
-    out_ref, query_ref, best_ref, meta_ref, work_ref, meta_sems, piece_sems = refs
+    meta_hbm, pieces, (own_hbm, other_ref), refs = refs[:2], refs[2 : 2 + n], refs[2 + n : 4 + n], refs[4 + n :]
+    if first:
+        out_ref, own_ref = refs[:2]
+    else:
+        (earlier_ref, out_ref), own_ref = refs[:2], own_hbm
+    query_ref, best_ref, meta_ref, work_ref, meta_sems, piece_sems, own_sems = refs[2:]
     q_tok, width = query_ref.shape[2:]
-    tok_slots = passage_refs[0].shape[1]
+    pass_dev, tok_slots = other_ref.shape[:2]
     per_source = best_ref.shape[0]
     lanes = pack * q_tok
     q_bits = q_tok.bit_length() - 1
     me, core = lax.axis_index("shard"), lax.axis_index("sub")
     copies = [pltpu.make_async_copy(meta_hbm[i], meta_ref.at[i], meta_sems.at[i]) for i in range(2)]
     copies += [pltpu.make_async_copy(piece, query_ref.at[i], piece_sems.at[i]) for i, piece in enumerate(reversed(pieces))]
-    for copy in copies:
+    size = pass_dev // CHUNKS
+    own_copies = [
+        pltpu.make_async_copy(own_hbm.at[pl.ds(i * size, size)], own_ref.at[pl.ds(i * size, size)], own_sems.at[i])
+        for i in range(CHUNKS if first else 0)
+    ]
+    for copy in copies + own_copies:
         copy.start()
     best_ref[...] = jnp.zeros_like(best_ref)
     token = lax.broadcasted_iota(jnp.int32, (tok_slots, lanes), 0)
@@ -71,10 +73,15 @@
     for copy in copies:
         copy.wait()
 
-    for which, passages in ((0, passage_refs[0]), (1, passage_refs[1])):
+    for which, passages in ((1, other_ref), (0, own_ref)):
         owner = core if which == 0 else 1 - core
+        if which == 0:
+            for copy in own_copies:
+                copy.wait()
 
         def shard_of(i):
+            if first:
+                return jnp.bitwise_xor(me, jnp.where(i == n - 1, 1, i * 2))
             return jnp.bitwise_xor(me, i * 2 + distances[0])
 
         def list_source(i, total):
@@ -121,22 +128,18 @@
     parts = jnp.dot(jnp.concatenate([high, middle, low], axis=0), add, preferred_element_type=jnp.float32)
     rows = best.shape[0]
     score = (parts[:rows] + parts[rows : 2 * rows] + parts[2 * rows :]) * (1.0 / q_tok)
-    out_ref[...] = score[:, :cap]
-
-
-def merge_kernel(here_ref, there_ref, *outs):
-    for i, out in enumerate(outs):
-        out[:2] = here_ref[2 * i : 2 * i + 2]
-        out[2:] = there_ref[2 * i : 2 * i + 2]
-
-
-def order_kernel(*refs):
-    refs, out_ref = refs[:-1], refs[-1]
-    me = lax.axis_index("shard")
-    for i, piece in enumerate(refs):
-        shard = jnp.bitwise_xor(me, 2 * i)
-        out_ref[0, pl.ds(shard * 2, 2), :] = piece[:2]
-        out_ref[0, pl.ds(jnp.bitwise_xor(shard, 1) * 2, 2), :] = piece[2:]
+    if first:
+        out_ref[...] = score[:, :cap]
+        return
+    for scores, at in ((earlier_ref[...], (*range(0, shards, 2), 1)), (score[:, :cap], distances)):
+        for i, d in enumerate(at):
+            out_ref[pl.ds((shards - 1 - jnp.bitwise_xor(me, d)) * 2, 2), :] = scores[2 * i : 2 * i + 2]
+
+
+def order_kernel(back_ref, out_ref):
+    shards = back_ref.shape[0] // 2
+    for i in range(shards):
+        out_ref[0, 2 * i : 2 * i + 2] = back_ref[2 * (shards - 1 - i) : 2 * (shards - i)]
 
 
 def on_device(shards, queries, passages, passage_len, slot_query, slot_passage, slot_count):
@@ -160,33 +163,34 @@
         pieces[d] = swapped(queries, d)
     other_passages = lax.ppermute(passages, "sub", swap)
 
-    mine, theirs, own_passages = pl.pallas_call(
+    mine, theirs = pl.pallas_call(
         functools.partial(pack_kernel, shards),
-        out_shape=[row, row, jax.ShapeDtypeStruct(passages.shape, passages.dtype)],
-        in_specs=[hbm] * 5,
-        out_specs=[vmem] * 3,
+        out_shape=[row, row],
+        in_specs=[hbm] * 4,
+        out_specs=[vmem] * 2,
         scratch_shapes=[
             pltpu.VMEM((sources, cap), jnp.int32),
             pltpu.VMEM((sources, cap), jnp.int32),
             pltpu.VMEM((sources,), jnp.int32),
             pltpu.VMEM(passage_len.shape, jnp.int32),
             pltpu.SemaphoreType.DMA((4,)),
-            pltpu.SemaphoreType.DMA((CHUNKS,)),
         ],
         compiler_params=params,
-    )(*placed(pltpu.HBM, slot_query.reshape(sources, cap), slot_passage.reshape(sources, cap), slot_count.reshape(sources), passage_len, passages))
-    theirs, pieces[-2] = lax.optimization_barrier((theirs, pieces[-2]))
+    )(*placed(pltpu.HBM, slot_query.reshape(sources, cap), slot_passage.reshape(sources, cap), slot_count.reshape(sources), passage_len))
+    theirs, pieces[-4] = lax.optimization_barrier((theirs, pieces[-4]))
     other = lax.ppermute(theirs, "sub", swap)
     for d in range(1, shards, 2):
         pieces[d] = swapped(pieces[d - 1], 1)
 
-    def scored(distances, after):
-        n = len(distances)
+    def scored(distances, own_passages, *earlier):
+        n, first = len(distances), not earlier
+        scores = jax.ShapeDtypeStruct((2 * n if first else sources, cap), jnp.float32)
+        loaded = jax.ShapeDtypeStruct(passages.shape, passages.dtype)
         return pl.pallas_call(
-            functools.partial(score_kernel, shards, distances, pack, cap),
-            out_shape=jax.ShapeDtypeStruct((2 * n, cap), jnp.float32),
-            in_specs=[anywhere] * (2 + n) + [vmem] * 2 + [anywhere] * len(after),
-            out_specs=vmem,
+            functools.partial(score_kernel, shards, distances, pack, cap, first),
+            out_shape=[scores, loaded] if first else scores,
+            in_specs=[anywhere] * (2 + n) + [hbm if first else vmem, vmem] + [vmem] * len(earlier),
+            out_specs=[vmem] * 2 if first else vmem,
             scratch_shapes=[
                 pltpu.VMEM((n, *queries.shape), queries.dtype),
                 pltpu.VMEM((per_source, 2 * n, 128), jnp.float32),
@@ -194,29 +198,24 @@
                 pltpu.SMEM((n * per_source + 2 * GROUPS,), jnp.int32),
                 pltpu.SemaphoreType.DMA((2,)),
                 pltpu.SemaphoreType.DMA((n,)),
+                pltpu.SemaphoreType.DMA((CHUNKS,)),
             ],
             compiler_params=params,
             cost_estimate=pl.CostEstimate(flops=1_000_000_000, bytes_accessed=9_000_000, transcendentals=0),
-        )(mine, other, *(pieces[d] for d in reversed(distances)), *placed(pltpu.VMEM, own_passages, other_passages), *after)
+        )(mine, other, *(pieces[d] for d in reversed(distances)), own_passages, *placed(pltpu.VMEM, other_passages), *earlier)
 
     pieces[0] = placed(pltpu.HBM, queries)[0]
-    even, odd = range(0, shards, 2), range(1, shards, 2)
-    here = scored(even, ())
-    there = swapped(scored(odd, (here,)), 1)
-    merged = pl.pallas_call(
-        merge_kernel,
-        out_shape=[jax.ShapeDtypeStruct((4, cap), jnp.float32)] * len(even),
-        in_specs=[vmem] * 2,
-        out_specs=[vmem] * len(even),
-        compiler_params=params,
-    )(here, there)
+    scores, own_passages = scored((*range(0, shards, 2), 1), *placed(pltpu.HBM, passages))
+    scores = scored(range(3, shards, 2), *placed(pltpu.VMEM, own_passages), scores)
+    order = [list(reversed(range(shards)))]
+    returned = lax.all_to_all(scores, "shard", split_axis=0, concat_axis=0, axis_index_groups=order, tiled=True)
     return pl.pallas_call(
         order_kernel,
         out_shape=jax.ShapeDtypeStruct((1, sources, cap), jnp.float32),
-        in_specs=[vmem] * len(even),
+        in_specs=[vmem],
         out_specs=vmem,
         compiler_params=params,
-    )(*(swapped(piece, d) if d else piece for d, piece in zip(even, merged)))
+    )(returned)
 
 
 def solution(mesh):

time: 34.1 us -> 30.7 us (0.900)
  blocking collectives: 0 us -> 8.32 us
  waiting for transfers between devices: 9.37 us -> 2.93 us
  starting transfers between devices: 16 us -> 10.7 us
    all_to_all x0 -> x1, blocking collectives: none -> 8.32 us  [on_device(): lax.all_to_all(scores, 'shard', split_axis=0, concat_axis=0, axis_index_g...]
    ppermute x11 -> x7, waiting for transfers between devices: 9.36 us -> 2.93 us  [swapped(): return lax.ppermute(piece, 'shard', [(i, i ^ d) for i in range(shards)])]
    ppermute x11 -> x7, starting transfers between devices: 15.5 us -> 10.2 us  [swapped(): return lax.ppermute(piece, 'shard', [(i, i ^ d) for i in range(shards)])]
    pallas_call x1, Pallas kernels: 2.29 us -> 0.91 us  [on_device(): pl.pallas_call(functools.partial(pack_kernel, shards), out_shape=[row, ro...]
    pallas_call x2, Pallas kernels: 5.67 us -> 6.74 us  [scored(): pl.pallas_call(functools.partial(score_kernel, shards, distances, pack, c...]
  transfers between devices with their start and end apart: 13 -> 9, of which waited for: 6 -> 2; matrix products, arithmetic and copies ran while one was open for 0% -> 0% of each run, Pallas kernels for 15% -> 16%
where the time goes in v6:
time: 30.7 us; the launch traced here: 30.2 us
  starting transfers between devices  10.7 us (35%)
  blocking collectives  8.32 us (27%)
  Pallas kernels  8.25 us (27%)
  waiting for transfers between devices  2.93 us (10%)
    ppermute x7, starting transfers between devices, swapped(): return lax.ppermute(piece, 'shard', [(i, i ^ d) for i in range(shards)])  10.2 us
    all_to_all x1, blocking collectives, on_device(): lax.all_to_all(scores, 'shard', split_axis=0, concat_axis=0, axis_index_g...  8.32 us
    pallas_call x2, Pallas kernels, scored(): pl.pallas_call(functools.partial(score_kernel, shards, distances, pack, c...  6.74 us
    ppermute x7, waiting for transfers between devices, swapped(): return lax.ppermute(piece, 'shard', [(i, i ^ d) for i in range(shards)])  2.93 us
    pallas_call x1, Pallas kernels, on_device(): pl.pallas_call(functools.partial(pack_kernel, shards), out_shape=[row, ro...  0.91 us
  transfers between devices with their start and end apart: 9, of which 2 were waited for; matrix products, arithmetic and copies ran while one was open for 0% of the time, Pallas kernels for 16%

profile of v6, /device:TPU:0, one launch (start us, length us, event | category | flops | bytes accessed | tf_op | source)
XLA Modules:
  0.0 30.2 jit_solution(12496133498129749879)
XLA Ops:
  0.0 0.5 %collective-permute-start.8 = (bf16[128,128,128]{2,1,0:T(8,128)(2,1)}, bf16[128,128,128]{2,1,0:T(8,128)(2,1)S(1)}, u32[]{:S(2)}, u32[]{:S(2)}) collective-permute-start(bf16[128,128,128]{2,1,0:T(8,128)(2,1)} %refs_7_.1), channel_id=1, source_target_pairs={{0,1},{1,0},{2,3},{3,2},{4,5},{5,4},{6,7},{7,6},{8,9},{9,8},{10,11... | collective-permute-start | bytes 12582920 | tf_op jit(solution)/shard_map/ppermute | solution.py:164
  0.5 3.6 %collective-permute-start = (bf16[8,32,128]{2,1,0:T(8,128)(2,1)}, bf16[8,32,128]{2,1,0:T(8,128)(2,1)S(1)}, u32[]{:S(2)}, u32[]{:S(2)}) collective-permute-start(bf16[8,32,128]{2,1,0:T(8,128)(2,1)} %refs_6_.1), channel_id=1, source_target_pairs={{0,8},{2,10},{4,12},{6,14},{8,0},{10,2},{12,4},{14,6},{1,9},{3,11}... | collective-permute-start | bytes 196616 | tf_op jit(solution)/shard_map/ppermute | solution.py:159
  4.0 1.3 %collective-permute-start.2 = (bf16[8,32,128]{2,1,0:T(8,128)(2,1)}, bf16[8,32,128]{2,1,0:T(8,128)(2,1)S(1)}, u32[]{:S(2)}, u32[]{:S(2)}) collective-permute-start(bf16[8,32,128]{2,1,0:T(8,128)(2,1)} %refs_6_.1), channel_id=1, source_target_pairs={{0,12},{2,14},{4,8},{6,10},{8,4},{10,6},{12,0},{14,2},{1,13},{3,15... | collective-permute-start | bytes 196616 | tf_op jit(solution)/shard_map/ppermute | solution.py:159
  5.4 0.2 collective-permute-start.5
  5.6 1.5 %collective-permute-start.7 = (bf16[8,32,128]{2,1,0:T(8,128)(2,1)}, bf16[8,32,128]{2,1,0:T(8,128)(2,1)S(1)}, u32[]{:S(2)}, u32[]{:S(2)}) collective-permute-start(bf16[8,32,128]{2,1,0:T(8,128)(2,1)} %refs_6_.1), channel_id=1, source_target_pairs={{0,2},{2,0},{4,6},{6,4},{8,10},{10,8},{12,14},{14,12},{1,3},{3,1},... | collective-permute-start | bytes 196616 | tf_op jit(solution)/shard_map/ppermute | solution.py:159
  7.1 0.9 %shard_map.64 = (s32[8,128]{1,0:T(8,128)S(1)}, s32[8,128]{1,0:T(8,128)S(1)}) custom-call(s32[16,24]{1,0:T(8,128)} %bitcast.7, s32[16,24]{1,0:T(8,128)} %bitcast.8, s32[16]{0:T(128)} %bitcast.9, s32[128]{0:T(128)} %length_hbm.1), custom_call_target="tpu_custom_call" | custom-call | tf_op jit(solution)/shard_map/pallas_call | solution.py:166
  8.1 0.5 %collective-permute-done.refs_4_ = bf16[8,32,128]{2,1,0:T(8,128)(2,1)S(1)} collective-permute-done((bf16[8,32,128]{2,1,0:T(8,128)(2,1)}, bf16[8,32,128]{2,1,0:T(8,128)(2,1)S(1)}, u32[]{:S(2)}, u32[]{:S(2)}) %collective-permute-start) | collective-permute-done | bytes 65568 | tf_op jit(solution)/shard_map/ppermute | solution.py:159
  8.6 0.0 collective-permute-start.1
  8.6 2.4 %collective-permute-done.2.refs_3_ = bf16[8,32,128]{2,1,0:T(8,128)(2,1)S(1)} collective-permute-done((bf16[8,32,128]{2,1,0:T(8,128)(2,1)}, bf16[8,32,128]{2,1,0:T(8,128)(2,1)S(1)}, u32[]{:S(2)}, u32[]{:S(2)}) %collective-permute-start.2) | collective-permute-done | bytes 65568 | tf_op jit(solution)/shard_map/ppermute | solution.py:159
  11.0 1.5 %collective-permute-start.4 = (bf16[8,32,128]{2,1,0:T(8,128)(2,1)S(1)}, bf16[8,32,128]{2,1,0:T(8,128)(2,1)S(1)}, u32[]{:S(2)}, u32[]{:S(2)}) collective-permute-start(bf16[8,32,128]{2,1,0:T(8,128)(2,1)S(1)} %collective-permute-done.refs_4_), channel_id=1, source_target_pairs={{0,2},{2,0},{4,6},{6,4},{8,10},{10,8},{12,14},{14,12},{1,3},{3,1},... | collective-permute-start | bytes 196616 | tf_op jit(solution)/shard_map/ppermute | solution.py:159
  12.5 0.0 collective-permute-done.5.refs_5_
  12.5 0.5 %collective-permute-start.3 = (bf16[8,32,128]{2,1,0:T(8,128)(2,1)S(1)}, bf16[8,32,128]{2,1,0:T(8,128)(2,1)S(1)}, u32[]{:S(2)}, u32[]{:S(2)}) collective-permute-start(bf16[8,32,128]{2,1,0:T(8,128)(2,1)S(1)} %collective-permute-done.2.refs_3_), channel_id=1, source_target_pairs={{0,2},{2,0},{4,6},{6,4},{8,10},{10,8},{12,14},{14,12},{1,3},{3,1},... | collective-permute-start | bytes 196616 | tf_op jit(solution)/shard_map/ppermute | solution.py:159
  13.0 0.0 collective-permute-done.7.refs_2_
  13.0 1.5 %collective-permute-start.6 = (bf16[8,32,128]{2,1,0:T(8,128)(2,1)S(1)}, bf16[8,32,128]{2,1,0:T(8,128)(2,1)S(1)}, u32[]{:S(2)}, u32[]{:S(2)}) collective-permute-start(bf16[8,32,128]{2,1,0:T(8,128)(2,1)S(1)} %collective-permute-done.5.refs_5_), channel_id=1, source_target_pairs={{0,2},{2,0},{4,6},{6,4},{8,10},{10,8},{12,14},{14,12},{1,3},{3,1},... | collective-permute-start | bytes 196616 | tf_op jit(solution)/shard_map/ppermute | solution.py:159
  14.5 0.0 collective-permute-done.1.refs_1_
  14.5 0.0 collective-permute-done.8.refs_8_.refs_6_
  14.5 3.9 %shard_map.65 = (f32[10,24]{1,0:T(8,128)S(1)}, bf16[128,128,128]{2,1,0:T(8,128)(2,1)S(1)}) custom-call(s32[8,128]{1,0:T(8,128)S(1)} %get-tuple-element.11.refs_0_, s32[8,128]{1,0:T(8,128)S(1)} %collective-permute-done.1.refs_1_, bf16[8,32,128]{2,1,0:T(8,128)(2,1)S(1)} %collective-permute-done.7.refs_2_, ...), custom_call_target="tpu_custom_call" | custom-call | flops 1000000000 | bytes 9000000 | tf_op jit(solution)/shard_map/pallas_call | solution.py:189
  18.4 0.0 collective-permute-done.4.refs_3_
  18.5 0.0 collective-permute-done.3.refs_2_
  18.5 0.0 collective-permute-done.6.refs_4_
  18.5 2.8 %shard_map.66 = f32[16,24]{1,0:T(8,128)S(1)} custom-call(s32[8,128]{1,0:T(8,128)S(1)} %get-tuple-element.11.refs_0_, s32[8,128]{1,0:T(8,128)S(1)} %collective-permute-done.1.refs_1_, bf16[8,32,128]{2,1,0:T(8,128)(2,1)S(1)} %collective-permute-done.3.refs_2_, bf16[8,32,128]{2,1,0:T(8,128)(2,1)S(1)} %collective-permute-done.4.refs_3_, ...), custom_call_target="tpu_custom_call" | custom-call | flops 1000000000 | bytes 9000000 | tf_op jit(solution)/shard_map/pallas_call | solution.py:189
  21.3 8.3 %all_to_all.11 = f32[8,2,24]{2,1,0:T(2,128)S(1)} all-to-all(f32[8,2,24]{2,1,0:T(2,128)S(1)} %bitcast.5), channel_id=1, replica_groups={{14,12,10,8,6,4,2,0},{15,13,11,9,7,5,3,1},{30,28,26,24,22,20,18,16},{31..., dimensions={0} | all-to-all | bytes 3072 | tf_op jit(solution)/shard_map/all_to_all | solution.py:211
  29.6 0.6 %shard_map.67 = f32[1,16,24]{2,1,0:T(8,128)} custom-call(f32[16,24]{1,0:T(8,128)S(1)} %bitcast.6), custom_call_target="tpu_custom_call" | custom-call | tf_op jit(solution)/shard_map/pallas_call | solution.py:212
Async XLA Ops:
  0.0 14.5 %collective-permute-start.8 = (bf16[128,128,128]{2,1,0:T(8,128)(2,1)}, bf16[128,128,128]{2,1,0:T(8,128)(2,1)S(1)}, u32[]{:S(2)}, u32[]{:S(2)}) collective-permute-start(bf16[128,128,128]{2,1,0:T(8,128)(2,1)} %refs_7_.1), channel_id=1, source_target_pairs={{0,1},{1,0},{2,3},{3,2},{4,5},{5,4},{6,7},{7,6},{8,9},{9,8},{10,11... | collective-permute-start | bytes 12582920 | tf_op jit(solution)/shard_map/ppermute | solution.py:164
  0.5 8.1 %collective-permute-start = (bf16[8,32,128]{2,1,0:T(8,128)(2,1)}, bf16[8,32,128]{2,1,0:T(8,128)(2,1)S(1)}, u32[]{:S(2)}, u32[]{:S(2)}) collective-permute-start(bf16[8,32,128]{2,1,0:T(8,128)(2,1)} %refs_6_.1), channel_id=1, source_target_pairs={{0,8},{2,10},{4,12},{6,14},{8,0},{10,2},{12,4},{14,6},{1,9},{3,11}... | collective-permute-start | bytes 196616 | tf_op jit(solution)/shard_map/ppermute | solution.py:159
  4.0 6.9 %collective-permute-start.2 = (bf16[8,32,128]{2,1,0:T(8,128)(2,1)}, bf16[8,32,128]{2,1,0:T(8,128)(2,1)S(1)}, u32[]{:S(2)}, u32[]{:S(2)}) collective-permute-start(bf16[8,32,128]{2,1,0:T(8,128)(2,1)} %refs_6_.1), channel_id=1, source_target_pairs={{0,12},{2,14},{4,8},{6,10},{8,4},{10,6},{12,0},{14,2},{1,13},{3,15... | collective-permute-start | bytes 196616 | tf_op jit(solution)/shard_map/ppermute | solution.py:159
  5.4 7.1 %collective-permute-start.5 = (bf16[8,32,128]{2,1,0:T(8,128)(2,1)}, bf16[8,32,128]{2,1,0:T(8,128)(2,1)S(1)}, u32[]{:S(2)}, u32[]{:S(2)}) collective-permute-start(bf16[8,32,128]{2,1,0:T(8,128)(2,1)} %refs_6_.1), channel_id=1, source_target_pairs={{0,4},{2,6},{4,0},{6,2},{8,12},{10,14},{12,8},{14,10},{1,5},{3,7},... | collective-permute-start | bytes 196616 | tf_op jit(solution)/shard_map/ppermute | solution.py:159
  5.6 7.4 %collective-permute-start.7 = (bf16[8,32,128]{2,1,0:T(8,128)(2,1)}, bf16[8,32,128]{2,1,0:T(8,128)(2,1)S(1)}, u32[]{:S(2)}, u32[]{:S(2)}) collective-permute-start(bf16[8,32,128]{2,1,0:T(8,128)(2,1)} %refs_6_.1), channel_id=1, source_target_pairs={{0,2},{2,0},{4,6},{6,4},{8,10},{10,8},{12,14},{14,12},{1,3},{3,1},... | collective-permute-start | bytes 196616 | tf_op jit(solution)/shard_map/ppermute | solution.py:159
  8.6 5.9 %collective-permute-start.1 = (s32[8,128]{1,0:T(8,128)S(1)}, s32[8,128]{1,0:T(8,128)S(1)}, u32[]{:S(2)}, u32[]{:S(2)}) collective-permute-start(s32[8,128]{1,0:T(8,128)S(1)} %get-tuple-element.13), channel_id=1, source_target_pairs={{0,1},{1,0},{2,3},{3,2},{4,5},{5,4},{6,7},{7,6},{8,9},{9,8},{10,11... | collective-permute-start | bytes 12296 | tf_op jit(solution)/shard_map/ppermute | solution.py:181
  11.0 7.5 %collective-permute-start.4 = (bf16[8,32,128]{2,1,0:T(8,128)(2,1)S(1)}, bf16[8,32,128]{2,1,0:T(8,128)(2,1)S(1)}, u32[]{:S(2)}, u32[]{:S(2)}) collective-permute-start(bf16[8,32,128]{2,1,0:T(8,128)(2,1)S(1)} %collective-permute-done.refs_4_), channel_id=1, source_target_pairs={{0,2},{2,0},{4,6},{6,4},{8,10},{10,8},{12,14},{14,12},{1,3},{3,1},... | collective-permute-start | bytes 196616 | tf_op jit(solution)/shard_map/ppermute | solution.py:159
  12.5 6.0 %collective-permute-start.3 = (bf16[8,32,128]{2,1,0:T(8,128)(2,1)S(1)}, bf16[8,32,128]{2,1,0:T(8,128)(2,1)S(1)}, u32[]{:S(2)}, u32[]{:S(2)}) collective-permute-start(bf16[8,32,128]{2,1,0:T(8,128)(2,1)S(1)} %collective-permute-done.2.refs_3_), channel_id=1, source_target_pairs={{0,2},{2,0},{4,6},{6,4},{8,10},{10,8},{12,14},{14,12},{1,3},{3,1},... | collective-permute-start | bytes 196616 | tf_op jit(solution)/shard_map/ppermute | solution.py:159
  13.0 5.5 %collective-permute-start.6 = (bf16[8,32,128]{2,1,0:T(8,128)(2,1)S(1)}, bf16[8,32,128]{2,1,0:T(8,128)(2,1)S(1)}, u32[]{:S(2)}, u32[]{:S(2)}) collective-permute-start(bf16[8,32,128]{2,1,0:T(8,128)(2,1)S(1)} %collective-permute-done.5.refs_5_), channel_id=1, source_target_pairs={{0,2},{2,0},{4,6},{6,4},{8,10},{10,8},{12,14},{14,12},{1,3},{3,1},... | collective-permute-start | bytes 196616 | tf_op jit(solution)/shard_map/ppermute | solution.py:159

commit v7 on v6

--- a/solution.py
+++ b/solution.py
@@ -13,14 +13,22 @@
 QUERY, PASSAGE, LENGTH, COUNT = 0, 32, 64, 96
 
 
-def pack_kernel(shards, query_hbm, passage_hbm, count_hbm, length_hbm, mine_ref, theirs_ref, query_ref, passage_ref, count_ref, length_ref, sems):
+def pack_kernel(
+    shards, query_hbm, passage_hbm, count_hbm, length_hbm, own_hbm,
+    mine_ref, theirs_ref, own_ref, query_ref, passage_ref, count_ref, length_ref, sems, own_sems,
+):
     copies = [
         pltpu.make_async_copy(src, dst, sems.at[i])
         for i, (src, dst) in enumerate(
             ((query_hbm, query_ref), (passage_hbm, passage_ref), (count_hbm, count_ref), (length_hbm, length_ref))
         )
     ]
-    for copy in copies:
+    size = own_ref.shape[0] // CHUNKS
+    own_copies = [
+        pltpu.make_async_copy(own_hbm.at[pl.ds(i * size, size)], own_ref.at[pl.ds(i * size, size)], own_sems.at[i])
+        for i in range(CHUNKS)
+    ]
+    for copy in copies + own_copies:
         copy.start()
     for copy in copies:
         copy.wait()
@@ -41,30 +49,24 @@
     first = lax.axis_index("sub") == 0
     mine_ref[...] = jnp.where(first, packed[:, 0], packed[:, 1])
     theirs_ref[...] = jnp.where(first, packed[:, 1], packed[:, 0])
+    for copy in own_copies:
+        copy.wait()
 
 
 def score_kernel(shards, distances, pack, cap, first, *refs):
     n = len(distances)
-    meta_hbm, pieces, (own_hbm, other_ref), refs = refs[:2], refs[2 : 2 + n], refs[2 + n : 4 + n], refs[4 + n :]
-    if first:
-        out_ref, own_ref = refs[:2]
-    else:
-        (earlier_ref, out_ref), own_ref = refs[:2], own_hbm
-    query_ref, best_ref, meta_ref, work_ref, meta_sems, piece_sems, own_sems = refs[2:]
+    meta_hbm, pieces, passage_refs, refs = refs[:2], refs[2 : 2 + n], refs[2 + n : 4 + n], refs[4 + n :]
+    earlier_ref = None if first else refs[0]
+    out_ref, query_ref, best_ref, meta_ref, work_ref, meta_sems, piece_sems = refs[-7:]
     q_tok, width = query_ref.shape[2:]
-    pass_dev, tok_slots = other_ref.shape[:2]
+    tok_slots = passage_refs[0].shape[1]
     per_source = best_ref.shape[0]
     lanes = pack * q_tok
     q_bits = q_tok.bit_length() - 1
     me, core = lax.axis_index("shard"), lax.axis_index("sub")
     copies = [pltpu.make_async_copy(meta_hbm[i], meta_ref.at[i], meta_sems.at[i]) for i in range(2)]
     copies += [pltpu.make_async_copy(piece, query_ref.at[i], piece_sems.at[i]) for i, piece in enumerate(reversed(pieces))]
-    size = pass_dev // CHUNKS
-    own_copies = [
-        pltpu.make_async_copy(own_hbm.at[pl.ds(i * size, size)], own_ref.at[pl.ds(i * size, size)], own_sems.at[i])
-        for i in range(CHUNKS if first else 0)
-    ]
-    for copy in copies + own_copies:
+    for copy in copies:
         copy.start()
     best_ref[...] = jnp.zeros_like(best_ref)
     token = lax.broadcasted_iota(jnp.int32, (tok_slots, lanes), 0)
@@ -73,11 +75,8 @@
     for copy in copies:
         copy.wait()
 
-    for which, passages in ((1, other_ref), (0, own_ref)):
+    for which, passages in enumerate(passage_refs):
         owner = core if which == 0 else 1 - core
-        if which == 0:
-            for copy in own_copies:
-                copy.wait()
 
         def shard_of(i):
             if first:
@@ -163,34 +162,33 @@
         pieces[d] = swapped(queries, d)
     other_passages = lax.ppermute(passages, "sub", swap)
 
-    mine, theirs = pl.pallas_call(
+    mine, theirs, own_passages = pl.pallas_call(
         functools.partial(pack_kernel, shards),
-        out_shape=[row, row],
-        in_specs=[hbm] * 4,
-        out_specs=[vmem] * 2,
+        out_shape=[row, row, jax.ShapeDtypeStruct(passages.shape, passages.dtype)],
+        in_specs=[hbm] * 5,
+        out_specs=[vmem] * 3,
         scratch_shapes=[
             pltpu.VMEM((sources, cap), jnp.int32),
             pltpu.VMEM((sources, cap), jnp.int32),
             pltpu.VMEM((sources,), jnp.int32),
             pltpu.VMEM(passage_len.shape, jnp.int32),
             pltpu.SemaphoreType.DMA((4,)),
+            pltpu.SemaphoreType.DMA((CHUNKS,)),
         ],
         compiler_params=params,
-    )(*placed(pltpu.HBM, slot_query.reshape(sources, cap), slot_passage.reshape(sources, cap), slot_count.reshape(sources), passage_len))
-    theirs, pieces[-4] = lax.optimization_barrier((theirs, pieces[-4]))
-    other = lax.ppermute(theirs, "sub", swap)
+    )(*placed(pltpu.HBM, slot_query.reshape(sources, cap), slot_passage.reshape(sources, cap), slot_count.reshape(sources), passage_len, passages))
     for d in range(1, shards, 2):
         pieces[d] = swapped(pieces[d - 1], 1)
-
-    def scored(distances, own_passages, *earlier):
+    theirs, _ = lax.optimization_barrier((theirs, pieces[1]))
+    other = lax.ppermute(theirs, "sub", swap)
+
+    def scored(distances, *earlier):
         n, first = len(distances), not earlier
-        scores = jax.ShapeDtypeStruct((2 * n if first else sources, cap), jnp.float32)
-        loaded = jax.ShapeDtypeStruct(passages.shape, passages.dtype)
         return pl.pallas_call(
             functools.partial(score_kernel, shards, distances, pack, cap, first),
-            out_shape=[scores, loaded] if first else scores,
-            in_specs=[anywhere] * (2 + n) + [hbm if first else vmem, vmem] + [vmem] * len(earlier),
-            out_specs=[vmem] * 2 if first else vmem,
+            out_shape=jax.ShapeDtypeStruct((2 * n if first else sources, cap), jnp.float32),
+            in_specs=[anywhere] * (2 + n) + [vmem] * (2 + len(earlier)),
+            out_specs=vmem,
             scratch_shapes=[
                 pltpu.VMEM((n, *queries.shape), queries.dtype),
                 pltpu.VMEM((per_source, 2 * n, 128), jnp.float32),
@@ -198,15 +196,14 @@
                 pltpu.SMEM((n * per_source + 2 * GROUPS,), jnp.int32),
                 pltpu.SemaphoreType.DMA((2,)),
                 pltpu.SemaphoreType.DMA((n,)),
-                pltpu.SemaphoreType.DMA((CHUNKS,)),
             ],
             compiler_params=params,
             cost_estimate=pl.CostEstimate(flops=1_000_000_000, bytes_accessed=9_000_000, transcendentals=0),
-        )(mine, other, *(pieces[d] for d in reversed(distances)), own_passages, *placed(pltpu.VMEM, other_passages), *earlier)
+        )(mine, other, *(pieces[d] for d in reversed(distances)), *placed(pltpu.VMEM, own_passages, other_passages), *earlier)
 
     pieces[0] = placed(pltpu.HBM, queries)[0]
-    scores, own_passages = scored((*range(0, shards, 2), 1), *placed(pltpu.HBM, passages))
-    scores = scored(range(3, shards, 2), *placed(pltpu.VMEM, own_passages), scores)
+    scores = scored((*range(0, shards, 2), 1))
+    scores = scored(range(3, shards, 2), scores)
     order = [list(reversed(range(shards)))]
     returned = lax.all_to_all(scores, "shard", split_axis=0, concat_axis=0, axis_index_groups=order, tiled=True)
     return pl.pallas_call(

time: 30.7 us -> 29.5 us (0.961)
  starting transfers between devices: 10.7 us -> 9.81 us
  Pallas kernels: 8.25 us -> 7.69 us
  blocking collectives: 8.32 us -> 8.79 us
    pallas_call x2, Pallas kernels: 6.74 us -> 4.8 us  [scored(): pl.pallas_call(functools.partial(score_kernel, shards, distances, pack, c...]
    pallas_call x1, Pallas kernels: 0.91 us -> 2.29 us  [on_device(): pl.pallas_call(functools.partial(pack_kernel, shards), out_shape=[row, ro...]
    ppermute x7, starting transfers between devices: 10.2 us -> 9.28 us  [swapped(): return lax.ppermute(piece, 'shard', [(i, i ^ d) for i in range(shards)])]
    all_to_all x1, blocking collectives: 8.32 us -> 8.79 us  [on_device(): lax.all_to_all(scores, 'shard', split_axis=0, concat_axis=0, axis_index_g...]
  transfers between devices with their start and end apart: 9 -> 9, of which waited for: 2 -> 2; matrix products, arithmetic and copies ran while one was open for 0% -> 0% of each run, Pallas kernels for 16% -> 18%
where the time goes in v7:
time: 29.5 us; the launch traced here: 29.2 us
  starting transfers between devices  9.81 us (33%)
  blocking collectives  8.79 us (30%)
  Pallas kernels  7.69 us (26%)
  waiting for transfers between devices  2.82 us (10%)
    ppermute x7, starting transfers between devices, swapped(): return lax.ppermute(piece, 'shard', [(i, i ^ d) for i in range(shards)])  9.28 us
    all_to_all x1, blocking collectives, on_device(): lax.all_to_all(scores, 'shard', split_axis=0, concat_axis=0, axis_index_g...  8.79 us
    pallas_call x2, Pallas kernels, scored(): pl.pallas_call(functools.partial(score_kernel, shards, distances, pack, c...  4.8 us
    ppermute x7, waiting for transfers between devices, swapped(): return lax.ppermute(piece, 'shard', [(i, i ^ d) for i in range(shards)])  2.81 us
    pallas_call x1, Pallas kernels, on_device(): pl.pallas_call(functools.partial(pack_kernel, shards), out_shape=[row, ro...  2.29 us
    pallas_call x1, Pallas kernels, on_device(): pl.pallas_call(order_kernel, out_shape=jax.ShapeDtypeStruct((1, sources,...  0.6 us
  transfers between devices with their start and end apart: 9, of which 2 were waited for; matrix products, arithmetic and copies ran while one was open for 0% of the time, Pallas kernels for 18%

profile of v7, /device:TPU:0, one launch (start us, length us, event | category | flops | bytes accessed | tf_op | source)
XLA Modules:
  0.0 29.2 jit_solution(13914818746361846685)
XLA Ops:
  0.0 0.5 %collective-permute-start.8 = (bf16[128,128,128]{2,1,0:T(8,128)(2,1)}, bf16[128,128,128]{2,1,0:T(8,128)(2,1)S(1)}, u32[]{:S(2)}, u32[]{:S(2)}) collective-permute-start(bf16[128,128,128]{2,1,0:T(8,128)(2,1)} %own_hbm.1), channel_id=1, source_target_pairs={{0,1},{1,0},{2,3},{3,2},{4,5},{5,4},{6,7},{7,6},{8,9},{9,8},{10,11... | collective-permute-start | bytes 12582920 | tf_op jit(solution)/shard_map/ppermute | solution.py:163
  0.5 2.5 %collective-permute-start = (bf16[8,32,128]{2,1,0:T(8,128)(2,1)}, bf16[8,32,128]{2,1,0:T(8,128)(2,1)S(1)}, u32[]{:S(2)}, u32[]{:S(2)}) collective-permute-start(bf16[8,32,128]{2,1,0:T(8,128)(2,1)} %refs_6_.1), channel_id=1, source_target_pairs={{0,2},{2,0},{4,6},{6,4},{8,10},{10,8},{12,14},{14,12},{1,3},{3,1},... | collective-permute-start | bytes 196616 | tf_op jit(solution)/shard_map/ppermute | solution.py:158
  3.0 3.6 %collective-permute-start.2 = (bf16[8,32,128]{2,1,0:T(8,128)(2,1)}, bf16[8,32,128]{2,1,0:T(8,128)(2,1)S(1)}, u32[]{:S(2)}, u32[]{:S(2)}) collective-permute-start(bf16[8,32,128]{2,1,0:T(8,128)(2,1)} %refs_6_.1), channel_id=1, source_target_pairs={{0,12},{2,14},{4,8},{6,10},{8,4},{10,6},{12,0},{14,2},{1,13},{3,15... | collective-permute-start | bytes 196616 | tf_op jit(solution)/shard_map/ppermute | solution.py:158
  6.6 0.0 collective-permute-start.4
  6.6 0.8 %collective-permute-start.6 = (bf16[8,32,128]{2,1,0:T(8,128)(2,1)}, bf16[8,32,128]{2,1,0:T(8,128)(2,1)S(1)}, u32[]{:S(2)}, u32[]{:S(2)}) collective-permute-start(bf16[8,32,128]{2,1,0:T(8,128)(2,1)} %refs_6_.1), channel_id=1, source_target_pairs={{0,4},{2,6},{4,0},{6,2},{8,12},{10,14},{12,8},{14,10},{1,5},{3,7},... | collective-permute-start | bytes 196616 | tf_op jit(solution)/shard_map/ppermute | solution.py:158
  7.4 2.3 %shard_map.64 = (s32[8,128]{1,0:T(8,128)S(1)}, s32[8,128]{1,0:T(8,128)S(1)}, bf16[128,128,128]{2,1,0:T(8,128)(2,1)S(1)}) custom-call(s32[16,24]{1,0:T(8,128)} %bitcast.7, s32[16,24]{1,0:T(8,128)} %bitcast.8, s32[16]{0:T(128)} %bitcast.9, s32[128]{0:T(128)} %length_hbm.1, bf16[128,128,128]{2,1,0:T(8,128)(2,1)} %own_hbm.1), custom_call_target="tpu_custom_call" | custom-call | tf_op jit(solution)/shard_map/pallas_call | solution.py:165
  9.7 0.0 collective-permute-done.refs_2_
  9.7 0.1 collective-permute-start.1
  9.7 0.0 collective-permute-done.2.refs_3_
  9.8 0.4 %collective-permute-start.3 = (bf16[8,32,128]{2,1,0:T(8,128)(2,1)S(1)}, bf16[8,32,128]{2,1,0:T(8,128)(2,1)S(1)}, u32[]{:S(2)}, u32[]{:S(2)}) collective-permute-start(bf16[8,32,128]{2,1,0:T(8,128)(2,1)S(1)} %collective-permute-done.2.refs_3_), channel_id=1, source_target_pairs={{0,2},{2,0},{4,6},{6,4},{8,10},{10,8},{12,14},{14,12},{1,3},{3,1},... | collective-permute-start | bytes 196616 | tf_op jit(solution)/shard_map/ppermute | solution.py:158
  10.1 2.6 %collective-permute-done.4.refs_4_ = bf16[8,32,128]{2,1,0:T(8,128)(2,1)S(1)} collective-permute-done((bf16[8,32,128]{2,1,0:T(8,128)(2,1)}, bf16[8,32,128]{2,1,0:T(8,128)(2,1)S(1)}, u32[]{:S(2)}, u32[]{:S(2)}) %collective-permute-start.4) | collective-permute-done | bytes 65568 | tf_op jit(solution)/shard_map/ppermute | solution.py:158
  12.7 0.5 %collective-permute-start.5 = (bf16[8,32,128]{2,1,0:T(8,128)(2,1)S(1)}, bf16[8,32,128]{2,1,0:T(8,128)(2,1)S(1)}, u32[]{:S(2)}, u32[]{:S(2)}) collective-permute-start(bf16[8,32,128]{2,1,0:T(8,128)(2,1)S(1)} %collective-permute-done.4.refs_4_), channel_id=1, source_target_pairs={{0,2},{2,0},{4,6},{6,4},{8,10},{10,8},{12,14},{14,12},{1,3},{3,1},... | collective-permute-start | bytes 196616 | tf_op jit(solution)/shard_map/ppermute | solution.py:158
  13.2 0.0 collective-permute-done.6.refs_5_
  13.2 1.5 %collective-permute-start.7 = (bf16[8,32,128]{2,1,0:T(8,128)(2,1)S(1)}, bf16[8,32,128]{2,1,0:T(8,128)(2,1)S(1)}, u32[]{:S(2)}, u32[]{:S(2)}) collective-permute-start(bf16[8,32,128]{2,1,0:T(8,128)(2,1)S(1)} %collective-permute-done.6.refs_5_), channel_id=1, source_target_pairs={{0,2},{2,0},{4,6},{6,4},{8,10},{10,8},{12,14},{14,12},{1,3},{3,1},... | collective-permute-start | bytes 196616 | tf_op jit(solution)/shard_map/ppermute | solution.py:158
  14.7 0.0 collective-permute-done.1.refs_1_
  14.7 0.0 collective-permute-done.8.refs_8_.refs_6_
  14.7 2.9 %shard_map.65.refs_7_ = f32[10,24]{1,0:T(8,128)S(1)} custom-call(s32[8,128]{1,0:T(8,128)S(1)} %get-tuple-element.9.refs_0_, s32[8,128]{1,0:T(8,128)S(1)} %collective-permute-done.1.refs_1_, bf16[8,32,128]{2,1,0:T(8,128)(2,1)S(1)} %collective-permute-done.refs_2_, bf16[8,32,128]{2,1,0:T(8,128)(2,1)S(1)} %collective-permute-done.2.refs_3_, ...), custom_call_target="tpu_custom_call" | custom-call | flops 1000000000 | bytes 9000000 | tf_op jit(solution)/shard_map/pallas_call | solution.py:187
  17.7 0.0 collective-permute-done.3.refs_2_
  17.7 0.0 collective-permute-done.5.refs_3_
  17.7 0.2 collective-permute-done.7.refs_4_
  17.9 1.9 %shard_map.66 = f32[16,24]{1,0:T(8,128)S(1)} custom-call(s32[8,128]{1,0:T(8,128)S(1)} %get-tuple-element.9.refs_0_, s32[8,128]{1,0:T(8,128)S(1)} %collective-permute-done.1.refs_1_, bf16[8,32,128]{2,1,0:T(8,128)(2,1)S(1)} %collective-permute-done.3.refs_2_, bf16[8,32,128]{2,1,0:T(8,128)(2,1)S(1)} %collective-permute-done.5.refs_3_, ...), custom_call_target="tpu_custom_call" | custom-call | flops 1000000000 | bytes 9000000 | tf_op jit(solution)/shard_map/pallas_call | solution.py:187
  19.8 8.8 %all_to_all.11 = f32[8,2,24]{2,1,0:T(2,128)S(1)} all-to-all(f32[8,2,24]{2,1,0:T(2,128)S(1)} %bitcast.5), channel_id=1, replica_groups={{14,12,10,8,6,4,2,0},{15,13,11,9,7,5,3,1},{30,28,26,24,22,20,18,16},{31..., dimensions={0} | all-to-all | bytes 3072 | tf_op jit(solution)/shard_map/all_to_all | solution.py:208
  28.6 0.6 %shard_map.67 = f32[1,16,24]{2,1,0:T(8,128)} custom-call(f32[16,24]{1,0:T(8,128)S(1)} %bitcast.6), custom_call_target="tpu_custom_call" | custom-call | tf_op jit(solution)/shard_map/pallas_call | solution.py:209
Async XLA Ops:
  0.0 14.7 %collective-permute-start.8 = (bf16[128,128,128]{2,1,0:T(8,128)(2,1)}, bf16[128,128,128]{2,1,0:T(8,128)(2,1)S(1)}, u32[]{:S(2)}, u32[]{:S(2)}) collective-permute-start(bf16[128,128,128]{2,1,0:T(8,128)(2,1)} %own_hbm.1), channel_id=1, source_target_pairs={{0,1},{1,0},{2,3},{3,2},{4,5},{5,4},{6,7},{7,6},{8,9},{9,8},{10,11... | collective-permute-start | bytes 12582920 | tf_op jit(solution)/shard_map/ppermute | solution.py:163
  0.5 9.2 %collective-permute-start = (bf16[8,32,128]{2,1,0:T(8,128)(2,1)}, bf16[8,32,128]{2,1,0:T(8,128)(2,1)S(1)}, u32[]{:S(2)}, u32[]{:S(2)}) collective-permute-start(bf16[8,32,128]{2,1,0:T(8,128)(2,1)} %refs_6_.1), channel_id=1, source_target_pairs={{0,2},{2,0},{4,6},{6,4},{8,10},{10,8},{12,14},{14,12},{1,3},{3,1},... | collective-permute-start | bytes 196616 | tf_op jit(solution)/shard_map/ppermute | solution.py:158
  3.0 6.8 %collective-permute-start.2 = (bf16[8,32,128]{2,1,0:T(8,128)(2,1)}, bf16[8,32,128]{2,1,0:T(8,128)(2,1)S(1)}, u32[]{:S(2)}, u32[]{:S(2)}) collective-permute-start(bf16[8,32,128]{2,1,0:T(8,128)(2,1)} %refs_6_.1), channel_id=1, source_target_pairs={{0,12},{2,14},{4,8},{6,10},{8,4},{10,6},{12,0},{14,2},{1,13},{3,15... | collective-permute-start | bytes 196616 | tf_op jit(solution)/shard_map/ppermute | solution.py:158
  6.6 6.1 %collective-permute-start.4 = (bf16[8,32,128]{2,1,0:T(8,128)(2,1)}, bf16[8,32,128]{2,1,0:T(8,128)(2,1)S(1)}, u32[]{:S(2)}, u32[]{:S(2)}) collective-permute-start(bf16[8,32,128]{2,1,0:T(8,128)(2,1)} %refs_6_.1), channel_id=1, source_target_pairs={{0,8},{2,10},{4,12},{6,14},{8,0},{10,2},{12,4},{14,6},{1,9},{3,11}... | collective-permute-start | bytes 196616 | tf_op jit(solution)/shard_map/ppermute | solution.py:158
  6.6 6.6 %collective-permute-start.6 = (bf16[8,32,128]{2,1,0:T(8,128)(2,1)}, bf16[8,32,128]{2,1,0:T(8,128)(2,1)S(1)}, u32[]{:S(2)}, u32[]{:S(2)}) collective-permute-start(bf16[8,32,128]{2,1,0:T(8,128)(2,1)} %refs_6_.1), channel_id=1, source_target_pairs={{0,4},{2,6},{4,0},{6,2},{8,12},{10,14},{12,8},{14,10},{1,5},{3,7},... | collective-permute-start | bytes 196616 | tf_op jit(solution)/shard_map/ppermute | solution.py:158
  9.7 5.0 %collective-permute-start.1 = (s32[8,128]{1,0:T(8,128)S(1)}, s32[8,128]{1,0:T(8,128)S(1)}, u32[]{:S(2)}, u32[]{:S(2)}) collective-permute-start(s32[8,128]{1,0:T(8,128)S(1)} %get-tuple-element.11), channel_id=1, source_target_pairs={{0,1},{1,0},{2,3},{3,2},{4,5},{5,4},{6,7},{7,6},{8,9},{9,8},{10,11... | collective-permute-start | bytes 12296 | tf_op jit(solution)/shard_map/ppermute | solution.py:183
  9.8 7.9 %collective-permute-start.3 = (bf16[8,32,128]{2,1,0:T(8,128)(2,1)S(1)}, bf16[8,32,128]{2,1,0:T(8,128)(2,1)S(1)}, u32[]{:S(2)}, u32[]{:S(2)}) collective-permute-start(bf16[8,32,128]{2,1,0:T(8,128)(2,1)S(1)} %collective-permute-done.2.refs_3_), channel_id=1, source_target_pairs={{0,2},{2,0},{4,6},{6,4},{8,10},{10,8},{12,14},{14,12},{1,3},{3,1},... | collective-permute-start | bytes 196616 | tf_op jit(solution)/shard_map/ppermute | solution.py:158
  12.7 5.0 %collective-permute-start.5 = (bf16[8,32,128]{2,1,0:T(8,128)(2,1)S(1)}, bf16[8,32,128]{2,1,0:T(8,128)(2,1)S(1)}, u32[]{:S(2)}, u32[]{:S(2)}) collective-permute-start(bf16[8,32,128]{2,1,0:T(8,128)(2,1)S(1)} %collective-permute-done.4.refs_4_), channel_id=1, source_target_pairs={{0,2},{2,0},{4,6},{6,4},{8,10},{10,8},{12,14},{14,12},{1,3},{3,1},... | collective-permute-start | bytes 196616 | tf_op jit(solution)/shard_map/ppermute | solution.py:158
  13.2 4.7 %collective-permute-start.7 = (bf16[8,32,128]{2,1,0:T(8,128)(2,1)S(1)}, bf16[8,32,128]{2,1,0:T(8,128)(2,1)S(1)}, u32[]{:S(2)}, u32[]{:S(2)}) collective-permute-start(bf16[8,32,128]{2,1,0:T(8,128)(2,1)S(1)} %collective-permute-done.6.refs_5_), channel_id=1, source_target_pairs={{0,2},{2,0},{4,6},{6,4},{8,10},{10,8},{12,14},{14,12},{1,3},{3,1},... | collective-permute-start | bytes 196616 | tf_op jit(solution)/shard_map/ppermute | solution.py:158

commit v8 on v7

--- a/solution.py
+++ b/solution.py
@@ -61,16 +61,14 @@
     q_tok, width = query_ref.shape[2:]
     tok_slots = passage_refs[0].shape[1]
     per_source = best_ref.shape[0]
-    lanes = pack * q_tok
-    q_bits = q_tok.bit_length() - 1
     me, core = lax.axis_index("shard"), lax.axis_index("sub")
     copies = [pltpu.make_async_copy(meta_hbm[i], meta_ref.at[i], meta_sems.at[i]) for i in range(2)]
     copies += [pltpu.make_async_copy(piece, query_ref.at[i], piece_sems.at[i]) for i, piece in enumerate(reversed(pieces))]
     for copy in copies:
         copy.start()
     best_ref[...] = jnp.zeros_like(best_ref)
-    token = lax.broadcasted_iota(jnp.int32, (tok_slots, lanes), 0)
-    place = lax.shift_right_logical(lax.broadcasted_iota(jnp.int32, (1, lanes), 1), q_bits)
+    token = lax.broadcasted_iota(jnp.int32, (q_tok, tok_slots), 1)
+    slot_lane = lax.broadcasted_iota(jnp.int32, best_ref.shape[2:], 1)
     blank = jnp.zeros((q_tok, width), query_ref.dtype)
     for copy in copies:
         copy.wait()
@@ -98,35 +96,29 @@
                 work = work_ref[step * GROUPS + j]
                 i, g = lax.shift_right_logical(work, SHIFT), jnp.bitwise_and(work, (1 << SHIFT) - 1)
                 shard = shard_of(i)
-                rows, cols, limit = [], [], jnp.zeros((1, lanes), jnp.int32)
-                for a in range(pack):
-                    slot = g * pack + a
-                    query, passage = meta_ref[which, shard, QUERY + slot], meta_ref[which, shard, PASSAGE + slot]
-                    rows.append(jnp.concatenate([blank] * a + [query_ref[i, query]] + [blank] * (pack - 1 - a), axis=1))
-                    cols.append(passages[passage])
-                    limit = jnp.where(place == a, meta_ref[which, shard, LENGTH + slot], limit)
-                sims = lax.dot_general(
-                    jnp.concatenate(cols, axis=1), jnp.concatenate(rows, axis=0),
-                    (((1,), (1,)), ((), ())), preferred_element_type=jnp.float32,
-                )
-                best = jnp.max(jnp.where(token < limit, sims, -1e30), axis=0, keepdims=True)
-                best = jnp.where(place + g * pack < meta_ref[which, shard, COUNT], best, 0.0)
-                best_ref[g, pl.ds(i * 2 + owner, 1), :] = best
+                best = jnp.zeros(best_ref.shape[2:], jnp.float32)
+                for a in range(0, pack, 2):
+                    slots = [g * pack + a, g * pack + a + 1]
+                    query = [query_ref[i, meta_ref[which, shard, QUERY + slot]] for slot in slots]
+                    passage = [passages[meta_ref[which, shard, PASSAGE + slot]] for slot in slots]
+                    sims = lax.dot_general(
+                        jnp.concatenate(
+                            [jnp.concatenate([query[0], blank], axis=1), jnp.concatenate([blank, query[1]], axis=1)], axis=0
+                        ),
+                        jnp.concatenate(passage, axis=1),
+                        (((1,), (1,)), ((), ())), preferred_element_type=jnp.float32,
+                    )
+                    for half, slot in enumerate(slots):
+                        live = token < meta_ref[which, shard, LENGTH + slot]
+                        most = jnp.max(jnp.where(live, sims[half * q_tok : (half + 1) * q_tok], -1e30), axis=1, keepdims=True)
+                        most = sum(most[r : r + 8] for r in range(0, q_tok, 8))
+                        best = jnp.where(slot_lane == slot, most, best)
+                best_ref[g, i * 2 + owner] = jnp.where(slot_lane < meta_ref[which, shard, COUNT], best, 0.0)
             return carry
 
         lax.fori_loop(0, lax.shift_right_logical(total + GROUPS - 1, GROUPS.bit_length() - 1), one_step, 0)
 
-    best = jnp.concatenate([best_ref[g] for g in range(per_source)], axis=1)
-    high = best.astype(jnp.bfloat16)
-    rest = best - high.astype(jnp.float32)
-    middle = rest.astype(jnp.bfloat16)
-    low = (rest - middle.astype(jnp.float32)).astype(jnp.bfloat16)
-    row = lax.broadcasted_iota(jnp.int32, (per_source * lanes, 128), 0)
-    col = lax.broadcasted_iota(jnp.int32, (per_source * lanes, 128), 1)
-    add = jnp.where(lax.shift_right_logical(row, q_bits) == col, 1.0, 0.0).astype(jnp.bfloat16)
-    parts = jnp.dot(jnp.concatenate([high, middle, low], axis=0), add, preferred_element_type=jnp.float32)
-    rows = best.shape[0]
-    score = (parts[:rows] + parts[rows : 2 * rows] + parts[2 * rows :]) * (1.0 / q_tok)
+    score = jnp.sum(sum(best_ref[g] for g in range(per_source)), axis=1) * (1.0 / q_tok)
     if first:
         out_ref[...] = score[:, :cap]
         return
@@ -144,7 +136,7 @@
 def on_device(shards, queries, passages, passage_len, slot_query, slot_passage, slot_count):
     sources, _, cap = slot_query.shape
     q_dev, q_tok, width = queries.shape
-    pack = 128 // q_tok
+    pack = 4
     per_source = -(-cap // pack)
     swap = [(0, 1), (1, 0)]
     vmem, hbm, anywhere = (pl.BlockSpec(memory_space=space) for space in (pltpu.VMEM, pltpu.HBM, pl.ANY))
@@ -191,7 +183,7 @@
             out_specs=vmem,
             scratch_shapes=[
                 pltpu.VMEM((n, *queries.shape), queries.dtype),
-                pltpu.VMEM((per_source, 2 * n, 128), jnp.float32),
+                pltpu.VMEM((per_source, 2 * n, 8, 128), jnp.float32),
                 pltpu.SMEM((2, shards, 128), jnp.int32),
                 pltpu.SMEM((n * per_source + 2 * GROUPS,), jnp.int32),
                 pltpu.SemaphoreType.DMA((2,)),

time: 29.5 us -> 30.1 us (1.020)
  Pallas kernels: 7.69 us -> 8.18 us
    pallas_call x2, Pallas kernels: 4.8 us -> 5.29 us  [scored(): pl.pallas_call(functools.partial(score_kernel, shards, distances, pack, c...]
  transfers between devices with their start and end apart: 9 -> 9, of which waited for: 2 -> 1; matrix products, arithmetic and copies ran while one was open for 0% -> 0% of each run, Pallas kernels for 18% -> 19%
where the time goes in v8:
time: 30.1 us; the launch traced here: 29.7 us
  starting transfers between devices  9.81 us (33%)
  blocking collectives  9.01 us (30%)
  Pallas kernels  8.18 us (27%)
  waiting for transfers between devices  2.58 us (9%)
    ppermute x7, starting transfers between devices, swapped(): return lax.ppermute(piece, 'shard', [(i, i ^ d) for i in range(shards)])  9.28 us
    all_to_all x1, blocking collectives, on_device(): lax.all_to_all(scores, 'shard', split_axis=0, concat_axis=0, axis_index_g...  9.01 us
    pallas_call x2, Pallas kernels, scored(): pl.pallas_call(functools.partial(score_kernel, shards, distances, pack, c...  5.29 us
    ppermute x7, waiting for transfers between devices, swapped(): return lax.ppermute(piece, 'shard', [(i, i ^ d) for i in range(shards)])  2.58 us
    pallas_call x1, Pallas kernels, on_device(): pl.pallas_call(functools.partial(pack_kernel, shards), out_shape=[row, ro...  2.29 us
    pallas_call x1, Pallas kernels, on_device(): pl.pallas_call(order_kernel, out_shape=jax.ShapeDtypeStruct((1, sources,...  0.6 us
  transfers between devices with their start and end apart: 9, of which 1 were waited for; matrix products, arithmetic and copies ran while one was open for 0% of the time, Pallas kernels for 19%

profile of v8, /device:TPU:0, one launch (start us, length us, event | category | flops | bytes accessed | tf_op | source)
XLA Modules:
  0.0 29.7 jit_solution(17534738402600385129)
XLA Ops:
  0.0 0.5 %collective-permute-start.8 = (bf16[128,128,128]{2,1,0:T(8,128)(2,1)}, bf16[128,128,128]{2,1,0:T(8,128)(2,1)S(1)}, u32[]{:S(2)}, u32[]{:S(2)}) collective-permute-start(bf16[128,128,128]{2,1,0:T(8,128)(2,1)} %own_hbm.1), channel_id=1, source_target_pairs={{0,1},{1,0},{2,3},{3,2},{4,5},{5,4},{6,7},{7,6},{8,9},{9,8},{10,11... | collective-permute-start | bytes 12582920 | tf_op jit(solution)/shard_map/ppermute | solution.py:155
  0.5 2.5 %collective-permute-start = (bf16[8,32,128]{2,1,0:T(8,128)(2,1)}, bf16[8,32,128]{2,1,0:T(8,128)(2,1)S(1)}, u32[]{:S(2)}, u32[]{:S(2)}) collective-permute-start(bf16[8,32,128]{2,1,0:T(8,128)(2,1)} %refs_6_.1), channel_id=1, source_target_pairs={{0,2},{2,0},{4,6},{6,4},{8,10},{10,8},{12,14},{14,12},{1,3},{3,1},... | collective-permute-start | bytes 196616 | tf_op jit(solution)/shard_map/ppermute | solution.py:150
  3.0 3.6 %collective-permute-start.2 = (bf16[8,32,128]{2,1,0:T(8,128)(2,1)}, bf16[8,32,128]{2,1,0:T(8,128)(2,1)S(1)}, u32[]{:S(2)}, u32[]{:S(2)}) collective-permute-start(bf16[8,32,128]{2,1,0:T(8,128)(2,1)} %refs_6_.1), channel_id=1, source_target_pairs={{0,12},{2,14},{4,8},{6,10},{8,4},{10,6},{12,0},{14,2},{1,13},{3,15... | collective-permute-start | bytes 196616 | tf_op jit(solution)/shard_map/ppermute | solution.py:150
  6.6 0.0 collective-permute-start.4
  6.6 0.8 %collective-permute-start.6 = (bf16[8,32,128]{2,1,0:T(8,128)(2,1)}, bf16[8,32,128]{2,1,0:T(8,128)(2,1)S(1)}, u32[]{:S(2)}, u32[]{:S(2)}) collective-permute-start(bf16[8,32,128]{2,1,0:T(8,128)(2,1)} %refs_6_.1), channel_id=1, source_target_pairs={{0,4},{2,6},{4,0},{6,2},{8,12},{10,14},{12,8},{14,10},{1,5},{3,7},... | collective-permute-start | bytes 196616 | tf_op jit(solution)/shard_map/ppermute | solution.py:150
  7.4 2.3 %shard_map.64 = (s32[8,128]{1,0:T(8,128)S(1)}, s32[8,128]{1,0:T(8,128)S(1)}, bf16[128,128,128]{2,1,0:T(8,128)(2,1)S(1)}) custom-call(s32[16,24]{1,0:T(8,128)} %bitcast.7, s32[16,24]{1,0:T(8,128)} %bitcast.8, s32[16]{0:T(128)} %bitcast.9, s32[128]{0:T(128)} %length_hbm.1, bf16[128,128,128]{2,1,0:T(8,128)(2,1)} %own_hbm.1), custom_call_target="tpu_custom_call" | custom-call | tf_op jit(solution)/shard_map/pallas_call | solution.py:157
  9.7 0.0 collective-permute-done.refs_2_
  9.7 0.1 collective-permute-start.1
  9.7 0.0 collective-permute-done.2.refs_3_
  9.8 0.4 %collective-permute-start.3 = (bf16[8,32,128]{2,1,0:T(8,128)(2,1)S(1)}, bf16[8,32,128]{2,1,0:T(8,128)(2,1)S(1)}, u32[]{:S(2)}, u32[]{:S(2)}) collective-permute-start(bf16[8,32,128]{2,1,0:T(8,128)(2,1)S(1)} %collective-permute-done.2.refs_3_), channel_id=1, source_target_pairs={{0,2},{2,0},{4,6},{6,4},{8,10},{10,8},{12,14},{14,12},{1,3},{3,1},... | collective-permute-start | bytes 196616 | tf_op jit(solution)/shard_map/ppermute | solution.py:150
  10.1 2.6 %collective-permute-done.4.refs_4_ = bf16[8,32,128]{2,1,0:T(8,128)(2,1)S(1)} collective-permute-done((bf16[8,32,128]{2,1,0:T(8,128)(2,1)}, bf16[8,32,128]{2,1,0:T(8,128)(2,1)S(1)}, u32[]{:S(2)}, u32[]{:S(2)}) %collective-permute-start.4) | collective-permute-done | bytes 65568 | tf_op jit(solution)/shard_map/ppermute | solution.py:150
  12.7 0.5 %collective-permute-start.5 = (bf16[8,32,128]{2,1,0:T(8,128)(2,1)S(1)}, bf16[8,32,128]{2,1,0:T(8,128)(2,1)S(1)}, u32[]{:S(2)}, u32[]{:S(2)}) collective-permute-start(bf16[8,32,128]{2,1,0:T(8,128)(2,1)S(1)} %collective-permute-done.4.refs_4_), channel_id=1, source_target_pairs={{0,2},{2,0},{4,6},{6,4},{8,10},{10,8},{12,14},{14,12},{1,3},{3,1},... | collective-permute-start | bytes 196616 | tf_op jit(solution)/shard_map/ppermute | solution.py:150
  13.2 0.0 collective-permute-done.6.refs_5_
  13.2 1.5 %collective-permute-start.7 = (bf16[8,32,128]{2,1,0:T(8,128)(2,1)S(1)}, bf16[8,32,128]{2,1,0:T(8,128)(2,1)S(1)}, u32[]{:S(2)}, u32[]{:S(2)}) collective-permute-start(bf16[8,32,128]{2,1,0:T(8,128)(2,1)S(1)} %collective-permute-done.6.refs_5_), channel_id=1, source_target_pairs={{0,2},{2,0},{4,6},{6,4},{8,10},{10,8},{12,14},{14,12},{1,3},{3,1},... | collective-permute-start | bytes 196616 | tf_op jit(solution)/shard_map/ppermute | solution.py:150
  14.7 0.0 collective-permute-done.1.refs_1_
  14.7 0.0 collective-permute-done.8.refs_8_.refs_6_
  14.7 3.3 %shard_map.65.refs_7_ = f32[10,24]{1,0:T(8,128)S(1)} custom-call(s32[8,128]{1,0:T(8,128)S(1)} %get-tuple-element.9.refs_0_, s32[8,128]{1,0:T(8,128)S(1)} %collective-permute-done.1.refs_1_, bf16[8,32,128]{2,1,0:T(8,128)(2,1)S(1)} %collective-permute-done.refs_2_, bf16[8,32,128]{2,1,0:T(8,128)(2,1)S(1)} %collective-permute-done.2.refs_3_, ...), custom_call_target="tpu_custom_call" | custom-call | flops 1000000000 | bytes 9000000 | tf_op jit(solution)/shard_map/pallas_call | solution.py:179
  18.0 0.0 collective-permute-done.3.refs_2_
  18.0 0.0 collective-permute-done.5.refs_3_
  18.0 0.0 collective-permute-done.7.refs_4_
  18.1 2.0 %shard_map.66 = f32[16,24]{1,0:T(8,128)S(1)} custom-call(s32[8,128]{1,0:T(8,128)S(1)} %get-tuple-element.9.refs_0_, s32[8,128]{1,0:T(8,128)S(1)} %collective-permute-done.1.refs_1_, bf16[8,32,128]{2,1,0:T(8,128)(2,1)S(1)} %collective-permute-done.3.refs_2_, bf16[8,32,128]{2,1,0:T(8,128)(2,1)S(1)} %collective-permute-done.5.refs_3_, ...), custom_call_target="tpu_custom_call" | custom-call | flops 1000000000 | bytes 9000000 | tf_op jit(solution)/shard_map/pallas_call | solution.py:179
  20.0 9.0 %all_to_all.11 = f32[8,2,24]{2,1,0:T(2,128)S(1)} all-to-all(f32[8,2,24]{2,1,0:T(2,128)S(1)} %bitcast.5), channel_id=1, replica_groups={{14,12,10,8,6,4,2,0},{15,13,11,9,7,5,3,1},{30,28,26,24,22,20,18,16},{31..., dimensions={0} | all-to-all | bytes 3072 | tf_op jit(solution)/shard_map/all_to_all | solution.py:200
  29.1 0.6 %shard_map.67 = f32[1,16,24]{2,1,0:T(8,128)} custom-call(f32[16,24]{1,0:T(8,128)S(1)} %bitcast.6), custom_call_target="tpu_custom_call" | custom-call | tf_op jit(solution)/shard_map/pallas_call | solution.py:201
Async XLA Ops:
  0.0 14.7 %collective-permute-start.8 = (bf16[128,128,128]{2,1,0:T(8,128)(2,1)}, bf16[128,128,128]{2,1,0:T(8,128)(2,1)S(1)}, u32[]{:S(2)}, u32[]{:S(2)}) collective-permute-start(bf16[128,128,128]{2,1,0:T(8,128)(2,1)} %own_hbm.1), channel_id=1, source_target_pairs={{0,1},{1,0},{2,3},{3,2},{4,5},{5,4},{6,7},{7,6},{8,9},{9,8},{10,11... | collective-permute-start | bytes 12582920 | tf_op jit(solution)/shard_map/ppermute | solution.py:155
  0.5 9.2 %collective-permute-start = (bf16[8,32,128]{2,1,0:T(8,128)(2,1)}, bf16[8,32,128]{2,1,0:T(8,128)(2,1)S(1)}, u32[]{:S(2)}, u32[]{:S(2)}) collective-permute-start(bf16[8,32,128]{2,1,0:T(8,128)(2,1)} %refs_6_.1), channel_id=1, source_target_pairs={{0,2},{2,0},{4,6},{6,4},{8,10},{10,8},{12,14},{14,12},{1,3},{3,1},... | collective-permute-start | bytes 196616 | tf_op jit(solution)/shard_map/ppermute | solution.py:150
  3.0 6.8 %collective-permute-start.2 = (bf16[8,32,128]{2,1,0:T(8,128)(2,1)}, bf16[8,32,128]{2,1,0:T(8,128)(2,1)S(1)}, u32[]{:S(2)}, u32[]{:S(2)}) collective-permute-start(bf16[8,32,128]{2,1,0:T(8,128)(2,1)} %refs_6_.1), channel_id=1, source_target_pairs={{0,12},{2,14},{4,8},{6,10},{8,4},{10,6},{12,0},{14,2},{1,13},{3,15... | collective-permute-start | bytes 196616 | tf_op jit(solution)/shard_map/ppermute | solution.py:150
  6.6 6.1 %collective-permute-start.4 = (bf16[8,32,128]{2,1,0:T(8,128)(2,1)}, bf16[8,32,128]{2,1,0:T(8,128)(2,1)S(1)}, u32[]{:S(2)}, u32[]{:S(2)}) collective-permute-start(bf16[8,32,128]{2,1,0:T(8,128)(2,1)} %refs_6_.1), channel_id=1, source_target_pairs={{0,8},{2,10},{4,12},{6,14},{8,0},{10,2},{12,4},{14,6},{1,9},{3,11}... | collective-permute-start | bytes 196616 | tf_op jit(solution)/shard_map/ppermute | solution.py:150
  6.6 6.6 %collective-permute-start.6 = (bf16[8,32,128]{2,1,0:T(8,128)(2,1)}, bf16[8,32,128]{2,1,0:T(8,128)(2,1)S(1)}, u32[]{:S(2)}, u32[]{:S(2)}) collective-permute-start(bf16[8,32,128]{2,1,0:T(8,128)(2,1)} %refs_6_.1), channel_id=1, source_target_pairs={{0,4},{2,6},{4,0},{6,2},{8,12},{10,14},{12,8},{14,10},{1,5},{3,7},... | collective-permute-start | bytes 196616 | tf_op jit(solution)/shard_map/ppermute | solution.py:150
  9.7 5.0 %collective-permute-start.1 = (s32[8,128]{1,0:T(8,128)S(1)}, s32[8,128]{1,0:T(8,128)S(1)}, u32[]{:S(2)}, u32[]{:S(2)}) collective-permute-start(s32[8,128]{1,0:T(8,128)S(1)} %get-tuple-element.11), channel_id=1, source_target_pairs={{0,1},{1,0},{2,3},{3,2},{4,5},{5,4},{6,7},{7,6},{8,9},{9,8},{10,11... | collective-permute-start | bytes 12296 | tf_op jit(solution)/shard_map/ppermute | solution.py:175
  9.8 8.3 %collective-permute-start.3 = (bf16[8,32,128]{2,1,0:T(8,128)(2,1)S(1)}, bf16[8,32,128]{2,1,0:T(8,128)(2,1)S(1)}, u32[]{:S(2)}, u32[]{:S(2)}) collective-permute-start(bf16[8,32,128]{2,1,0:T(8,128)(2,1)S(1)} %collective-permute-done.2.refs_3_), channel_id=1, source_target_pairs={{0,2},{2,0},{4,6},{6,4},{8,10},{10,8},{12,14},{14,12},{1,3},{3,1},... | collective-permute-start | bytes 196616 | tf_op jit(solution)/shard_map/ppermute | solution.py:150
  12.7 5.4 %collective-permute-start.5 = (bf16[8,32,128]{2,1,0:T(8,128)(2,1)S(1)}, bf16[8,32,128]{2,1,0:T(8,128)(2,1)S(1)}, u32[]{:S(2)}, u32[]{:S(2)}) collective-permute-start(bf16[8,32,128]{2,1,0:T(8,128)(2,1)S(1)} %collective-permute-done.4.refs_4_), channel_id=1, source_target_pairs={{0,2},{2,0},{4,6},{6,4},{8,10},{10,8},{12,14},{14,12},{1,3},{3,1},... | collective-permute-start | bytes 196616 | tf_op jit(solution)/shard_map/ppermute | solution.py:150
  13.2 4.9 %collective-permute-start.7 = (bf16[8,32,128]{2,1,0:T(8,128)(2,1)S(1)}, bf16[8,32,128]{2,1,0:T(8,128)(2,1)S(1)}, u32[]{:S(2)}, u32[]{:S(2)}) collective-permute-start(bf16[8,32,128]{2,1,0:T(8,128)(2,1)S(1)} %collective-permute-done.6.refs_5_), channel_id=1, source_target_pairs={{0,2},{2,0},{4,6},{6,4},{8,10},{10,8},{12,14},{14,12},{1,3},{3,1},... | collective-permute-start | bytes 196616 | tf_op jit(solution)/shard_map/ppermute | solution.py:150

commit v9 on v7

--- a/solution.py
+++ b/solution.py
@@ -57,7 +57,7 @@
     n = len(distances)
     meta_hbm, pieces, passage_refs, refs = refs[:2], refs[2 : 2 + n], refs[2 + n : 4 + n], refs[4 + n :]
     earlier_ref = None if first else refs[0]
-    out_ref, query_ref, best_ref, meta_ref, work_ref, meta_sems, piece_sems = refs[-7:]
+    out_ref, query_ref, best_ref, wide_ref, meta_ref, work_ref, meta_sems, piece_sems = refs[-8:]
     q_tok, width = query_ref.shape[2:]
     tok_slots = passage_refs[0].shape[1]
     per_source = best_ref.shape[0]
@@ -130,9 +130,26 @@
     if first:
         out_ref[...] = score[:, :cap]
         return
-    for scores, at in ((earlier_ref[...], (*range(0, shards, 2), 1)), (score[:, :cap], distances)):
+    parts = ((earlier_ref[...], (*range(0, shards, 2), 1)), (score[:, :cap], distances))
+    if out_ref.shape[0] == cap:
+        wide_ref[...] = jnp.zeros_like(wide_ref)
+        for scores, at in parts:
+            for i, d in enumerate(at):
+                wide_ref[pl.ds((jnp.bitwise_xor(me, d) * shards + me) * 2, 2), :cap] = scores[2 * i : 2 * i + 2]
+        out_ref[...] = wide_ref[...].T[:cap]
+        return
+    for scores, at in parts:
         for i, d in enumerate(at):
             out_ref[pl.ds((shards - 1 - jnp.bitwise_xor(me, d)) * 2, 2), :] = scores[2 * i : 2 * i + 2]
+
+
+def pick_kernel(sum_ref, out_ref, wide_ref):
+    sources = out_ref.shape[1]
+    wide_ref[...] = jnp.zeros_like(wide_ref)
+    wide_ref[: sum_ref.shape[0], :] = sum_ref[...]
+    wide_ref[...] = wide_ref[...].T
+    start = pl.multiple_of(lax.axis_index("shard") * sources, 8)
+    out_ref[0] = wide_ref[pl.ds(start, sources), : out_ref.shape[2]]
 
 
 def order_kernel(back_ref, out_ref):
@@ -182,16 +199,20 @@
     theirs, _ = lax.optimization_barrier((theirs, pieces[1]))
     other = lax.ppermute(theirs, "sub", swap)
 
+    summed = shards * sources == 128
+    returns = (cap, 128) if summed else (sources, cap)
+
     def scored(distances, *earlier):
         n, first = len(distances), not earlier
         return pl.pallas_call(
             functools.partial(score_kernel, shards, distances, pack, cap, first),
-            out_shape=jax.ShapeDtypeStruct((2 * n if first else sources, cap), jnp.float32),
+            out_shape=jax.ShapeDtypeStruct((2 * n, cap) if first else returns, jnp.float32),
             in_specs=[anywhere] * (2 + n) + [vmem] * (2 + len(earlier)),
             out_specs=vmem,
             scratch_shapes=[
                 pltpu.VMEM((n, *queries.shape), queries.dtype),
                 pltpu.VMEM((per_source, 2 * n, 128), jnp.float32),
+                pltpu.VMEM((128, 128), jnp.float32),
                 pltpu.SMEM((2, shards, 128), jnp.int32),
                 pltpu.SMEM((n * per_source + 2 * GROUPS,), jnp.int32),
                 pltpu.SemaphoreType.DMA((2,)),
@@ -204,13 +225,17 @@
     pieces[0] = placed(pltpu.HBM, queries)[0]
     scores = scored((*range(0, shards, 2), 1))
     scores = scored(range(3, shards, 2), scores)
-    order = [list(reversed(range(shards)))]
-    returned = lax.all_to_all(scores, "shard", split_axis=0, concat_axis=0, axis_index_groups=order, tiled=True)
+    if summed:
+        returned = lax.psum(scores, "shard")
+    else:
+        order = [list(reversed(range(shards)))]
+        returned = lax.all_to_all(scores, "shard", split_axis=0, concat_axis=0, axis_index_groups=order, tiled=True)
     return pl.pallas_call(
-        order_kernel,
+        pick_kernel if summed else order_kernel,
         out_shape=jax.ShapeDtypeStruct((1, sources, cap), jnp.float32),
         in_specs=[vmem],
         out_specs=vmem,
+        scratch_shapes=[pltpu.VMEM((128, 128), jnp.float32)] * summed,
         compiler_params=params,
     )(returned)
 

time: 29.5 us -> 57 us (1.93)
  blocking collectives: 8.79 us -> 34.3 us
  Pallas kernels: 7.69 us -> 9.67 us
    psum x0 -> x1, blocking collectives: none -> 34.3 us  [on_device(): returned = lax.psum(scores, 'shard')]
    all_to_all x1 -> x0, blocking collectives: 8.79 us -> none  [on_device(): lax.all_to_all(scores, 'shard', split_axis=0, concat_axis=0, axis_index_g...]
    pallas_call x2, Pallas kernels: 4.8 us -> 6.68 us  [scored(): pl.pallas_call(functools.partial(score_kernel, shards, distances, pack, c...]
  transfers between devices with their start and end apart: 9 -> 9, of which waited for: 2 -> 1; matrix products, arithmetic and copies ran while one was open for 0% -> 0% of each run, Pallas kernels for 18% -> 11%
where the time goes in v9:
time: 57 us; the launch traced here: 56.4 us
  blocking collectives  34.3 us (60%)
  starting transfers between devices  9.81 us (17%)
  Pallas kernels  9.67 us (17%)
  waiting for transfers between devices  2.58 us (5%)
    psum x1, blocking collectives, on_device(): returned = lax.psum(scores, 'shard')  34.3 us
    ppermute x7, starting transfers between devices, swapped(): return lax.ppermute(piece, 'shard', [(i, i ^ d) for i in range(shards)])  9.28 us
    pallas_call x2, Pallas kernels, scored(): pl.pallas_call(functools.partial(score_kernel, shards, distances, pack, c...  6.68 us
    ppermute x7, waiting for transfers between devices, swapped(): return lax.ppermute(piece, 'shard', [(i, i ^ d) for i in range(shards)])  2.58 us
    pallas_call x1, Pallas kernels, on_device(): pl.pallas_call(functools.partial(pack_kernel, shards), out_shape=[row, ro...  2.29 us
  transfers between devices with their start and end apart: 9, of which 1 were waited for; matrix products, arithmetic and copies ran while one was open for 0% of the time, Pallas kernels for 11%

profile of v9, /device:TPU:0, one launch (start us, length us, event | category | flops | bytes accessed | tf_op | source)
XLA Modules:
  0.0 56.4 jit_solution(7215264459878100400)
XLA Ops:
  0.0 0.5 collective-permute-start.8
  0.5 2.5 %collective-permute-start = (bf16[8,32,128]{2,1,0:T(8,128)(2,1)}, bf16[8,32,128]{2,1,0:T(8,128)(2,1)S(1)}, u32[]{:S(2)}, u32[]{:S(2)}) collective-permute-start(bf16[8,32,128]{2,1,0:T(8,128)(2,1)} %refs_6_.1), channel_id=1, source_target_pairs={{0,2},{2,0},{4,6},{6,4},{8,10},{10,8},{12,14},{14,12},{1,3},{3,1},... | collective-permute-start | bytes 196616 | tf_op jit(solution)/shard_map/ppermute | solution.py:175
  3.0 3.6 %collective-permute-start.2 = (bf16[8,32,128]{2,1,0:T(8,128)(2,1)}, bf16[8,32,128]{2,1,0:T(8,128)(2,1)S(1)}, u32[]{:S(2)}, u32[]{:S(2)}) collective-permute-start(bf16[8,32,128]{2,1,0:T(8,128)(2,1)} %refs_6_.1), channel_id=1, source_target_pairs={{0,12},{2,14},{4,8},{6,10},{8,4},{10,6},{12,0},{14,2},{1,13},{3,15... | collective-permute-start | bytes 196616 | tf_op jit(solution)/shard_map/ppermute | solution.py:175
  6.6 0.0 collective-permute-start.4
  6.6 0.8 %collective-permute-start.6 = (bf16[8,32,128]{2,1,0:T(8,128)(2,1)}, bf16[8,32,128]{2,1,0:T(8,128)(2,1)S(1)}, u32[]{:S(2)}, u32[]{:S(2)}) collective-permute-start(bf16[8,32,128]{2,1,0:T(8,128)(2,1)} %refs_6_.1), channel_id=1, source_target_pairs={{0,4},{2,6},{4,0},{6,2},{8,12},{10,14},{12,8},{14,10},{1,5},{3,7},... | collective-permute-start | bytes 196616 | tf_op jit(solution)/shard_map/ppermute | solution.py:175
  7.4 2.3 %shard_map.64 = (s32[8,128]{1,0:T(8,128)S(1)}, s32[8,128]{1,0:T(8,128)S(1)}, bf16[128,128,128]{2,1,0:T(8,128)(2,1)S(1)}) custom-call(s32[16,24]{1,0:T(8,128)} %bitcast.3, s32[16,24]{1,0:T(8,128)} %bitcast.4, s32[16]{0:T(128)} %bitcast.5, s32[128]{0:T(128)} %length_hbm.1, bf16[128,128,128]{2,1,0:T(8,128)(2,1)} %own_hbm.1), custom_call_target="tpu_custom_call" | custom-call | tf_op jit(solution)/shard_map/pallas_call | solution.py:182
  9.7 0.0 collective-permute-done.refs_2_
  9.7 0.1 collective-permute-start.1
  9.7 0.0 collective-permute-done.2.refs_3_
  9.8 0.4 collective-permute-start.3
  10.1 2.6 %collective-permute-done.4.refs_4_ = bf16[8,32,128]{2,1,0:T(8,128)(2,1)S(1)} collective-permute-done((bf16[8,32,128]{2,1,0:T(8,128)(2,1)}, bf16[8,32,128]{2,1,0:T(8,128)(2,1)S(1)}, u32[]{:S(2)}, u32[]{:S(2)}) %collective-permute-start.4) | collective-permute-done | bytes 65568 | tf_op jit(solution)/shard_map/ppermute | solution.py:175
  12.7 0.5 collective-permute-start.5
  13.2 0.0 collective-permute-done.6.refs_5_
  13.2 1.5 %collective-permute-start.7 = (bf16[8,32,128]{2,1,0:T(8,128)(2,1)S(1)}, bf16[8,32,128]{2,1,0:T(8,128)(2,1)S(1)}, u32[]{:S(2)}, u32[]{:S(2)}) collective-permute-start(bf16[8,32,128]{2,1,0:T(8,128)(2,1)S(1)} %collective-permute-done.6.refs_5_), channel_id=1, source_target_pairs={{0,2},{2,0},{4,6},{6,4},{8,10},{10,8},{12,14},{14,12},{1,3},{3,1},... | collective-permute-start | bytes 196616 | tf_op jit(solution)/shard_map/ppermute | solution.py:175
  14.7 0.0 collective-permute-done.1.refs_1_
  14.7 0.0 collective-permute-done.8.refs_8_.refs_6_
  14.7 3.8 %shard_map.65.refs_7_ = f32[10,24]{1,0:T(8,128)S(1)} custom-call(s32[8,128]{1,0:T(8,128)S(1)} %get-tuple-element.9.refs_0_, s32[8,128]{1,0:T(8,128)S(1)} %collective-permute-done.1.refs_1_, bf16[8,32,128]{2,1,0:T(8,128)(2,1)S(1)} %collective-permute-done.refs_2_, bf16[8,32,128]{2,1,0:T(8,128)(2,1)S(1)} %collective-permute-done.2.refs_3_, ...), custom_call_target="tpu_custom_call" | custom-call | flops 1000000000 | bytes 9000000 | tf_op jit(solution)/shard_map/pallas_call | solution.py:207
  18.5 0.0 collective-permute-done.3.refs_2_
  18.6 0.0 collective-permute-done.5.refs_3_
  18.6 0.0 collective-permute-done.7.refs_4_
  18.6 2.9 %shard_map.66 = f32[24,128]{1,0:T(8,128)S(1)} custom-call(s32[8,128]{1,0:T(8,128)S(1)} %get-tuple-element.9.refs_0_, s32[8,128]{1,0:T(8,128)S(1)} %collective-permute-done.1.refs_1_, bf16[8,32,128]{2,1,0:T(8,128)(2,1)S(1)} %collective-permute-done.3.refs_2_, bf16[8,32,128]{2,1,0:T(8,128)(2,1)S(1)} %collective-permute-done.5.refs_3_, ...), custom_call_target="tpu_custom_call" | custom-call | flops 1000000000 | bytes 9000000 | tf_op jit(solution)/shard_map/pallas_call | solution.py:207
  21.4 34.3 %psum.7.sum_ref = f32[24,128]{1,0:T(8,128)S(1)} all-reduce(f32[24,128]{1,0:T(8,128)S(1)} %shard_map.66), channel_id=1, replica_groups=mesh['groups'=2,'shard'=8,'sub'=2] {'shard'}, use_global_device_ids=true, to_apply=%region_0.0 | all-reduce | flops 3072 | bytes 24576 | tf_op jit(solution)/shard_map/psum | solution.py:229
  55.7 0.7 %shard_map.67 = f32[1,16,24]{2,1,0:T(8,128)} custom-call(f32[24,128]{1,0:T(8,128)S(1)} %psum.7.sum_ref), custom_call_target="tpu_custom_call" | custom-call | tf_op jit(solution)/shard_map/pallas_call | solution.py:233
Async XLA Ops:
  0.0 14.7 %collective-permute-start.8 = (bf16[128,128,128]{2,1,0:T(8,128)(2,1)}, bf16[128,128,128]{2,1,0:T(8,128)(2,1)S(1)}, u32[]{:S(2)}, u32[]{:S(2)}) collective-permute-start(bf16[128,128,128]{2,1,0:T(8,128)(2,1)} %own_hbm.1), channel_id=1, source_target_pairs={{0,1},{1,0},{2,3},{3,2},{4,5},{5,4},{6,7},{7,6},{8,9},{9,8},{10,11... | collective-permute-start | bytes 12582920 | tf_op jit(solution)/shard_map/ppermute | solution.py:180
  0.5 9.2 %collective-permute-start = (bf16[8,32,128]{2,1,0:T(8,128)(2,1)}, bf16[8,32,128]{2,1,0:T(8,128)(2,1)S(1)}, u32[]{:S(2)}, u32[]{:S(2)}) collective-permute-start(bf16[8,32,128]{2,1,0:T(8,128)(2,1)} %refs_6_.1), channel_id=1, source_target_pairs={{0,2},{2,0},{4,6},{6,4},{8,10},{10,8},{12,14},{14,12},{1,3},{3,1},... | collective-permute-start | bytes 196616 | tf_op jit(solution)/shard_map/ppermute | solution.py:175
  3.0 6.8 %collective-permute-start.2 = (bf16[8,32,128]{2,1,0:T(8,128)(2,1)}, bf16[8,32,128]{2,1,0:T(8,128)(2,1)S(1)}, u32[]{:S(2)}, u32[]{:S(2)}) collective-permute-start(bf16[8,32,128]{2,1,0:T(8,128)(2,1)} %refs_6_.1), channel_id=1, source_target_pairs={{0,12},{2,14},{4,8},{6,10},{8,4},{10,6},{12,0},{14,2},{1,13},{3,15... | collective-permute-start | bytes 196616 | tf_op jit(solution)/shard_map/ppermute | solution.py:175
  6.6 6.1 %collective-permute-start.4 = (bf16[8,32,128]{2,1,0:T(8,128)(2,1)}, bf16[8,32,128]{2,1,0:T(8,128)(2,1)S(1)}, u32[]{:S(2)}, u32[]{:S(2)}) collective-permute-start(bf16[8,32,128]{2,1,0:T(8,128)(2,1)} %refs_6_.1), channel_id=1, source_target_pairs={{0,8},{2,10},{4,12},{6,14},{8,0},{10,2},{12,4},{14,6},{1,9},{3,11}... | collective-permute-start | bytes 196616 | tf_op jit(solution)/shard_map/ppermute | solution.py:175
  6.6 6.6 %collective-permute-start.6 = (bf16[8,32,128]{2,1,0:T(8,128)(2,1)}, bf16[8,32,128]{2,1,0:T(8,128)(2,1)S(1)}, u32[]{:S(2)}, u32[]{:S(2)}) collective-permute-start(bf16[8,32,128]{2,1,0:T(8,128)(2,1)} %refs_6_.1), channel_id=1, source_target_pairs={{0,4},{2,6},{4,0},{6,2},{8,12},{10,14},{12,8},{14,10},{1,5},{3,7},... | collective-permute-start | bytes 196616 | tf_op jit(solution)/shard_map/ppermute | solution.py:175
  9.7 5.0 %collective-permute-start.1 = (s32[8,128]{1,0:T(8,128)S(1)}, s32[8,128]{1,0:T(8,128)S(1)}, u32[]{:S(2)}, u32[]{:S(2)}) collective-permute-start(s32[8,128]{1,0:T(8,128)S(1)} %get-tuple-element.11), channel_id=1, source_target_pairs={{0,1},{1,0},{2,3},{3,2},{4,5},{5,4},{6,7},{7,6},{8,9},{9,8},{10,11... | collective-permute-start | bytes 12296 | tf_op jit(solution)/shard_map/ppermute | solution.py:200
  9.8 8.8 %collective-permute-start.3 = (bf16[8,32,128]{2,1,0:T(8,128)(2,1)S(1)}, bf16[8,32,128]{2,1,0:T(8,128)(2,1)S(1)}, u32[]{:S(2)}, u32[]{:S(2)}) collective-permute-start(bf16[8,32,128]{2,1,0:T(8,128)(2,1)S(1)} %collective-permute-done.2.refs_3_), channel_id=1, source_target_pairs={{0,2},{2,0},{4,6},{6,4},{8,10},{10,8},{12,14},{14,12},{1,3},{3,1},... | collective-permute-start | bytes 196616 | tf_op jit(solution)/shard_map/ppermute | solution.py:175
  12.7 5.9 %collective-permute-start.5 = (bf16[8,32,128]{2,1,0:T(8,128)(2,1)S(1)}, bf16[8,32,128]{2,1,0:T(8,128)(2,1)S(1)}, u32[]{:S(2)}, u32[]{:S(2)}) collective-permute-start(bf16[8,32,128]{2,1,0:T(8,128)(2,1)S(1)} %collective-permute-done.4.refs_4_), channel_id=1, source_target_pairs={{0,2},{2,0},{4,6},{6,4},{8,10},{10,8},{12,14},{14,12},{1,3},{3,1},... | collective-permute-start | bytes 196616 | tf_op jit(solution)/shard_map/ppermute | solution.py:175
  13.2 5.4 %collective-permute-start.7 = (bf16[8,32,128]{2,1,0:T(8,128)(2,1)S(1)}, bf16[8,32,128]{2,1,0:T(8,128)(2,1)S(1)}, u32[]{:S(2)}, u32[]{:S(2)}) collective-permute-start(bf16[8,32,128]{2,1,0:T(8,128)(2,1)S(1)} %collective-permute-done.6.refs_5_), channel_id=1, source_target_pairs={{0,2},{2,0},{4,6},{6,4},{8,10},{10,8},{12,14},{14,12},{1,3},{3,1},... | collective-permute-start | bytes 196616 | tf_op jit(solution)/shard_map/ppermute | solution.py:175

commit v10 on v7

--- a/solution.py
+++ b/solution.py
@@ -14,13 +14,19 @@
 
 
 def pack_kernel(
-    shards, query_hbm, passage_hbm, count_hbm, length_hbm, own_hbm,
-    mine_ref, theirs_ref, own_ref, query_ref, passage_ref, count_ref, length_ref, sems, own_sems,
+    shards, query_hbm, passage_hbm, count_hbm, length_hbm, tokens_hbm, own_hbm,
+    mine_ref, theirs_ref, tokens_ref, own_ref, query_ref, passage_ref, count_ref, length_ref, sems, own_sems,
 ):
     copies = [
         pltpu.make_async_copy(src, dst, sems.at[i])
         for i, (src, dst) in enumerate(
-            ((query_hbm, query_ref), (passage_hbm, passage_ref), (count_hbm, count_ref), (length_hbm, length_ref))
+            (
+                (query_hbm, query_ref),
+                (passage_hbm, passage_ref),
+                (count_hbm, count_ref),
+                (length_hbm, length_ref),
+                (tokens_hbm, tokens_ref),
+            )
         )
     ]
     size = own_ref.shape[0] // CHUNKS
@@ -55,7 +61,8 @@
 
 def score_kernel(shards, distances, pack, cap, first, *refs):
     n = len(distances)
-    meta_hbm, pieces, passage_refs, refs = refs[:2], refs[2 : 2 + n], refs[2 + n : 4 + n], refs[4 + n :]
+    p = n if first else n - 1
+    meta_hbm, pieces, passage_refs, refs = refs[:2], refs[2 : 2 + p], refs[2 + p : 4 + p], refs[4 + p :]
     earlier_ref = None if first else refs[0]
     out_ref, query_ref, best_ref, meta_ref, work_ref, meta_sems, piece_sems = refs[-7:]
     q_tok, width = query_ref.shape[2:]
@@ -65,11 +72,14 @@
     q_bits = q_tok.bit_length() - 1
     me, core = lax.axis_index("shard"), lax.axis_index("sub")
     copies = [pltpu.make_async_copy(meta_hbm[i], meta_ref.at[i], meta_sems.at[i]) for i in range(2)]
-    copies += [pltpu.make_async_copy(piece, query_ref.at[i], piece_sems.at[i]) for i, piece in enumerate(reversed(pieces))]
+    for i, piece in enumerate(reversed(pieces)):
+        at = query_ref.at[i] if first else query_ref.at[pl.ds(0, 2)] if i == 0 else query_ref.at[i + 1]
+        copies.append(pltpu.make_async_copy(piece, at, piece_sems.at[i]))
     for copy in copies:
         copy.start()
     best_ref[...] = jnp.zeros_like(best_ref)
-    token = lax.broadcasted_iota(jnp.int32, (tok_slots, lanes), 0)
+    token = lax.broadcasted_iota(jnp.int32, (tok_slots, 2 * q_tok), 0)
+    left = lax.broadcasted_iota(jnp.int32, (1, 2 * q_tok), 1) < q_tok
     place = lax.shift_right_logical(lax.broadcasted_iota(jnp.int32, (1, lanes), 1), q_bits)
     blank = jnp.zeros((q_tok, width), query_ref.dtype)
     for copy in copies:
@@ -80,8 +90,8 @@
 
         def shard_of(i):
             if first:
-                return jnp.bitwise_xor(me, jnp.where(i == n - 1, 1, i * 2))
-            return jnp.bitwise_xor(me, i * 2 + distances[0])
+                return jnp.bitwise_xor(me, jnp.where(i == 1, 1, i * 2))
+            return jnp.bitwise_xor(me, jnp.where(i == 0, 2, i * 2 + 1))
 
         def list_source(i, total):
             live = meta_ref[which, shard_of(i), COUNT]
@@ -98,18 +108,24 @@
                 work = work_ref[step * GROUPS + j]
                 i, g = lax.shift_right_logical(work, SHIFT), jnp.bitwise_and(work, (1 << SHIFT) - 1)
                 shard = shard_of(i)
-                rows, cols, limit = [], [], jnp.zeros((1, lanes), jnp.int32)
-                for a in range(pack):
-                    slot = g * pack + a
-                    query, passage = meta_ref[which, shard, QUERY + slot], meta_ref[which, shard, PASSAGE + slot]
-                    rows.append(jnp.concatenate([blank] * a + [query_ref[i, query]] + [blank] * (pack - 1 - a), axis=1))
-                    cols.append(passages[passage])
-                    limit = jnp.where(place == a, meta_ref[which, shard, LENGTH + slot], limit)
-                sims = lax.dot_general(
-                    jnp.concatenate(cols, axis=1), jnp.concatenate(rows, axis=0),
-                    (((1,), (1,)), ((), ())), preferred_element_type=jnp.float32,
-                )
-                best = jnp.max(jnp.where(token < limit, sims, -1e30), axis=0, keepdims=True)
+                best = []
+                for a in range(0, pack, 2):
+                    slots = [g * pack + a, g * pack + a + 1]
+                    if cap % pack:
+                        slots = [jnp.minimum(slot, cap - 1) for slot in slots]
+                    query = [query_ref[i, meta_ref[which, shard, QUERY + slot]] for slot in slots]
+                    passage = [meta_ref[which, shard, PASSAGE + slot] for slot in slots]
+                    limit = [meta_ref[which, shard, LENGTH + slot] for slot in slots]
+                    sims = lax.dot_general(
+                        jnp.concatenate([passages[p] for p in passage], axis=1),
+                        jnp.concatenate(
+                            [jnp.concatenate([query[0], blank], axis=1), jnp.concatenate([blank, query[1]], axis=1)], axis=0
+                        ),
+                        (((1,), (1,)), ((), ())), preferred_element_type=jnp.float32,
+                    )
+                    live = token < jnp.where(left, limit[0], limit[1])
+                    best.append(jnp.max(jnp.where(live, sims, -1e30), axis=0, keepdims=True))
+                best = jnp.concatenate(best, axis=1)
                 best = jnp.where(place + g * pack < meta_ref[which, shard, COUNT], best, 0.0)
                 best_ref[g, pl.ds(i * 2 + owner, 1), :] = best
             return carry
@@ -130,9 +146,14 @@
     if first:
         out_ref[...] = score[:, :cap]
         return
-    for scores, at in ((earlier_ref[...], (*range(0, shards, 2), 1)), (score[:, :cap], distances)):
+    for scores, at in ((earlier_ref[...], (0, 1, *range(4, shards, 2))), (score[:, :cap], distances)):
         for i, d in enumerate(at):
             out_ref[pl.ds((shards - 1 - jnp.bitwise_xor(me, d)) * 2, 2), :] = scores[2 * i : 2 * i + 2]
+
+
+def pair_kernel(one_ref, other_ref, out_ref):
+    out_ref[0] = one_ref[...]
+    out_ref[1] = other_ref[...]
 
 
 def order_kernel(back_ref, out_ref):
@@ -157,37 +178,46 @@
     def swapped(piece, d):
         return lax.ppermute(piece, "shard", [(i, i ^ d) for i in range(shards)])
 
-    pieces = [queries] + [None] * (shards - 1)
-    for d in reversed(range(2, shards, 2)):
+    pieces = [queries, swapped(queries, 1)] + [None] * (shards - 2)
+    for d in range(4, shards, 2):
         pieces[d] = swapped(queries, d)
     other_passages = lax.ppermute(passages, "sub", swap)
 
-    mine, theirs, own_passages = pl.pallas_call(
+    mine, theirs, own_queries, own_passages = pl.pallas_call(
         functools.partial(pack_kernel, shards),
-        out_shape=[row, row, jax.ShapeDtypeStruct(passages.shape, passages.dtype)],
-        in_specs=[hbm] * 5,
-        out_specs=[vmem] * 3,
+        out_shape=[row, row, *(jax.ShapeDtypeStruct(x.shape, x.dtype) for x in (queries, passages))],
+        in_specs=[hbm] * 6,
+        out_specs=[vmem] * 4,
         scratch_shapes=[
             pltpu.VMEM((sources, cap), jnp.int32),
             pltpu.VMEM((sources, cap), jnp.int32),
             pltpu.VMEM((sources,), jnp.int32),
             pltpu.VMEM(passage_len.shape, jnp.int32),
-            pltpu.SemaphoreType.DMA((4,)),
+            pltpu.SemaphoreType.DMA((5,)),
             pltpu.SemaphoreType.DMA((CHUNKS,)),
         ],
         compiler_params=params,
-    )(*placed(pltpu.HBM, slot_query.reshape(sources, cap), slot_passage.reshape(sources, cap), slot_count.reshape(sources), passage_len, passages))
-    for d in range(1, shards, 2):
-        pieces[d] = swapped(pieces[d - 1], 1)
+    )(*placed(pltpu.HBM, slot_query.reshape(sources, cap), slot_passage.reshape(sources, cap), slot_count.reshape(sources), passage_len, queries, passages))
+    both = pl.pallas_call(
+        pair_kernel,
+        out_shape=jax.ShapeDtypeStruct((2, *queries.shape), queries.dtype),
+        in_specs=[vmem] * 2,
+        out_specs=vmem,
+        compiler_params=params,
+    )(own_queries, pieces[1])
+    both = swapped(both, 2)
+    for d in range(5, shards, 2):
+        pieces[d] = swapped(pieces[d - 1], 1) if d == shards - 1 else swapped(pieces[1], d - 1)
     theirs, _ = lax.optimization_barrier((theirs, pieces[1]))
     other = lax.ppermute(theirs, "sub", swap)
 
     def scored(distances, *earlier):
         n, first = len(distances), not earlier
+        parts = [pieces[d] for d in reversed(distances)] if first else [*(pieces[d] for d in reversed(distances[2:])), both]
         return pl.pallas_call(
             functools.partial(score_kernel, shards, distances, pack, cap, first),
             out_shape=jax.ShapeDtypeStruct((2 * n if first else sources, cap), jnp.float32),
-            in_specs=[anywhere] * (2 + n) + [vmem] * (2 + len(earlier)),
+            in_specs=[anywhere] * (2 + len(parts)) + [vmem] * (2 + len(earlier)),
             out_specs=vmem,
             scratch_shapes=[
                 pltpu.VMEM((n, *queries.shape), queries.dtype),
@@ -199,11 +229,11 @@
             ],
             compiler_params=params,
             cost_estimate=pl.CostEstimate(flops=1_000_000_000, bytes_accessed=9_000_000, transcendentals=0),
-        )(mine, other, *(pieces[d] for d in reversed(distances)), *placed(pltpu.VMEM, own_passages, other_passages), *earlier)
-
-    pieces[0] = placed(pltpu.HBM, queries)[0]
-    scores = scored((*range(0, shards, 2), 1))
-    scores = scored(range(3, shards, 2), scores)
+        )(mine, other, *parts, *placed(pltpu.VMEM, own_passages, other_passages), *earlier)
+
+    pieces[0] = own_queries
+    scores = scored((0, 1, *range(4, shards, 2)))
+    scores = scored((2, *range(3, shards, 2)), scores)
     order = [list(reversed(range(shards)))]
     returned = lax.all_to_all(scores, "shard", split_axis=0, concat_axis=0, axis_index_groups=order, tiled=True)
     return pl.pallas_call(

time: 29.5 us -> 29.5 us (level); the launches traced: 29.2 us -> 29.8 us
  blocking collectives: 8.79 us -> 10.5 us
  waiting for transfers between devices: 2.82 us -> 1.73 us
  Pallas kernels: 7.69 us -> 7.35 us
    all_to_all x1, blocking collectives: 8.79 us -> 10.5 us  [on_device(): lax.all_to_all(scores, 'shard', split_axis=0, concat_axis=0, axis_index_g...]
    ppermute x7 -> x6, waiting for transfers between devices: 2.81 us -> 1.72 us  [swapped(): return lax.ppermute(piece, 'shard', [(i, i ^ d) for i in range(shards)])]
    pallas_call x2, Pallas kernels: 4.8 us -> 4.41 us  [scored(): pl.pallas_call(functools.partial(score_kernel, shards, distances, pack, c...]
    ppermute x7 -> x6, starting transfers between devices: 9.28 us -> 9.65 us  [swapped(): return lax.ppermute(piece, 'shard', [(i, i ^ d) for i in range(shards)])]
  transfers between devices with their start and end apart: 9 -> 8, of which waited for: 2 -> 2; matrix products, arithmetic and copies ran while one was open for 0% -> 0% of each run, Pallas kernels for 18% -> 16%
where the time goes in v10:
time: 29.5 us; the launch traced here: 29.8 us
  blocking collectives  10.5 us (36%)
  starting transfers between devices  10.1 us (34%)
  Pallas kernels  7.35 us (25%)
  waiting for transfers between devices  1.73 us (6%)
    all_to_all x1, blocking collectives, on_device(): lax.all_to_all(scores, 'shard', split_axis=0, concat_axis=0, axis_index_g...  10.5 us
    ppermute x6, starting transfers between devices, swapped(): return lax.ppermute(piece, 'shard', [(i, i ^ d) for i in range(shards)])  9.65 us
    pallas_call x2, Pallas kernels, scored(): pl.pallas_call(functools.partial(score_kernel, shards, distances, pack, c...  4.41 us
    pallas_call x1, Pallas kernels, on_device(): pl.pallas_call(functools.partial(pack_kernel, shards), out_shape=[row, ro...  2.33 us
    ppermute x6, waiting for transfers between devices, swapped(): return lax.ppermute(piece, 'shard', [(i, i ^ d) for i in range(shards)])  1.72 us
    pallas_call x1, Pallas kernels, on_device(): pl.pallas_call(order_kernel, out_shape=jax.ShapeDtypeStruct((1, sources,...  0.6 us
  transfers between devices with their start and end apart: 8, of which 2 were waited for; matrix products, arithmetic and copies ran while one was open for 0% of the time, Pallas kernels for 16%

profile of v10, /device:TPU:0, one launch (start us, length us, event | category | flops | bytes accessed | tf_op | source)
XLA Modules:
  0.0 29.8 jit_solution(18110371986110956935)
XLA Ops:
  0.0 0.5 %collective-permute-start.6 = (bf16[128,128,128]{2,1,0:T(8,128)(2,1)}, bf16[128,128,128]{2,1,0:T(8,128)(2,1)S(1)}, u32[]{:S(2)}, u32[]{:S(2)}) collective-permute-start(bf16[128,128,128]{2,1,0:T(8,128)(2,1)} %own_hbm.1), channel_id=1, source_target_pairs={{0,1},{1,0},{2,3},{3,2},{4,5},{5,4},{6,7},{7,6},{8,9},{9,8},{10,11... | collective-permute-start | bytes 12582920 | tf_op jit(solution)/shard_map/ppermute | solution.py:184
  0.5 2.5 %collective-permute-start = (bf16[8,32,128]{2,1,0:T(8,128)(2,1)}, bf16[8,32,128]{2,1,0:T(8,128)(2,1)S(1)}, u32[]{:S(2)}, u32[]{:S(2)}) collective-permute-start(bf16[8,32,128]{2,1,0:T(8,128)(2,1)} %tokens_hbm.1), channel_id=1, source_target_pairs={{0,2},{2,0},{4,6},{6,4},{8,10},{10,8},{12,14},{14,12},{1,3},{3,1},... | collective-permute-start | bytes 196616 | tf_op jit(solution)/shard_map/ppermute | solution.py:179
  3.0 2.6 %collective-permute-start.7 = (bf16[8,32,128]{2,1,0:T(8,128)(2,1)}, bf16[8,32,128]{2,1,0:T(8,128)(2,1)S(1)}, u32[]{:S(2)}, u32[]{:S(2)}) collective-permute-start(bf16[8,32,128]{2,1,0:T(8,128)(2,1)} %tokens_hbm.1), channel_id=1, source_target_pairs={{0,8},{2,10},{4,12},{6,14},{8,0},{10,2},{12,4},{14,6},{1,9},{3,11}... | collective-permute-start | bytes 196616 | tf_op jit(solution)/shard_map/ppermute | solution.py:179
  5.6 1.3 %collective-permute-start.2 = (bf16[8,32,128]{2,1,0:T(8,128)(2,1)}, bf16[8,32,128]{2,1,0:T(8,128)(2,1)S(1)}, u32[]{:S(2)}, u32[]{:S(2)}) collective-permute-start(bf16[8,32,128]{2,1,0:T(8,128)(2,1)} %tokens_hbm.1), channel_id=1, source_target_pairs={{0,12},{2,14},{4,8},{6,10},{8,4},{10,6},{12,0},{14,2},{1,13},{3,15... | collective-permute-start | bytes 196616 | tf_op jit(solution)/shard_map/ppermute | solution.py:179
  6.9 2.3 %shard_map.64 = (s32[8,128]{1,0:T(8,128)S(1)}, s32[8,128]{1,0:T(8,128)S(1)}, bf16[8,32,128]{2,1,0:T(8,128)(2,1)S(1)}, bf16[128,128,128]{2,1,0:T(8,128)(2,1)S(1)}) custom-call(s32[16,24]{1,0:T(8,128)} %bitcast.7, s32[16,24]{1,0:T(8,128)} %bitcast.8, s32[16]{0:T(128)} %bitcast.9, s32[128]{0:T(128)} %length_hbm.1, bf16[8,32,128]{2,1,0:T(8,128)(2,1)} %tokens_hbm.1, ...), custom_call_target="tpu_custom_call" | custom-call | tf_op jit(solution)/shard_map/pallas_call | solution.py:186
  9.2 0.0 collective-permute-done.other_ref.refs_4_
  9.3 0.3 collective-permute-start.5
  9.6 0.0 collective-permute-start.1
  9.6 0.4 %collective-permute-done.7.refs_3_ = bf16[8,32,128]{2,1,0:T(8,128)(2,1)S(1)} collective-permute-done((bf16[8,32,128]{2,1,0:T(8,128)(2,1)}, bf16[8,32,128]{2,1,0:T(8,128)(2,1)S(1)}, u32[]{:S(2)}, u32[]{:S(2)}) %collective-permute-start.7) | collective-permute-done | bytes 65568 | tf_op jit(solution)/shard_map/ppermute | solution.py:179
  10.0 2.4 %collective-permute-start.4 = (bf16[8,32,128]{2,1,0:T(8,128)(2,1)S(1)}, bf16[8,32,128]{2,1,0:T(8,128)(2,1)S(1)}, u32[]{:S(2)}, u32[]{:S(2)}) collective-permute-start(bf16[8,32,128]{2,1,0:T(8,128)(2,1)S(1)} %collective-permute-done.other_ref.refs_4_), channel_id=1, source_target_pairs={{0,8},{2,10},{4,12},{6,14},{8,0},{10,2},{12,4},{14,6},{1,9},{3,11}... | collective-permute-start | bytes 196616 | tf_op jit(solution)/shard_map/ppermute | solution.py:179
  12.4 0.0 collective-permute-done.2.refs_2_
  12.4 0.5 %collective-permute-start.3 = (bf16[8,32,128]{2,1,0:T(8,128)(2,1)S(1)}, bf16[8,32,128]{2,1,0:T(8,128)(2,1)S(1)}, u32[]{:S(2)}, u32[]{:S(2)}) collective-permute-start(bf16[8,32,128]{2,1,0:T(8,128)(2,1)S(1)} %collective-permute-done.2.refs_2_), channel_id=1, source_target_pairs={{0,2},{2,0},{4,6},{6,4},{8,10},{10,8},{12,14},{14,12},{1,3},{3,1},... | collective-permute-start | bytes 196616 | tf_op jit(solution)/shard_map/ppermute | solution.py:179
  12.9 0.0 collective-permute-done.1.refs_1_
  12.9 0.0 collective-permute-done.6.refs_7_.refs_6_
  12.9 2.4 %shard_map.66.refs_7_ = f32[8,24]{1,0:T(8,128)S(1)} custom-call(s32[8,128]{1,0:T(8,128)S(1)} %get-tuple-element.10.refs_0_, s32[8,128]{1,0:T(8,128)S(1)} %collective-permute-done.1.refs_1_, bf16[8,32,128]{2,1,0:T(8,128)(2,1)S(1)} %collective-permute-done.2.refs_2_, bf16[8,32,128]{2,1,0:T(8,128)(2,1)S(1)} %collective-permute-done.7.refs_3_, ...), custom_call_target="tpu_custom_call" | custom-call | flops 1000000000 | bytes 9000000 | tf_op jit(solution)/shard_map/pallas_call | solution.py:217
  15.4 0.0 collective-permute-done.4.refs_3_
  15.4 1.3 %collective-permute-done.3.refs_2_ = bf16[8,32,128]{2,1,0:T(8,128)(2,1)S(1)} collective-permute-done((bf16[8,32,128]{2,1,0:T(8,128)(2,1)S(1)}, bf16[8,32,128]{2,1,0:T(8,128)(2,1)S(1)}, u32[]{:S(2)}, u32[]{:S(2)}) %collective-permute-start.3) | collective-permute-done | bytes 65568 | tf_op jit(solution)/shard_map/ppermute | solution.py:179
  16.7 0.0 collective-permute-done.5.refs_4_
  16.7 2.0 %shard_map.67 = f32[16,24]{1,0:T(8,128)S(1)} custom-call(s32[8,128]{1,0:T(8,128)S(1)} %get-tuple-element.10.refs_0_, s32[8,128]{1,0:T(8,128)S(1)} %collective-permute-done.1.refs_1_, bf16[8,32,128]{2,1,0:T(8,128)(2,1)S(1)} %collective-permute-done.3.refs_2_, bf16[8,32,128]{2,1,0:T(8,128)(2,1)S(1)} %collective-permute-done.4.refs_3_, ...), custom_call_target="tpu_custom_call" | custom-call | flops 1000000000 | bytes 9000000 | tf_op jit(solution)/shard_map/pallas_call | solution.py:217
  18.6 10.5 %all_to_all.11 = f32[8,2,24]{2,1,0:T(2,128)S(1)} all-to-all(f32[8,2,24]{2,1,0:T(2,128)S(1)} %bitcast.6), channel_id=1, replica_groups={{14,12,10,8,6,4,2,0},{15,13,11,9,7,5,3,1},{30,28,26,24,22,20,18,16},{31..., dimensions={0} | all-to-all | bytes 3072 | tf_op jit(solution)/shard_map/all_to_all | solution.py:238
  29.2 0.6 %shard_map.68 = f32[1,16,24]{2,1,0:T(8,128)} custom-call(f32[16,24]{1,0:T(8,128)S(1)} %bitcast.5), custom_call_target="tpu_custom_call" | custom-call | tf_op jit(solution)/shard_map/pallas_call | solution.py:239
  (1 shorter events, 0.0 us)
Async XLA Ops:
  0.0 12.9 %collective-permute-start.6 = (bf16[128,128,128]{2,1,0:T(8,128)(2,1)}, bf16[128,128,128]{2,1,0:T(8,128)(2,1)S(1)}, u32[]{:S(2)}, u32[]{:S(2)}) collective-permute-start(bf16[128,128,128]{2,1,0:T(8,128)(2,1)} %own_hbm.1), channel_id=1, source_target_pairs={{0,1},{1,0},{2,3},{3,2},{4,5},{5,4},{6,7},{7,6},{8,9},{9,8},{10,11... | collective-permute-start | bytes 12582920 | tf_op jit(solution)/shard_map/ppermute | solution.py:184
  0.5 8.8 %collective-permute-start = (bf16[8,32,128]{2,1,0:T(8,128)(2,1)}, bf16[8,32,128]{2,1,0:T(8,128)(2,1)S(1)}, u32[]{:S(2)}, u32[]{:S(2)}) collective-permute-start(bf16[8,32,128]{2,1,0:T(8,128)(2,1)} %tokens_hbm.1), channel_id=1, source_target_pairs={{0,2},{2,0},{4,6},{6,4},{8,10},{10,8},{12,14},{14,12},{1,3},{3,1},... | collective-permute-start | bytes 196616 | tf_op jit(solution)/shard_map/ppermute | solution.py:179
  3.0 7.0 %collective-permute-start.7 = (bf16[8,32,128]{2,1,0:T(8,128)(2,1)}, bf16[8,32,128]{2,1,0:T(8,128)(2,1)S(1)}, u32[]{:S(2)}, u32[]{:S(2)}) collective-permute-start(bf16[8,32,128]{2,1,0:T(8,128)(2,1)} %tokens_hbm.1), channel_id=1, source_target_pairs={{0,8},{2,10},{4,12},{6,14},{8,0},{10,2},{12,4},{14,6},{1,9},{3,11}... | collective-permute-start | bytes 196616 | tf_op jit(solution)/shard_map/ppermute | solution.py:179
  5.6 6.8 %collective-permute-start.2 = (bf16[8,32,128]{2,1,0:T(8,128)(2,1)}, bf16[8,32,128]{2,1,0:T(8,128)(2,1)S(1)}, u32[]{:S(2)}, u32[]{:S(2)}) collective-permute-start(bf16[8,32,128]{2,1,0:T(8,128)(2,1)} %tokens_hbm.1), channel_id=1, source_target_pairs={{0,12},{2,14},{4,8},{6,10},{8,4},{10,6},{12,0},{14,2},{1,13},{3,15... | collective-permute-start | bytes 196616 | tf_op jit(solution)/shard_map/ppermute | solution.py:179
  9.3 7.4 %collective-permute-start.5 = (bf16[2,8,32,128]{3,2,1,0:T(8,128)(2,1)S(1)}, bf16[2,8,32,128]{3,2,1,0:T(8,128)(2,1)S(1)}, u32[]{:S(2)}, u32[]{:S(2)}) collective-permute-start(bf16[2,8,32,128]{3,2,1,0:T(8,128)(2,1)S(1)} %shard_map.65), channel_id=1, source_target_pairs={{0,4},{2,6},{4,0},{6,2},{8,12},{10,14},{12,8},{14,10},{1,5},{3,7},... | collective-permute-start | bytes 393224 | tf_op jit(solution)/shard_map/ppermute | solution.py:179
  9.6 3.3 %collective-permute-start.1 = (s32[8,128]{1,0:T(8,128)S(1)}, s32[8,128]{1,0:T(8,128)S(1)}, u32[]{:S(2)}, u32[]{:S(2)}) collective-permute-start(s32[8,128]{1,0:T(8,128)S(1)} %get-tuple-element.12), channel_id=1, source_target_pairs={{0,1},{1,0},{2,3},{3,2},{4,5},{5,4},{6,7},{7,6},{8,9},{9,8},{10,11... | collective-permute-start | bytes 12296 | tf_op jit(solution)/shard_map/ppermute | solution.py:212
  10.0 5.4 %collective-permute-start.4 = (bf16[8,32,128]{2,1,0:T(8,128)(2,1)S(1)}, bf16[8,32,128]{2,1,0:T(8,128)(2,1)S(1)}, u32[]{:S(2)}, u32[]{:S(2)}) collective-permute-start(bf16[8,32,128]{2,1,0:T(8,128)(2,1)S(1)} %collective-permute-done.other_ref.refs_4_), channel_id=1, source_target_pairs={{0,8},{2,10},{4,12},{6,14},{8,0},{10,2},{12,4},{14,6},{1,9},{3,11}... | collective-permute-start | bytes 196616 | tf_op jit(solution)/shard_map/ppermute | solution.py:179
  12.4 4.3 %collective-permute-start.3 = (bf16[8,32,128]{2,1,0:T(8,128)(2,1)S(1)}, bf16[8,32,128]{2,1,0:T(8,128)(2,1)S(1)}, u32[]{:S(2)}, u32[]{:S(2)}) collective-permute-start(bf16[8,32,128]{2,1,0:T(8,128)(2,1)S(1)} %collective-permute-done.2.refs_2_), channel_id=1, source_target_pairs={{0,2},{2,0},{4,6},{6,4},{8,10},{10,8},{12,14},{14,12},{1,3},{3,1},... | collective-permute-start | bytes 196616 | tf_op jit(solution)/shard_map/ppermute | solution.py:179

commit v11 on v10

--- a/solution.py
+++ b/solution.py
@@ -7,7 +7,7 @@
 from jax.experimental.pallas import tpu as pltpu
 from jax.sharding import PartitionSpec as P
 
-GROUPS = 8
+GROUPS = 4
 CHUNKS = 8
 SHIFT = 8
 QUERY, PASSAGE, LENGTH, COUNT = 0, 32, 64, 96
@@ -78,8 +78,7 @@
     for copy in copies:
         copy.start()
     best_ref[...] = jnp.zeros_like(best_ref)
-    token = lax.broadcasted_iota(jnp.int32, (tok_slots, 2 * q_tok), 0)
-    left = lax.broadcasted_iota(jnp.int32, (1, 2 * q_tok), 1) < q_tok
+    token = lax.broadcasted_iota(jnp.int32, (tok_slots, lanes), 0)
     place = lax.shift_right_logical(lax.broadcasted_iota(jnp.int32, (1, lanes), 1), q_bits)
     blank = jnp.zeros((q_tok, width), query_ref.dtype)
     for copy in copies:
@@ -108,24 +107,18 @@
                 work = work_ref[step * GROUPS + j]
                 i, g = lax.shift_right_logical(work, SHIFT), jnp.bitwise_and(work, (1 << SHIFT) - 1)
                 shard = shard_of(i)
-                best = []
-                for a in range(0, pack, 2):
-                    slots = [g * pack + a, g * pack + a + 1]
-                    if cap % pack:
-                        slots = [jnp.minimum(slot, cap - 1) for slot in slots]
-                    query = [query_ref[i, meta_ref[which, shard, QUERY + slot]] for slot in slots]
-                    passage = [meta_ref[which, shard, PASSAGE + slot] for slot in slots]
-                    limit = [meta_ref[which, shard, LENGTH + slot] for slot in slots]
-                    sims = lax.dot_general(
-                        jnp.concatenate([passages[p] for p in passage], axis=1),
-                        jnp.concatenate(
-                            [jnp.concatenate([query[0], blank], axis=1), jnp.concatenate([blank, query[1]], axis=1)], axis=0
-                        ),
-                        (((1,), (1,)), ((), ())), preferred_element_type=jnp.float32,
-                    )
-                    live = token < jnp.where(left, limit[0], limit[1])
-                    best.append(jnp.max(jnp.where(live, sims, -1e30), axis=0, keepdims=True))
-                best = jnp.concatenate(best, axis=1)
+                rows, cols, limit = [], [], jnp.zeros((1, lanes), jnp.int32)
+                for a in range(pack):
+                    slot = g * pack + a
+                    query, passage = meta_ref[which, shard, QUERY + slot], meta_ref[which, shard, PASSAGE + slot]
+                    rows.append(jnp.concatenate([blank] * a + [query_ref[i, query]] + [blank] * (pack - 1 - a), axis=1))
+                    cols.append(passages[passage])
+                    limit = jnp.where(place == a, meta_ref[which, shard, LENGTH + slot], limit)
+                sims = lax.dot_general(
+                    jnp.concatenate(cols, axis=1), jnp.concatenate(rows, axis=0),
+                    (((1,), (1,)), ((), ())), preferred_element_type=jnp.float32,
+                )
+                best = jnp.max(jnp.where(token < limit, sims, -1e30), axis=0, keepdims=True)
                 best = jnp.where(place + g * pack < meta_ref[which, shard, COUNT], best, 0.0)
                 best_ref[g, pl.ds(i * 2 + owner, 1), :] = best
             return carry
@@ -207,7 +200,7 @@
     )(own_queries, pieces[1])
     both = swapped(both, 2)
     for d in range(5, shards, 2):
-        pieces[d] = swapped(pieces[d - 1], 1) if d == shards - 1 else swapped(pieces[1], d - 1)
+        pieces[d] = swapped(pieces[d - 1], 1)
     theirs, _ = lax.optimization_barrier((theirs, pieces[1]))
     other = lax.ppermute(theirs, "sub", swap)
 

time: 29.5 us -> 29.5 us (level); the launches traced: 29.8 us -> 29.1 us
  starting transfers between devices: 10.1 us -> 8.1 us
  waiting for transfers between devices: 1.73 us -> 3.17 us
  blocking collectives: 10.5 us -> 10 us
  Pallas kernels: 7.35 us -> 7.69 us
    ppermute x6, starting transfers between devices: 9.65 us -> 7.64 us  [swapped(): return lax.ppermute(piece, 'shard', [(i, i ^ d) for i in range(shards)])]
    ppermute x6, waiting for transfers between devices: 1.72 us -> 3.16 us  [swapped(): return lax.ppermute(piece, 'shard', [(i, i ^ d) for i in range(shards)])]
    all_to_all x1, blocking collectives: 10.5 us -> 10 us  [on_device(): lax.all_to_all(scores, 'shard', split_axis=0, concat_axis=0, axis_index_g...]
    pallas_call x2, Pallas kernels: 4.41 us -> 4.75 us  [scored(): pl.pallas_call(functools.partial(score_kernel, shards, distances, pack, c...]
  transfers between devices with their start and end apart: 8 -> 8, of which waited for: 2 -> 3; matrix products, arithmetic and copies ran while one was open for 0% -> 0% of each run, Pallas kernels for 16% -> 17%
where the time goes in v11:
time: 29.5 us; the launch traced here: 29.1 us
  blocking collectives  10 us (34%)
  starting transfers between devices  8.1 us (27%)
  Pallas kernels  7.69 us (26%)
  waiting for transfers between devices  3.17 us (11%)
    all_to_all x1, blocking collectives, on_device(): lax.all_to_all(scores, 'shard', split_axis=0, concat_axis=0, axis_index_g...  10 us
    ppermute x6, starting transfers between devices, swapped(): return lax.ppermute(piece, 'shard', [(i, i ^ d) for i in range(shards)])  7.64 us
    pallas_call x2, Pallas kernels, scored(): pl.pallas_call(functools.partial(score_kernel, shards, distances, pack, c...  4.75 us
    ppermute x6, waiting for transfers between devices, swapped(): return lax.ppermute(piece, 'shard', [(i, i ^ d) for i in range(shards)])  3.16 us
    pallas_call x1, Pallas kernels, on_device(): pl.pallas_call(functools.partial(pack_kernel, shards), out_shape=[row, ro...  2.33 us
    pallas_call x1, Pallas kernels, on_device(): pl.pallas_call(order_kernel, out_shape=jax.ShapeDtypeStruct((1, sources,...  0.6 us
  transfers between devices with their start and end apart: 8, of which 3 were waited for; matrix products, arithmetic and copies ran while one was open for 0% of the time, Pallas kernels for 17%

profile of v11, /device:TPU:0, one launch (start us, length us, event | category | flops | bytes accessed | tf_op | source)
XLA Modules:
  0.0 29.1 jit_solution(1613800842638579831)
XLA Ops:
  0.0 0.5 %collective-permute-start.7 = (bf16[128,128,128]{2,1,0:T(8,128)(2,1)}, bf16[128,128,128]{2,1,0:T(8,128)(2,1)S(1)}, u32[]{:S(2)}, u32[]{:S(2)}) collective-permute-start(bf16[128,128,128]{2,1,0:T(8,128)(2,1)} %own_hbm.1), channel_id=1, source_target_pairs={{0,1},{1,0},{2,3},{3,2},{4,5},{5,4},{6,7},{7,6},{8,9},{9,8},{10,11... | collective-permute-start | bytes 12582920 | tf_op jit(solution)/shard_map/ppermute | solution.py:177
  0.5 2.5 %collective-permute-start = (bf16[8,32,128]{2,1,0:T(8,128)(2,1)}, bf16[8,32,128]{2,1,0:T(8,128)(2,1)S(1)}, u32[]{:S(2)}, u32[]{:S(2)}) collective-permute-start(bf16[8,32,128]{2,1,0:T(8,128)(2,1)} %tokens_hbm.1), channel_id=1, source_target_pairs={{0,2},{2,0},{4,6},{6,4},{8,10},{10,8},{12,14},{14,12},{1,3},{3,1},... | collective-permute-start | bytes 196616 | tf_op jit(solution)/shard_map/ppermute | solution.py:172
  3.0 2.6 %collective-permute-start.4 = (bf16[8,32,128]{2,1,0:T(8,128)(2,1)}, bf16[8,32,128]{2,1,0:T(8,128)(2,1)S(1)}, u32[]{:S(2)}, u32[]{:S(2)}) collective-permute-start(bf16[8,32,128]{2,1,0:T(8,128)(2,1)} %tokens_hbm.1), channel_id=1, source_target_pairs={{0,8},{2,10},{4,12},{6,14},{8,0},{10,2},{12,4},{14,6},{1,9},{3,11}... | collective-permute-start | bytes 196616 | tf_op jit(solution)/shard_map/ppermute | solution.py:172
  5.6 1.3 %collective-permute-start.2 = (bf16[8,32,128]{2,1,0:T(8,128)(2,1)}, bf16[8,32,128]{2,1,0:T(8,128)(2,1)S(1)}, u32[]{:S(2)}, u32[]{:S(2)}) collective-permute-start(bf16[8,32,128]{2,1,0:T(8,128)(2,1)} %tokens_hbm.1), channel_id=1, source_target_pairs={{0,12},{2,14},{4,8},{6,10},{8,4},{10,6},{12,0},{14,2},{1,13},{3,15... | collective-permute-start | bytes 196616 | tf_op jit(solution)/shard_map/ppermute | solution.py:172
  6.9 2.3 %shard_map.64 = (s32[8,128]{1,0:T(8,128)S(1)}, s32[8,128]{1,0:T(8,128)S(1)}, bf16[8,32,128]{2,1,0:T(8,128)(2,1)S(1)}, bf16[128,128,128]{2,1,0:T(8,128)(2,1)S(1)}) custom-call(s32[16,24]{1,0:T(8,128)} %bitcast.7, s32[16,24]{1,0:T(8,128)} %bitcast.8, s32[16]{0:T(128)} %bitcast.9, s32[128]{0:T(128)} %length_hbm.1, bf16[8,32,128]{2,1,0:T(8,128)(2,1)} %tokens_hbm.1, ...), custom_call_target="tpu_custom_call" | custom-call | tf_op jit(solution)/shard_map/pallas_call | solution.py:179
  9.2 0.0 collective-permute-done.other_ref.refs_4_
  9.3 0.3 %collective-permute-start.6 = (bf16[2,8,32,128]{3,2,1,0:T(8,128)(2,1)S(1)}, bf16[2,8,32,128]{3,2,1,0:T(8,128)(2,1)S(1)}, u32[]{:S(2)}, u32[]{:S(2)}) collective-permute-start(bf16[2,8,32,128]{3,2,1,0:T(8,128)(2,1)S(1)} %shard_map.65), channel_id=1, source_target_pairs={{0,4},{2,6},{4,0},{6,2},{8,12},{10,14},{12,8},{14,10},{1,5},{3,7},... | collective-permute-start | bytes 393224 | tf_op jit(solution)/shard_map/ppermute | solution.py:172
  9.6 0.0 collective-permute-start.1
  9.6 0.4 %collective-permute-done.4.refs_3_ = bf16[8,32,128]{2,1,0:T(8,128)(2,1)S(1)} collective-permute-done((bf16[8,32,128]{2,1,0:T(8,128)(2,1)}, bf16[8,32,128]{2,1,0:T(8,128)(2,1)S(1)}, u32[]{:S(2)}, u32[]{:S(2)}) %collective-permute-start.4) | collective-permute-done | bytes 65568 | tf_op jit(solution)/shard_map/ppermute | solution.py:172
  10.0 0.4 %collective-permute-start.5 = (bf16[8,32,128]{2,1,0:T(8,128)(2,1)S(1)}, bf16[8,32,128]{2,1,0:T(8,128)(2,1)S(1)}, u32[]{:S(2)}, u32[]{:S(2)}) collective-permute-start(bf16[8,32,128]{2,1,0:T(8,128)(2,1)S(1)} %collective-permute-done.4.refs_3_), channel_id=1, source_target_pairs={{0,2},{2,0},{4,6},{6,4},{8,10},{10,8},{12,14},{14,12},{1,3},{3,1},... | collective-permute-start | bytes 196616 | tf_op jit(solution)/shard_map/ppermute | solution.py:172
  10.4 1.5 %collective-permute-done.2.refs_2_ = bf16[8,32,128]{2,1,0:T(8,128)(2,1)S(1)} collective-permute-done((bf16[8,32,128]{2,1,0:T(8,128)(2,1)}, bf16[8,32,128]{2,1,0:T(8,128)(2,1)S(1)}, u32[]{:S(2)}, u32[]{:S(2)}) %collective-permute-start.2) | collective-permute-done | bytes 65568 | tf_op jit(solution)/shard_map/ppermute | solution.py:172
  11.9 0.5 %collective-permute-start.3 = (bf16[8,32,128]{2,1,0:T(8,128)(2,1)S(1)}, bf16[8,32,128]{2,1,0:T(8,128)(2,1)S(1)}, u32[]{:S(2)}, u32[]{:S(2)}) collective-permute-start(bf16[8,32,128]{2,1,0:T(8,128)(2,1)S(1)} %collective-permute-done.2.refs_2_), channel_id=1, source_target_pairs={{0,2},{2,0},{4,6},{6,4},{8,10},{10,8},{12,14},{14,12},{1,3},{3,1},... | collective-permute-start | bytes 196616 | tf_op jit(solution)/shard_map/ppermute | solution.py:172
  12.4 0.0 collective-permute-done.1.refs_1_
  12.4 0.0 collective-permute-done.7.refs_7_.refs_6_
  12.4 2.5 %shard_map.66.refs_7_ = f32[8,24]{1,0:T(8,128)S(1)} custom-call(s32[8,128]{1,0:T(8,128)S(1)} %get-tuple-element.10.refs_0_, s32[8,128]{1,0:T(8,128)S(1)} %collective-permute-done.1.refs_1_, bf16[8,32,128]{2,1,0:T(8,128)(2,1)S(1)} %collective-permute-done.2.refs_2_, bf16[8,32,128]{2,1,0:T(8,128)(2,1)S(1)} %collective-permute-done.4.refs_3_, ...), custom_call_target="tpu_custom_call" | custom-call | flops 1000000000 | bytes 9000000 | tf_op jit(solution)/shard_map/pallas_call | solution.py:210
  15.0 0.0 collective-permute-done.5.refs_3_
  15.0 1.2 %collective-permute-done.3.refs_2_ = bf16[8,32,128]{2,1,0:T(8,128)(2,1)S(1)} collective-permute-done((bf16[8,32,128]{2,1,0:T(8,128)(2,1)S(1)}, bf16[8,32,128]{2,1,0:T(8,128)(2,1)S(1)}, u32[]{:S(2)}, u32[]{:S(2)}) %collective-permute-start.3) | collective-permute-done | bytes 65568 | tf_op jit(solution)/shard_map/ppermute | solution.py:172
  16.2 0.0 collective-permute-done.6.refs_4_
  16.2 2.2 %shard_map.67 = f32[16,24]{1,0:T(8,128)S(1)} custom-call(s32[8,128]{1,0:T(8,128)S(1)} %get-tuple-element.10.refs_0_, s32[8,128]{1,0:T(8,128)S(1)} %collective-permute-done.1.refs_1_, bf16[8,32,128]{2,1,0:T(8,128)(2,1)S(1)} %collective-permute-done.3.refs_2_, bf16[8,32,128]{2,1,0:T(8,128)(2,1)S(1)} %collective-permute-done.5.refs_3_, ...), custom_call_target="tpu_custom_call" | custom-call | flops 1000000000 | bytes 9000000 | tf_op jit(solution)/shard_map/pallas_call | solution.py:210
  18.4 10.0 %all_to_all.11 = f32[8,2,24]{2,1,0:T(2,128)S(1)} all-to-all(f32[8,2,24]{2,1,0:T(2,128)S(1)} %bitcast.6), channel_id=1, replica_groups={{14,12,10,8,6,4,2,0},{15,13,11,9,7,5,3,1},{30,28,26,24,22,20,18,16},{31..., dimensions={0} | all-to-all | bytes 3072 | tf_op jit(solution)/shard_map/all_to_all | solution.py:231
  28.5 0.6 %shard_map.68 = f32[1,16,24]{2,1,0:T(8,128)} custom-call(f32[16,24]{1,0:T(8,128)S(1)} %bitcast.5), custom_call_target="tpu_custom_call" | custom-call | tf_op jit(solution)/shard_map/pallas_call | solution.py:232
  (1 shorter events, 0.0 us)
Async XLA Ops:
  0.0 12.4 %collective-permute-start.7 = (bf16[128,128,128]{2,1,0:T(8,128)(2,1)}, bf16[128,128,128]{2,1,0:T(8,128)(2,1)S(1)}, u32[]{:S(2)}, u32[]{:S(2)}) collective-permute-start(bf16[128,128,128]{2,1,0:T(8,128)(2,1)} %own_hbm.1), channel_id=1, source_target_pairs={{0,1},{1,0},{2,3},{3,2},{4,5},{5,4},{6,7},{7,6},{8,9},{9,8},{10,11... | collective-permute-start | bytes 12582920 | tf_op jit(solution)/shard_map/ppermute | solution.py:177
  0.5 8.8 %collective-permute-start = (bf16[8,32,128]{2,1,0:T(8,128)(2,1)}, bf16[8,32,128]{2,1,0:T(8,128)(2,1)S(1)}, u32[]{:S(2)}, u32[]{:S(2)}) collective-permute-start(bf16[8,32,128]{2,1,0:T(8,128)(2,1)} %tokens_hbm.1), channel_id=1, source_target_pairs={{0,2},{2,0},{4,6},{6,4},{8,10},{10,8},{12,14},{14,12},{1,3},{3,1},... | collective-permute-start | bytes 196616 | tf_op jit(solution)/shard_map/ppermute | solution.py:172
  3.0 7.0 %collective-permute-start.4 = (bf16[8,32,128]{2,1,0:T(8,128)(2,1)}, bf16[8,32,128]{2,1,0:T(8,128)(2,1)S(1)}, u32[]{:S(2)}, u32[]{:S(2)}) collective-permute-start(bf16[8,32,128]{2,1,0:T(8,128)(2,1)} %tokens_hbm.1), channel_id=1, source_target_pairs={{0,8},{2,10},{4,12},{6,14},{8,0},{10,2},{12,4},{14,6},{1,9},{3,11}... | collective-permute-start | bytes 196616 | tf_op jit(solution)/shard_map/ppermute | solution.py:172
  5.6 6.4 %collective-permute-start.2 = (bf16[8,32,128]{2,1,0:T(8,128)(2,1)}, bf16[8,32,128]{2,1,0:T(8,128)(2,1)S(1)}, u32[]{:S(2)}, u32[]{:S(2)}) collective-permute-start(bf16[8,32,128]{2,1,0:T(8,128)(2,1)} %tokens_hbm.1), channel_id=1, source_target_pairs={{0,12},{2,14},{4,8},{6,10},{8,4},{10,6},{12,0},{14,2},{1,13},{3,15... | collective-permute-start | bytes 196616 | tf_op jit(solution)/shard_map/ppermute | solution.py:172
  9.3 6.9 %collective-permute-start.6 = (bf16[2,8,32,128]{3,2,1,0:T(8,128)(2,1)S(1)}, bf16[2,8,32,128]{3,2,1,0:T(8,128)(2,1)S(1)}, u32[]{:S(2)}, u32[]{:S(2)}) collective-permute-start(bf16[2,8,32,128]{3,2,1,0:T(8,128)(2,1)S(1)} %shard_map.65), channel_id=1, source_target_pairs={{0,4},{2,6},{4,0},{6,2},{8,12},{10,14},{12,8},{14,10},{1,5},{3,7},... | collective-permute-start | bytes 393224 | tf_op jit(solution)/shard_map/ppermute | solution.py:172
  9.6 2.8 %collective-permute-start.1 = (s32[8,128]{1,0:T(8,128)S(1)}, s32[8,128]{1,0:T(8,128)S(1)}, u32[]{:S(2)}, u32[]{:S(2)}) collective-permute-start(s32[8,128]{1,0:T(8,128)S(1)} %get-tuple-element.12), channel_id=1, source_target_pairs={{0,1},{1,0},{2,3},{3,2},{4,5},{5,4},{6,7},{7,6},{8,9},{9,8},{10,11... | collective-permute-start | bytes 12296 | tf_op jit(solution)/shard_map/ppermute | solution.py:205
  10.0 5.0 %collective-permute-start.5 = (bf16[8,32,128]{2,1,0:T(8,128)(2,1)S(1)}, bf16[8,32,128]{2,1,0:T(8,128)(2,1)S(1)}, u32[]{:S(2)}, u32[]{:S(2)}) collective-permute-start(bf16[8,32,128]{2,1,0:T(8,128)(2,1)S(1)} %collective-permute-done.4.refs_3_), channel_id=1, source_target_pairs={{0,2},{2,0},{4,6},{6,4},{8,10},{10,8},{12,14},{14,12},{1,3},{3,1},... | collective-permute-start | bytes 196616 | tf_op jit(solution)/shard_map/ppermute | solution.py:172
  11.9 4.3 %collective-permute-start.3 = (bf16[8,32,128]{2,1,0:T(8,128)(2,1)S(1)}, bf16[8,32,128]{2,1,0:T(8,128)(2,1)S(1)}, u32[]{:S(2)}, u32[]{:S(2)}) collective-permute-start(bf16[8,32,128]{2,1,0:T(8,128)(2,1)S(1)} %collective-permute-done.2.refs_2_), channel_id=1, source_target_pairs={{0,2},{2,0},{4,6},{6,4},{8,10},{10,8},{12,14},{14,12},{1,3},{3,1},... | collective-permute-start | bytes 196616 | tf_op jit(solution)/shard_map/ppermute | solution.py:172

commit v12 on v11

--- a/solution.py
+++ b/solution.py
@@ -7,7 +7,7 @@
 from jax.experimental.pallas import tpu as pltpu
 from jax.sharding import PartitionSpec as P
 
-GROUPS = 4
+GROUPS = 8
 CHUNKS = 8
 SHIFT = 8
 QUERY, PASSAGE, LENGTH, COUNT = 0, 32, 64, 96
@@ -102,9 +102,9 @@
         for g in range(GROUPS):
             work_ref[total + g] = 0
 
-        def one_step(step, carry):
-            for j in range(GROUPS):
-                work = work_ref[step * GROUPS + j]
+        def one_step(first_group, groups):
+            for j in range(groups):
+                work = work_ref[first_group + j]
                 i, g = lax.shift_right_logical(work, SHIFT), jnp.bitwise_and(work, (1 << SHIFT) - 1)
                 shard = shard_of(i)
                 rows, cols, limit = [], [], jnp.zeros((1, lanes), jnp.int32)
@@ -121,9 +121,17 @@
                 best = jnp.max(jnp.where(token < limit, sims, -1e30), axis=0, keepdims=True)
                 best = jnp.where(place + g * pack < meta_ref[which, shard, COUNT], best, 0.0)
                 best_ref[g, pl.ds(i * 2 + owner, 1), :] = best
-            return carry
-
-        lax.fori_loop(0, lax.shift_right_logical(total + GROUPS - 1, GROUPS.bit_length() - 1), one_step, 0)
+
+        half = GROUPS // 2
+        steps = lax.shift_right_logical(total + half - 1, GROUPS.bit_length() - 1)
+
+        @pl.loop(0, steps)
+        def _(step):
+            one_step(step * GROUPS, GROUPS)
+
+        @pl.when(total > steps * GROUPS)
+        def _():
+            one_step(steps * GROUPS, half)
 
     best = jnp.concatenate([best_ref[g] for g in range(per_source)], axis=1)
     high = best.astype(jnp.bfloat16)

time: 29.5 us -> 28.7 us (0.973); the launches traced: 29.1 us -> 28.7 us
  blocking collectives: 10 us -> 9.33 us
  waiting for transfers between devices: 3.17 us -> 3.79 us
  Pallas kernels: 7.69 us -> 7.39 us
    all_to_all x1, blocking collectives: 10 us -> 9.33 us  [on_device(): lax.all_to_all(scores, 'shard', split_axis=0, concat_axis=0, axis_index_g...]
    ppermute x6, waiting for transfers between devices: 3.16 us -> 3.78 us  [swapped(): return lax.ppermute(piece, 'shard', [(i, i ^ d) for i in range(shards)])]
    pallas_call x2, Pallas kernels: 4.75 us -> 4.44 us  [scored(): pl.pallas_call(functools.partial(score_kernel, shards, distances, pack, c...]
  transfers between devices with their start and end apart: 8 -> 8, of which waited for: 3 -> 4; matrix products, arithmetic and copies ran while one was open for 0% -> 0% of each run, Pallas kernels for 17% -> 15%
where the time goes in v12:
time: 28.7 us
  blocking collectives  9.33 us (33%)
  starting transfers between devices  8.1 us (28%)
  Pallas kernels  7.39 us (26%)
  waiting for transfers between devices  3.79 us (13%)
    all_to_all x1, blocking collectives, on_device(): lax.all_to_all(scores, 'shard', split_axis=0, concat_axis=0, axis_index_g...  9.33 us
    ppermute x6, starting transfers between devices, swapped(): return lax.ppermute(piece, 'shard', [(i, i ^ d) for i in range(shards)])  7.64 us
    pallas_call x2, Pallas kernels, scored(): pl.pallas_call(functools.partial(score_kernel, shards, distances, pack, c...  4.44 us
    ppermute x6, waiting for transfers between devices, swapped(): return lax.ppermute(piece, 'shard', [(i, i ^ d) for i in range(shards)])  3.78 us
    pallas_call x1, Pallas kernels, on_device(): pl.pallas_call(functools.partial(pack_kernel, shards), out_shape=[row, ro...  2.33 us
    pallas_call x1, Pallas kernels, on_device(): pl.pallas_call(order_kernel, out_shape=jax.ShapeDtypeStruct((1, sources,...  0.6 us
  transfers between devices with their start and end apart: 8, of which 4 were waited for; matrix products, arithmetic and copies ran while one was open for 0% of the time, Pallas kernels for 15%

profile of v12, /device:TPU:0, one launch (start us, length us, event | category | flops | bytes accessed | tf_op | source)
XLA Modules:
  0.0 28.7 jit_solution(1930133717169510507)
XLA Ops:
  0.0 0.5 %collective-permute-start.7 = (bf16[128,128,128]{2,1,0:T(8,128)(2,1)}, bf16[128,128,128]{2,1,0:T(8,128)(2,1)S(1)}, u32[]{:S(2)}, u32[]{:S(2)}) collective-permute-start(bf16[128,128,128]{2,1,0:T(8,128)(2,1)} %own_hbm.1), channel_id=1, source_target_pairs={{0,1},{1,0},{2,3},{3,2},{4,5},{5,4},{6,7},{7,6},{8,9},{9,8},{10,11... | collective-permute-start | bytes 12582920 | tf_op jit(solution)/shard_map/ppermute | solution.py:185
  0.5 2.5 %collective-permute-start = (bf16[8,32,128]{2,1,0:T(8,128)(2,1)}, bf16[8,32,128]{2,1,0:T(8,128)(2,1)S(1)}, u32[]{:S(2)}, u32[]{:S(2)}) collective-permute-start(bf16[8,32,128]{2,1,0:T(8,128)(2,1)} %tokens_hbm.1), channel_id=1, source_target_pairs={{0,2},{2,0},{4,6},{6,4},{8,10},{10,8},{12,14},{14,12},{1,3},{3,1},... | collective-permute-start | bytes 196616 | tf_op jit(solution)/shard_map/ppermute | solution.py:180
  3.0 2.6 %collective-permute-start.4 = (bf16[8,32,128]{2,1,0:T(8,128)(2,1)}, bf16[8,32,128]{2,1,0:T(8,128)(2,1)S(1)}, u32[]{:S(2)}, u32[]{:S(2)}) collective-permute-start(bf16[8,32,128]{2,1,0:T(8,128)(2,1)} %tokens_hbm.1), channel_id=1, source_target_pairs={{0,8},{2,10},{4,12},{6,14},{8,0},{10,2},{12,4},{14,6},{1,9},{3,11}... | collective-permute-start | bytes 196616 | tf_op jit(solution)/shard_map/ppermute | solution.py:180
  5.6 1.3 %collective-permute-start.2 = (bf16[8,32,128]{2,1,0:T(8,128)(2,1)}, bf16[8,32,128]{2,1,0:T(8,128)(2,1)S(1)}, u32[]{:S(2)}, u32[]{:S(2)}) collective-permute-start(bf16[8,32,128]{2,1,0:T(8,128)(2,1)} %tokens_hbm.1), channel_id=1, source_target_pairs={{0,12},{2,14},{4,8},{6,10},{8,4},{10,6},{12,0},{14,2},{1,13},{3,15... | collective-permute-start | bytes 196616 | tf_op jit(solution)/shard_map/ppermute | solution.py:180
  6.9 2.3 %shard_map.64 = (s32[8,128]{1,0:T(8,128)S(1)}, s32[8,128]{1,0:T(8,128)S(1)}, bf16[8,32,128]{2,1,0:T(8,128)(2,1)S(1)}, bf16[128,128,128]{2,1,0:T(8,128)(2,1)S(1)}) custom-call(s32[16,24]{1,0:T(8,128)} %bitcast.7, s32[16,24]{1,0:T(8,128)} %bitcast.8, s32[16]{0:T(128)} %bitcast.9, s32[128]{0:T(128)} %length_hbm.1, bf16[8,32,128]{2,1,0:T(8,128)(2,1)} %tokens_hbm.1, ...), custom_call_target="tpu_custom_call" | custom-call | tf_op jit(solution)/shard_map/pallas_call | solution.py:187
  9.2 0.0 collective-permute-done.other_ref.refs_4_
  9.3 0.3 %collective-permute-start.6 = (bf16[2,8,32,128]{3,2,1,0:T(8,128)(2,1)S(1)}, bf16[2,8,32,128]{3,2,1,0:T(8,128)(2,1)S(1)}, u32[]{:S(2)}, u32[]{:S(2)}) collective-permute-start(bf16[2,8,32,128]{3,2,1,0:T(8,128)(2,1)S(1)} %shard_map.65), channel_id=1, source_target_pairs={{0,4},{2,6},{4,0},{6,2},{8,12},{10,14},{12,8},{14,10},{1,5},{3,7},... | collective-permute-start | bytes 393224 | tf_op jit(solution)/shard_map/ppermute | solution.py:180
  9.6 0.0 collective-permute-start.1
  9.6 0.4 %collective-permute-done.4.refs_3_ = bf16[8,32,128]{2,1,0:T(8,128)(2,1)S(1)} collective-permute-done((bf16[8,32,128]{2,1,0:T(8,128)(2,1)}, bf16[8,32,128]{2,1,0:T(8,128)(2,1)S(1)}, u32[]{:S(2)}, u32[]{:S(2)}) %collective-permute-start.4) | collective-permute-done | bytes 65568 | tf_op jit(solution)/shard_map/ppermute | solution.py:180
  10.0 0.4 %collective-permute-start.5 = (bf16[8,32,128]{2,1,0:T(8,128)(2,1)S(1)}, bf16[8,32,128]{2,1,0:T(8,128)(2,1)S(1)}, u32[]{:S(2)}, u32[]{:S(2)}) collective-permute-start(bf16[8,32,128]{2,1,0:T(8,128)(2,1)S(1)} %collective-permute-done.4.refs_3_), channel_id=1, source_target_pairs={{0,2},{2,0},{4,6},{6,4},{8,10},{10,8},{12,14},{14,12},{1,3},{3,1},... | collective-permute-start | bytes 196616 | tf_op jit(solution)/shard_map/ppermute | solution.py:180
  10.4 1.5 %collective-permute-done.2.refs_2_ = bf16[8,32,128]{2,1,0:T(8,128)(2,1)S(1)} collective-permute-done((bf16[8,32,128]{2,1,0:T(8,128)(2,1)}, bf16[8,32,128]{2,1,0:T(8,128)(2,1)S(1)}, u32[]{:S(2)}, u32[]{:S(2)}) %collective-permute-start.2) | collective-permute-done | bytes 65568 | tf_op jit(solution)/shard_map/ppermute | solution.py:180
  11.9 0.5 %collective-permute-start.3 = (bf16[8,32,128]{2,1,0:T(8,128)(2,1)S(1)}, bf16[8,32,128]{2,1,0:T(8,128)(2,1)S(1)}, u32[]{:S(2)}, u32[]{:S(2)}) collective-permute-start(bf16[8,32,128]{2,1,0:T(8,128)(2,1)S(1)} %collective-permute-done.2.refs_2_), channel_id=1, source_target_pairs={{0,2},{2,0},{4,6},{6,4},{8,10},{10,8},{12,14},{14,12},{1,3},{3,1},... | collective-permute-start | bytes 196616 | tf_op jit(solution)/shard_map/ppermute | solution.py:180
  12.4 0.0 collective-permute-done.1.refs_1_
  12.4 0.0 collective-permute-done.7.refs_7_.refs_6_
  12.4 1.9 %shard_map.66.refs_7_ = f32[8,24]{1,0:T(8,128)S(1)} custom-call(s32[8,128]{1,0:T(8,128)S(1)} %get-tuple-element.10.refs_0_, s32[8,128]{1,0:T(8,128)S(1)} %collective-permute-done.1.refs_1_, bf16[8,32,128]{2,1,0:T(8,128)(2,1)S(1)} %collective-permute-done.2.refs_2_, bf16[8,32,128]{2,1,0:T(8,128)(2,1)S(1)} %collective-permute-done.4.refs_3_, ...), custom_call_target="tpu_custom_call" | custom-call | flops 1000000000 | bytes 9000000 | tf_op jit(solution)/shard_map/pallas_call | solution.py:218
  14.3 0.4 %collective-permute-done.5.refs_3_ = bf16[8,32,128]{2,1,0:T(8,128)(2,1)S(1)} collective-permute-done((bf16[8,32,128]{2,1,0:T(8,128)(2,1)S(1)}, bf16[8,32,128]{2,1,0:T(8,128)(2,1)S(1)}, u32[]{:S(2)}, u32[]{:S(2)}) %collective-permute-start.5) | collective-permute-done | bytes 65568 | tf_op jit(solution)/shard_map/ppermute | solution.py:180
  14.8 1.4 %collective-permute-done.3.refs_2_ = bf16[8,32,128]{2,1,0:T(8,128)(2,1)S(1)} collective-permute-done((bf16[8,32,128]{2,1,0:T(8,128)(2,1)S(1)}, bf16[8,32,128]{2,1,0:T(8,128)(2,1)S(1)}, u32[]{:S(2)}, u32[]{:S(2)}) %collective-permute-start.3) | collective-permute-done | bytes 65568 | tf_op jit(solution)/shard_map/ppermute | solution.py:180
  16.2 0.0 collective-permute-done.6.refs_4_
  16.2 2.5 %shard_map.67 = f32[16,24]{1,0:T(8,128)S(1)} custom-call(s32[8,128]{1,0:T(8,128)S(1)} %get-tuple-element.10.refs_0_, s32[8,128]{1,0:T(8,128)S(1)} %collective-permute-done.1.refs_1_, bf16[8,32,128]{2,1,0:T(8,128)(2,1)S(1)} %collective-permute-done.3.refs_2_, bf16[8,32,128]{2,1,0:T(8,128)(2,1)S(1)} %collective-permute-done.5.refs_3_, ...), custom_call_target="tpu_custom_call" | custom-call | flops 1000000000 | bytes 9000000 | tf_op jit(solution)/shard_map/pallas_call | solution.py:218
  18.7 9.3 %all_to_all.11 = f32[8,2,24]{2,1,0:T(2,128)S(1)} all-to-all(f32[8,2,24]{2,1,0:T(2,128)S(1)} %bitcast.6), channel_id=1, replica_groups={{14,12,10,8,6,4,2,0},{15,13,11,9,7,5,3,1},{30,28,26,24,22,20,18,16},{31..., dimensions={0} | all-to-all | bytes 3072 | tf_op jit(solution)/shard_map/all_to_all | solution.py:239
  28.1 0.6 %shard_map.68 = f32[1,16,24]{2,1,0:T(8,128)} custom-call(f32[16,24]{1,0:T(8,128)S(1)} %bitcast.5), custom_call_target="tpu_custom_call" | custom-call | tf_op jit(solution)/shard_map/pallas_call | solution.py:240
  (1 shorter events, 0.0 us)
Async XLA Ops:
  0.0 12.4 %collective-permute-start.7 = (bf16[128,128,128]{2,1,0:T(8,128)(2,1)}, bf16[128,128,128]{2,1,0:T(8,128)(2,1)S(1)}, u32[]{:S(2)}, u32[]{:S(2)}) collective-permute-start(bf16[128,128,128]{2,1,0:T(8,128)(2,1)} %own_hbm.1), channel_id=1, source_target_pairs={{0,1},{1,0},{2,3},{3,2},{4,5},{5,4},{6,7},{7,6},{8,9},{9,8},{10,11... | collective-permute-start | bytes 12582920 | tf_op jit(solution)/shard_map/ppermute | solution.py:185
  0.5 8.8 %collective-permute-start = (bf16[8,32,128]{2,1,0:T(8,128)(2,1)}, bf16[8,32,128]{2,1,0:T(8,128)(2,1)S(1)}, u32[]{:S(2)}, u32[]{:S(2)}) collective-permute-start(bf16[8,32,128]{2,1,0:T(8,128)(2,1)} %tokens_hbm.1), channel_id=1, source_target_pairs={{0,2},{2,0},{4,6},{6,4},{8,10},{10,8},{12,14},{14,12},{1,3},{3,1},... | collective-permute-start | bytes 196616 | tf_op jit(solution)/shard_map/ppermute | solution.py:180
  3.0 7.0 %collective-permute-start.4 = (bf16[8,32,128]{2,1,0:T(8,128)(2,1)}, bf16[8,32,128]{2,1,0:T(8,128)(2,1)S(1)}, u32[]{:S(2)}, u32[]{:S(2)}) collective-permute-start(bf16[8,32,128]{2,1,0:T(8,128)(2,1)} %tokens_hbm.1), channel_id=1, source_target_pairs={{0,8},{2,10},{4,12},{6,14},{8,0},{10,2},{12,4},{14,6},{1,9},{3,11}... | collective-permute-start | bytes 196616 | tf_op jit(solution)/shard_map/ppermute | solution.py:180
  5.6 6.4 %collective-permute-start.2 = (bf16[8,32,128]{2,1,0:T(8,128)(2,1)}, bf16[8,32,128]{2,1,0:T(8,128)(2,1)S(1)}, u32[]{:S(2)}, u32[]{:S(2)}) collective-permute-start(bf16[8,32,128]{2,1,0:T(8,128)(2,1)} %tokens_hbm.1), channel_id=1, source_target_pairs={{0,12},{2,14},{4,8},{6,10},{8,4},{10,6},{12,0},{14,2},{1,13},{3,15... | collective-permute-start | bytes 196616 | tf_op jit(solution)/shard_map/ppermute | solution.py:180
  9.3 6.9 %collective-permute-start.6 = (bf16[2,8,32,128]{3,2,1,0:T(8,128)(2,1)S(1)}, bf16[2,8,32,128]{3,2,1,0:T(8,128)(2,1)S(1)}, u32[]{:S(2)}, u32[]{:S(2)}) collective-permute-start(bf16[2,8,32,128]{3,2,1,0:T(8,128)(2,1)S(1)} %shard_map.65), channel_id=1, source_target_pairs={{0,4},{2,6},{4,0},{6,2},{8,12},{10,14},{12,8},{14,10},{1,5},{3,7},... | collective-permute-start | bytes 393224 | tf_op jit(solution)/shard_map/ppermute | solution.py:180
  9.6 2.8 %collective-permute-start.1 = (s32[8,128]{1,0:T(8,128)S(1)}, s32[8,128]{1,0:T(8,128)S(1)}, u32[]{:S(2)}, u32[]{:S(2)}) collective-permute-start(s32[8,128]{1,0:T(8,128)S(1)} %get-tuple-element.12), channel_id=1, source_target_pairs={{0,1},{1,0},{2,3},{3,2},{4,5},{5,4},{6,7},{7,6},{8,9},{9,8},{10,11... | collective-permute-start | bytes 12296 | tf_op jit(solution)/shard_map/ppermute | solution.py:213
  10.0 4.8 %collective-permute-start.5 = (bf16[8,32,128]{2,1,0:T(8,128)(2,1)S(1)}, bf16[8,32,128]{2,1,0:T(8,128)(2,1)S(1)}, u32[]{:S(2)}, u32[]{:S(2)}) collective-permute-start(bf16[8,32,128]{2,1,0:T(8,128)(2,1)S(1)} %collective-permute-done.4.refs_3_), channel_id=1, source_target_pairs={{0,2},{2,0},{4,6},{6,4},{8,10},{10,8},{12,14},{14,12},{1,3},{3,1},... | collective-permute-start | bytes 196616 | tf_op jit(solution)/shard_map/ppermute | solution.py:180
  11.9 4.3 %collective-permute-start.3 = (bf16[8,32,128]{2,1,0:T(8,128)(2,1)S(1)}, bf16[8,32,128]{2,1,0:T(8,128)(2,1)S(1)}, u32[]{:S(2)}, u32[]{:S(2)}) collective-permute-start(bf16[8,32,128]{2,1,0:T(8,128)(2,1)S(1)} %collective-permute-done.2.refs_2_), channel_id=1, source_target_pairs={{0,2},{2,0},{4,6},{6,4},{8,10},{10,8},{12,14},{14,12},{1,3},{3,1},... | collective-permute-start | bytes 196616 | tf_op jit(solution)/shard_map/ppermute | solution.py:180

commit v13 on v12

--- a/solution.py
+++ b/solution.py
@@ -152,7 +152,7 @@
             out_ref[pl.ds((shards - 1 - jnp.bitwise_xor(me, d)) * 2, 2), :] = scores[2 * i : 2 * i + 2]
 
 
-def pair_kernel(one_ref, other_ref, out_ref):
+def pair_kernel(one_ref, other_ref, earlier_ref, out_ref):
     out_ref[0] = one_ref[...]
     out_ref[1] = other_ref[...]
 
@@ -202,14 +202,14 @@
     both = pl.pallas_call(
         pair_kernel,
         out_shape=jax.ShapeDtypeStruct((2, *queries.shape), queries.dtype),
-        in_specs=[vmem] * 2,
+        in_specs=[vmem, vmem, anywhere],
         out_specs=vmem,
         compiler_params=params,
-    )(own_queries, pieces[1])
+    )(own_queries, pieces[1], pieces[4])
     both = swapped(both, 2)
     for d in range(5, shards, 2):
         pieces[d] = swapped(pieces[d - 1], 1)
-    theirs, _ = lax.optimization_barrier((theirs, pieces[1]))
+    theirs, _ = lax.optimization_barrier((theirs, pieces[4]))
     other = lax.ppermute(theirs, "sub", swap)
 
     def scored(distances, *earlier):

time: 28.7 us -> 29.5 us (1.028)
  waiting for transfers between devices: 3.79 us -> 1.36 us
  starting transfers between devices: 8.1 us -> 10 us
  Pallas kernels: 7.39 us -> 8.58 us
    ppermute x6, waiting for transfers between devices: 3.78 us -> 1.35 us  [swapped(): return lax.ppermute(piece, 'shard', [(i, i ^ d) for i in range(shards)])]
    ppermute x6, starting transfers between devices: 7.64 us -> 9.56 us  [swapped(): return lax.ppermute(piece, 'shard', [(i, i ^ d) for i in range(shards)])]
    pallas_call x2, Pallas kernels: 4.44 us -> 5.64 us  [scored(): pl.pallas_call(functools.partial(score_kernel, shards, distances, pack, c...]
  transfers between devices with their start and end apart: 8 -> 8, of which waited for: 4 -> 1; matrix products, arithmetic and copies ran while one was open for 0% -> 0% of each run, Pallas kernels for 15% -> 17%
where the time goes in v13:
time: 29.5 us; the launch traced here: 29.6 us
  starting transfers between devices  10 us (34%)
  blocking collectives  9.58 us (32%)
  Pallas kernels  8.58 us (29%)
  waiting for transfers between devices  1.36 us (5%)
    all_to_all x1, blocking collectives, on_device(): lax.all_to_all(scores, 'shard', split_axis=0, concat_axis=0, axis_index_g...  9.58 us
    ppermute x6, starting transfers between devices, swapped(): return lax.ppermute(piece, 'shard', [(i, i ^ d) for i in range(shards)])  9.56 us
    pallas_call x2, Pallas kernels, scored(): pl.pallas_call(functools.partial(score_kernel, shards, distances, pack, c...  5.64 us
    pallas_call x1, Pallas kernels, on_device(): pl.pallas_call(functools.partial(pack_kernel, shards), out_shape=[row, ro...  2.33 us
    ppermute x6, waiting for transfers between devices, swapped(): return lax.ppermute(piece, 'shard', [(i, i ^ d) for i in range(shards)])  1.35 us
    pallas_call x1, Pallas kernels, on_device(): pl.pallas_call(order_kernel, out_shape=jax.ShapeDtypeStruct((1, sources,...  0.6 us
  transfers between devices with their start and end apart: 8, of which 1 were waited for; matrix products, arithmetic and copies ran while one was open for 0% of the time, Pallas kernels for 17%

profile of v13, /device:TPU:0, one launch (start us, length us, event | category | flops | bytes accessed | tf_op | source)
XLA Modules:
  0.0 29.6 jit_solution(12741945937538882685)
XLA Ops:
  0.0 0.5 %collective-permute-start.7 = (bf16[128,128,128]{2,1,0:T(8,128)(2,1)}, bf16[128,128,128]{2,1,0:T(8,128)(2,1)S(1)}, u32[]{:S(2)}, u32[]{:S(2)}) collective-permute-start(bf16[128,128,128]{2,1,0:T(8,128)(2,1)} %own_hbm.1), channel_id=1, source_target_pairs={{0,1},{1,0},{2,3},{3,2},{4,5},{5,4},{6,7},{7,6},{8,9},{9,8},{10,11... | collective-permute-start | bytes 12582920 | tf_op jit(solution)/shard_map/ppermute | solution.py:185
  0.5 3.6 %collective-permute-start = (bf16[8,32,128]{2,1,0:T(8,128)(2,1)}, bf16[8,32,128]{2,1,0:T(8,128)(2,1)S(1)}, u32[]{:S(2)}, u32[]{:S(2)}) collective-permute-start(bf16[8,32,128]{2,1,0:T(8,128)(2,1)} %tokens_hbm.1), channel_id=1, source_target_pairs={{0,8},{2,10},{4,12},{6,14},{8,0},{10,2},{12,4},{14,6},{1,9},{3,11}... | collective-permute-start | bytes 196616 | tf_op jit(solution)/shard_map/ppermute | solution.py:180
  4.0 1.5 %collective-permute-start.5 = (bf16[8,32,128]{2,1,0:T(8,128)(2,1)}, bf16[8,32,128]{2,1,0:T(8,128)(2,1)S(1)}, u32[]{:S(2)}, u32[]{:S(2)}) collective-permute-start(bf16[8,32,128]{2,1,0:T(8,128)(2,1)} %tokens_hbm.1), channel_id=1, source_target_pairs={{0,2},{2,0},{4,6},{6,4},{8,10},{10,8},{12,14},{14,12},{1,3},{3,1},... | collective-permute-start | bytes 196616 | tf_op jit(solution)/shard_map/ppermute | solution.py:180
  5.6 1.3 %collective-permute-start.2 = (bf16[8,32,128]{2,1,0:T(8,128)(2,1)}, bf16[8,32,128]{2,1,0:T(8,128)(2,1)S(1)}, u32[]{:S(2)}, u32[]{:S(2)}) collective-permute-start(bf16[8,32,128]{2,1,0:T(8,128)(2,1)} %tokens_hbm.1), channel_id=1, source_target_pairs={{0,12},{2,14},{4,8},{6,10},{8,4},{10,6},{12,0},{14,2},{1,13},{3,15... | collective-permute-start | bytes 196616 | tf_op jit(solution)/shard_map/ppermute | solution.py:180
  6.9 2.3 %shard_map.64 = (s32[8,128]{1,0:T(8,128)S(1)}, s32[8,128]{1,0:T(8,128)S(1)}, bf16[8,32,128]{2,1,0:T(8,128)(2,1)S(1)}, bf16[128,128,128]{2,1,0:T(8,128)(2,1)S(1)}) custom-call(s32[16,24]{1,0:T(8,128)} %bitcast.7, s32[16,24]{1,0:T(8,128)} %bitcast.8, s32[16]{0:T(128)} %bitcast.9, s32[128]{0:T(128)} %length_hbm.1, bf16[8,32,128]{2,1,0:T(8,128)(2,1)} %tokens_hbm.1, ...), custom_call_target="tpu_custom_call" | custom-call | tf_op jit(solution)/shard_map/pallas_call | solution.py:187
  9.2 0.0 collective-permute-done.earlier_ref.refs_3_
  9.3 0.0 collective-permute-done.5.other_ref.refs_4_
  9.3 0.9 %collective-permute-start.6 = (bf16[2,8,32,128]{3,2,1,0:T(8,128)(2,1)S(1)}, bf16[2,8,32,128]{3,2,1,0:T(8,128)(2,1)S(1)}, u32[]{:S(2)}, u32[]{:S(2)}) collective-permute-start(bf16[2,8,32,128]{3,2,1,0:T(8,128)(2,1)S(1)} %shard_map.65), channel_id=1, source_target_pairs={{0,4},{2,6},{4,0},{6,2},{8,12},{10,14},{12,8},{14,10},{1,5},{3,7},... | collective-permute-start | bytes 393224 | tf_op jit(solution)/shard_map/ppermute | solution.py:180
  10.2 0.0 collective-permute-start.1
  10.2 2.1 %collective-permute-start.4 = (bf16[8,32,128]{2,1,0:T(8,128)(2,1)S(1)}, bf16[8,32,128]{2,1,0:T(8,128)(2,1)S(1)}, u32[]{:S(2)}, u32[]{:S(2)}) collective-permute-start(bf16[8,32,128]{2,1,0:T(8,128)(2,1)S(1)} %collective-permute-done.earlier_ref.refs_3_), channel_id=1, source_target_pairs={{0,2},{2,0},{4,6},{6,4},{8,10},{10,8},{12,14},{14,12},{1,3},{3,1},... | collective-permute-start | bytes 196616 | tf_op jit(solution)/shard_map/ppermute | solution.py:180
  12.3 0.0 collective-permute-done.2.refs_2_
  12.3 0.1 collective-permute-start.3
  12.4 0.0 collective-permute-done.1.refs_1_
  12.4 0.0 collective-permute-done.7.refs_7_.refs_6_
  12.4 2.8 %shard_map.66.refs_7_ = f32[8,24]{1,0:T(8,128)S(1)} custom-call(s32[8,128]{1,0:T(8,128)S(1)} %get-tuple-element.10.refs_0_, s32[8,128]{1,0:T(8,128)S(1)} %collective-permute-done.1.refs_1_, bf16[8,32,128]{2,1,0:T(8,128)(2,1)S(1)} %collective-permute-done.2.refs_2_, bf16[8,32,128]{2,1,0:T(8,128)(2,1)S(1)} %collective-permute-done.earlier_ref.refs_3_, ...), custom_call_target="tpu_custom_call" | custom-call | flops 1000000000 | bytes 9000000 | tf_op jit(solution)/shard_map/pallas_call | solution.py:218
  15.2 0.0 collective-permute-done.4.refs_3_
  15.2 1.3 %collective-permute-done.3.refs_2_ = bf16[8,32,128]{2,1,0:T(8,128)(2,1)S(1)} collective-permute-done((bf16[8,32,128]{2,1,0:T(8,128)(2,1)S(1)}, bf16[8,32,128]{2,1,0:T(8,128)(2,1)S(1)}, u32[]{:S(2)}, u32[]{:S(2)}) %collective-permute-start.3) | collective-permute-done | bytes 65568 | tf_op jit(solution)/shard_map/ppermute | solution.py:180
  16.6 0.0 collective-permute-done.6.refs_4_
  16.6 2.8 %shard_map.67 = f32[16,24]{1,0:T(8,128)S(1)} custom-call(s32[8,128]{1,0:T(8,128)S(1)} %get-tuple-element.10.refs_0_, s32[8,128]{1,0:T(8,128)S(1)} %collective-permute-done.1.refs_1_, bf16[8,32,128]{2,1,0:T(8,128)(2,1)S(1)} %collective-permute-done.3.refs_2_, bf16[8,32,128]{2,1,0:T(8,128)(2,1)S(1)} %collective-permute-done.4.refs_3_, ...), custom_call_target="tpu_custom_call" | custom-call | flops 1000000000 | bytes 9000000 | tf_op jit(solution)/shard_map/pallas_call | solution.py:218
  19.4 9.6 %all_to_all.11 = f32[8,2,24]{2,1,0:T(2,128)S(1)} all-to-all(f32[8,2,24]{2,1,0:T(2,128)S(1)} %bitcast.6), channel_id=1, replica_groups={{14,12,10,8,6,4,2,0},{15,13,11,9,7,5,3,1},{30,28,26,24,22,20,18,16},{31..., dimensions={0} | all-to-all | bytes 3072 | tf_op jit(solution)/shard_map/all_to_all | solution.py:239
  29.0 0.6 %shard_map.68 = f32[1,16,24]{2,1,0:T(8,128)} custom-call(f32[16,24]{1,0:T(8,128)S(1)} %bitcast.5), custom_call_target="tpu_custom_call" | custom-call | tf_op jit(solution)/shard_map/pallas_call | solution.py:240
  (1 shorter events, 0.0 us)
Async XLA Ops:
  0.0 12.4 %collective-permute-start.7 = (bf16[128,128,128]{2,1,0:T(8,128)(2,1)}, bf16[128,128,128]{2,1,0:T(8,128)(2,1)S(1)}, u32[]{:S(2)}, u32[]{:S(2)}) collective-permute-start(bf16[128,128,128]{2,1,0:T(8,128)(2,1)} %own_hbm.1), channel_id=1, source_target_pairs={{0,1},{1,0},{2,3},{3,2},{4,5},{5,4},{6,7},{7,6},{8,9},{9,8},{10,11... | collective-permute-start | bytes 12582920 | tf_op jit(solution)/shard_map/ppermute | solution.py:185
  0.5 8.8 %collective-permute-start = (bf16[8,32,128]{2,1,0:T(8,128)(2,1)}, bf16[8,32,128]{2,1,0:T(8,128)(2,1)S(1)}, u32[]{:S(2)}, u32[]{:S(2)}) collective-permute-start(bf16[8,32,128]{2,1,0:T(8,128)(2,1)} %tokens_hbm.1), channel_id=1, source_target_pairs={{0,8},{2,10},{4,12},{6,14},{8,0},{10,2},{12,4},{14,6},{1,9},{3,11}... | collective-permute-start | bytes 196616 | tf_op jit(solution)/shard_map/ppermute | solution.py:180
  4.0 5.2 %collective-permute-start.5 = (bf16[8,32,128]{2,1,0:T(8,128)(2,1)}, bf16[8,32,128]{2,1,0:T(8,128)(2,1)S(1)}, u32[]{:S(2)}, u32[]{:S(2)}) collective-permute-start(bf16[8,32,128]{2,1,0:T(8,128)(2,1)} %tokens_hbm.1), channel_id=1, source_target_pairs={{0,2},{2,0},{4,6},{6,4},{8,10},{10,8},{12,14},{14,12},{1,3},{3,1},... | collective-permute-start | bytes 196616 | tf_op jit(solution)/shard_map/ppermute | solution.py:180
  5.6 6.7 %collective-permute-start.2 = (bf16[8,32,128]{2,1,0:T(8,128)(2,1)}, bf16[8,32,128]{2,1,0:T(8,128)(2,1)S(1)}, u32[]{:S(2)}, u32[]{:S(2)}) collective-permute-start(bf16[8,32,128]{2,1,0:T(8,128)(2,1)} %tokens_hbm.1), channel_id=1, source_target_pairs={{0,12},{2,14},{4,8},{6,10},{8,4},{10,6},{12,0},{14,2},{1,13},{3,15... | collective-permute-start | bytes 196616 | tf_op jit(solution)/shard_map/ppermute | solution.py:180
  9.3 7.3 %collective-permute-start.6 = (bf16[2,8,32,128]{3,2,1,0:T(8,128)(2,1)S(1)}, bf16[2,8,32,128]{3,2,1,0:T(8,128)(2,1)S(1)}, u32[]{:S(2)}, u32[]{:S(2)}) collective-permute-start(bf16[2,8,32,128]{3,2,1,0:T(8,128)(2,1)S(1)} %shard_map.65), channel_id=1, source_target_pairs={{0,4},{2,6},{4,0},{6,2},{8,12},{10,14},{12,8},{14,10},{1,5},{3,7},... | collective-permute-start | bytes 393224 | tf_op jit(solution)/shard_map/ppermute | solution.py:180
  10.2 2.2 %collective-permute-start.1 = (s32[8,128]{1,0:T(8,128)S(1)}, s32[8,128]{1,0:T(8,128)S(1)}, u32[]{:S(2)}, u32[]{:S(2)}) collective-permute-start(s32[8,128]{1,0:T(8,128)S(1)} %get-tuple-element.12), channel_id=1, source_target_pairs={{0,1},{1,0},{2,3},{3,2},{4,5},{5,4},{6,7},{7,6},{8,9},{9,8},{10,11... | collective-permute-start | bytes 12296 | tf_op jit(solution)/shard_map/ppermute | solution.py:213
  10.2 5.0 %collective-permute-start.4 = (bf16[8,32,128]{2,1,0:T(8,128)(2,1)S(1)}, bf16[8,32,128]{2,1,0:T(8,128)(2,1)S(1)}, u32[]{:S(2)}, u32[]{:S(2)}) collective-permute-start(bf16[8,32,128]{2,1,0:T(8,128)(2,1)S(1)} %collective-permute-done.earlier_ref.refs_3_), channel_id=1, source_target_pairs={{0,2},{2,0},{4,6},{6,4},{8,10},{10,8},{12,14},{14,12},{1,3},{3,1},... | collective-permute-start | bytes 196616 | tf_op jit(solution)/shard_map/ppermute | solution.py:180
  12.3 4.3 %collective-permute-start.3 = (bf16[8,32,128]{2,1,0:T(8,128)(2,1)S(1)}, bf16[8,32,128]{2,1,0:T(8,128)(2,1)S(1)}, u32[]{:S(2)}, u32[]{:S(2)}) collective-permute-start(bf16[8,32,128]{2,1,0:T(8,128)(2,1)S(1)} %collective-permute-done.2.refs_2_), channel_id=1, source_target_pairs={{0,2},{2,0},{4,6},{6,4},{8,10},{10,8},{12,14},{14,12},{1,3},{3,1},... | collective-permute-start | bytes 196616 | tf_op jit(solution)/shard_map/ppermute | solution.py:180
